TPU v7x, 128 devices: a whole 4x4x4 slice. The times are simulated.
128 devices in a mesh: group: 4 (over z), dom: 32 (over x, y, core).
Axes of the slice: x: 4, y: 4, z: 4, core: 2. Of those that a mesh axis runs over, the one named last changes fastest.
Arguments:
- node_features: bfloat16 [131072, 128], P(('group', 'dom')), may hold values from -6 to 6
- edge_features: bfloat16 [524288, 128], P(('group', 'dom')), may hold values from -6 to 6
- coarse_features: bfloat16 [32768, 128], P(('group', 'dom')), may hold values from -6 to 6
- edge_w_one: bfloat16 [384, 128], replicated, may hold values from -0.3125 to 0.3125
- edge_w_two: bfloat16 [128, 128], replicated, may hold values from -0.5 to 0.5
- node_w_one: bfloat16 [256, 128], replicated, may hold values from -0.375 to 0.375
- node_w_two: bfloat16 [128, 128], replicated, may hold values from -0.5 to 0.5
- coarse_w_one: bfloat16 [256, 128], replicated, may hold values from -0.375 to 0.375
- coarse_w_two: bfloat16 [128, 128], replicated, may hold values from -0.5 to 0.5
- edge_source: int32 [524288], P(('group', 'dom')), may hold values from 0 to 1535, as said below
- edge_target: int32 [524288], P(('group', 'dom')), may hold values from 0 to 1023
- boundary: int32 [128, 256], P(('group', 'dom')), may hold values from 0 to 1023, as said below
- ghost_pos: int32 [128, 32, 16], P(('group', 'dom')), may hold values from 0 to 255
- restr_order: int32 [128, 1024], P(('group', 'dom')), may hold values from 0 to 1023, each once within a row
- restr_count: int32 [128, 4], P(('group', 'dom')), may hold values from 1 to 512, 1024 in all within a row
- coarse_slot: int32 [128, 4, 512], P(('group', 'dom')), may hold values from 0 to 255
- node_cotangent: bfloat16 [131072, 128], P(('group', 'dom')), may hold values from -6 to 6
- edge_cotangent: bfloat16 [524288, 128], P(('group', 'dom')), may hold values from -6 to 6
- coarse_cotangent: bfloat16 [32768, 128], P(('group', 'dom')), may hold values from -6 to 6
Outputs:
- grad_nodes: float32 [131072, 128], P(('group', 'dom'))
- grad_edges: float32 [524288, 128], P(('group', 'dom'))
- grad_coarse: float32 [32768, 128], P(('group', 'dom'))
- grad_edge_w_one: float32 [384, 128], replicated
- grad_edge_w_two: float32 [128, 128], replicated
- grad_node_w_one: float32 [256, 128], replicated
- grad_node_w_two: float32 [128, 128], replicated
- grad_coarse_w_one: float32 [256, 128], replicated
- grad_coarse_w_two: float32 [128, 128], replicated
Inputs may be any that keep to these rules, and one draw needn't show every extreme that they name: `boundary`: the 256 rows of a partition are distinct. `edge_source`: about one entry in four names a ghost row. `restr_count`: each partition's counts sum to 1024; its largest is exactly 512.
All inputs are finite; a program needn't handle non-finite values.
Results may differ from a plain program's by a relative error of at most 0.01.
Values may be sent and summed in bfloat16 or wider, within the bound.
No kernel may reach another device: no remote copies, remote signals or barrier semaphores. Data moves between devices by JAX's collectives and lax.ppermute only.
A program may use at most 64 MiB of HBM per device.

v0:
```python
import jax
import jax.numpy as jnp
from jax import lax
from jax.sharding import PartitionSpec as P

NORM_EPSILON = 1e-05
POOL_SHARE = 0.25


def silu_slope(values):
    sig_val = jax.nn.sigmoid(values)
    return sig_val * (1.0 + values * (1.0 - sig_val))


def norm_rows(values):
    centred = values - jnp.mean(values, axis=-1, keepdims=True)
    return centred * lax.rsqrt(jnp.mean(centred * centred, axis=-1, keepdims=True) + NORM_EPSILON)


def norm_back(values, grad_in):
    centred = values - jnp.mean(values, axis=-1, keepdims=True)
    inv_std = lax.rsqrt(jnp.mean(centred * centred, axis=-1, keepdims=True) + NORM_EPSILON)
    normed = centred * inv_std
    return inv_std * (
        grad_in
        - jnp.mean(grad_in, axis=-1, keepdims=True)
        - normed * jnp.mean(grad_in * normed, axis=-1, keepdims=True)
    )


def outer_sum(first_op, second_op):
    return lax.dot_general(
        first_op, second_op, (((0,), (0,)), ((), ())), preferred_element_type=jnp.float32
    )


def edge_forward(lookup, edges, source, target, w_one, w_two):
    stacked = jnp.concatenate([lookup[source], lookup[target], edges], axis=1)
    pre_act = jnp.dot(stacked, w_one, preferred_element_type=jnp.float32)
    hidden = jax.nn.silu(pre_act).astype(jnp.bfloat16)
    pre_norm = jnp.dot(hidden, w_two, preferred_element_type=jnp.float32)
    return (stacked, pre_act, hidden, pre_norm)


def node_forward(node_rows, message, target, v_one, v_two):
    row_count = node_rows.shape[0]
    summed = jax.ops.segment_sum(norm_rows(message), target, num_segments=row_count)
    joined = jnp.concatenate([node_rows, summed.astype(jnp.bfloat16)], axis=1)
    pre_act = jnp.dot(joined, v_one, preferred_element_type=jnp.float32)
    hidden = jax.nn.silu(pre_act).astype(jnp.bfloat16)
    pre_norm = jnp.dot(hidden, v_two, preferred_element_type=jnp.float32)
    updated = (node_rows.astype(jnp.float32) + norm_rows(pre_norm)).astype(jnp.bfloat16)
    return (joined, pre_act, hidden, pre_norm, updated)


def mlp_back(inputs_rows, pre_act, hidden, pre_norm, grad_out, w_one, w_two):
    grad_norm = norm_back(pre_norm, grad_out).astype(jnp.bfloat16)
    grad_w_two = outer_sum(hidden, grad_norm)
    grad_hidden = jnp.dot(grad_norm, w_two.T, preferred_element_type=jnp.float32)
    grad_pre = (grad_hidden * silu_slope(pre_act)).astype(jnp.bfloat16)
    grad_w_one = outer_sum(inputs_rows, grad_pre)
    grad_inputs = jnp.dot(grad_pre, w_one.T, preferred_element_type=jnp.float32)
    return (grad_inputs, grad_w_one, grad_w_two)


def local(
    node_features,
    edge_features,
    coarse_features,
    edge_w_one,
    edge_w_two,
    node_w_one,
    node_w_two,
    coarse_w_one,
    coarse_w_two,
    edge_source,
    edge_target,
    boundary,
    ghost_pos,
    restr_order,
    restr_count,
    coarse_slot,
    node_cotangent,
    edge_cotangent,
    coarse_cotangent,
):
    latent = node_features.shape[1]
    here_rows = node_features.shape[0]
    groups = lax.axis_size("group")
    domains = lax.axis_size("dom")
    part_total = groups * domains
    border = boundary.reshape(-1)
    border_count = border.shape[0]
    requests = ghost_pos.reshape(domains, -1)
    shared = node_features[border]
    published = lax.all_gather(shared, "dom", axis=0, tiled=True)
    wanted = (jnp.arange(domains, dtype=jnp.int32)[:, None] * border_count + requests).reshape(-1)
    ghosts = published[wanted]
    lookup = jnp.concatenate([node_features, ghosts], axis=0)
    stacked, edge_pre, edge_hidden, message = edge_forward(
        lookup, edge_features, edge_source, edge_target, edge_w_one, edge_w_two
    )
    joined, node_pre, node_hidden, node_pre_norm, updated = node_forward(
        node_features, message, edge_target, node_w_one, node_w_two
    )
    counts = restr_count.reshape(-1)
    offsets = jnp.cumsum(counts) - counts
    capacity = coarse_slot.shape[2]
    slot_ids = jnp.arange(capacity, dtype=jnp.int32)
    is_valid = slot_ids[None, :] < counts[:, None]
    send_order = restr_order.reshape(-1)
    send_rows = send_order[jnp.minimum(offsets[:, None] + slot_ids[None, :], here_rows - 1)]
    keep_mask = is_valid[:, :, None].astype(jnp.bfloat16)
    coarse_rows = coarse_features.shape[0]
    sent_updated = updated[send_rows] * keep_mask
    sent_cotangent = node_cotangent[send_rows] * keep_mask
    got_updated, got_cotangent = (
        lax.all_to_all(sent_updated, "group", split_axis=0, concat_axis=0, tiled=True),
        lax.all_to_all(sent_cotangent, "group", split_axis=0, concat_axis=0, tiled=True),
    )
    coarse_ids = coarse_slot.reshape(-1)
    pooled_sum = jax.ops.segment_sum(
        got_updated.reshape(-1, latent).astype(jnp.float32), coarse_ids, num_segments=coarse_rows
    )
    from_fine = jax.ops.segment_sum(
        got_cotangent.reshape(-1, latent).astype(jnp.float32), coarse_ids, num_segments=coarse_rows
    )
    pooled = (pooled_sum * POOL_SHARE).astype(jnp.bfloat16)
    coarse_grad_out = (coarse_cotangent.astype(jnp.float32) + from_fine).astype(jnp.bfloat16)
    coarse_joined = jnp.concatenate([coarse_features, pooled], axis=1)
    coarse_pre = jnp.dot(coarse_joined, coarse_w_one, preferred_element_type=jnp.float32)
    coarse_hidden = jax.nn.silu(coarse_pre).astype(jnp.bfloat16)
    grad_c_two = outer_sum(coarse_hidden, coarse_grad_out)
    coarse_grad_hidden = jnp.dot(
        coarse_grad_out, coarse_w_two.T, preferred_element_type=jnp.float32
    )
    coarse_grad_pre = (coarse_grad_hidden * silu_slope(coarse_pre)).astype(jnp.bfloat16)
    grad_c_one = outer_sum(coarse_joined, coarse_grad_pre)
    coarse_grad_in = jnp.dot(coarse_grad_pre, coarse_w_one.T, preferred_element_type=jnp.float32)
    grad_coarse = coarse_cotangent.astype(jnp.float32) + coarse_grad_in[:, :latent]
    grad_pooled = coarse_grad_in[:, latent:] * POOL_SHARE
    returned = lax.all_to_all(
        grad_pooled[coarse_ids].reshape(groups, capacity, latent).astype(jnp.bfloat16),
        "group",
        split_axis=0,
        concat_axis=0,
        tiled=True,
    ).astype(jnp.float32)
    returned = returned * is_valid[:, :, None].astype(jnp.float32)
    fine_back = jax.ops.segment_sum(
        returned.reshape(-1, latent), send_rows.reshape(-1), num_segments=here_rows
    )
    updated_grad = node_cotangent.astype(jnp.float32) + fine_back
    node_grad_join, grad_v_one, grad_v_two = mlp_back(
        joined, node_pre, node_hidden, node_pre_norm, updated_grad, node_w_one, node_w_two
    )
    message_grad = edge_cotangent.astype(jnp.float32) + node_grad_join[:, latent:][edge_target]
    stacked_grad, grad_w_one, grad_w_two = mlp_back(
        stacked, edge_pre, edge_hidden, message, message_grad, edge_w_one, edge_w_two
    )
    grad_edges = edge_cotangent.astype(jnp.float32) + stacked_grad[:, 2 * latent :]
    lookup_grad = jax.ops.segment_sum(
        stacked_grad[:, :latent], edge_source, num_segments=lookup.shape[0]
    )
    target_grad = jax.ops.segment_sum(
        stacked_grad[:, latent : 2 * latent], edge_target, num_segments=here_rows
    )
    local_grad = updated_grad + node_grad_join[:, :latent] + lookup_grad[:here_rows] + target_grad
    ghost_grad = lookup_grad[here_rows:]
    gathered_grad = jax.ops.segment_sum(ghost_grad, wanted, num_segments=domains * border_count)
    border_grad = lax.psum_scatter(
        gathered_grad.astype(jnp.bfloat16), "dom", scatter_dimension=0, tiled=True
    ).astype(jnp.float32)
    grad_nodes = local_grad + jax.ops.segment_sum(border_grad, border, num_segments=here_rows)
    totals = lax.psum(
        (grad_w_one, grad_w_two, grad_v_one, grad_v_two, grad_c_one, grad_c_two), ("group", "dom")
    )
    edge_scale = (edge_features.shape[0] * part_total) ** (-0.5)
    node_scale = (here_rows * part_total) ** (-0.5)
    coarse_scale = (coarse_rows * part_total) ** (-0.5)
    return (
        grad_nodes,
        grad_edges,
        grad_coarse,
        totals[0] * edge_scale,
        totals[1] * edge_scale,
        totals[2] * node_scale,
        totals[3] * node_scale,
        totals[4] * coarse_scale,
        totals[5] * coarse_scale,
    )


def solution(mesh):
    placed = (
        P(("group", "dom"), None),
        P(("group", "dom"), None),
        P(("group", "dom"), None),
        P(),
        P(),
        P(),
        P(),
        P(),
        P(),
        P(("group", "dom")),
        P(("group", "dom")),
        P(("group", "dom"), None),
        P(("group", "dom"), None, None),
        P(("group", "dom"), None),
        P(("group", "dom"), None),
        P(("group", "dom"), None, None),
        P(("group", "dom"), None),
        P(("group", "dom"), None),
        P(("group", "dom"), None),
    )
    return jax.shard_map(
        local,
        mesh=mesh,
        in_specs=placed,
        out_specs=(
            P(("group", "dom"), None),
            P(("group", "dom"), None),
            P(("group", "dom"), None),
            P(),
            P(),
            P(),
            P(),
            P(),
            P(),
        ),
        check_vma=False,
    )
```

profile of v0, /device:TPU:1, one launch (start us, length us, event | category | flops | bytes accessed | tf_op | source)
XLA Modules:
  0.0 486.0 jit_solution(10884135439350040282)
XLA Ops:
  13.7 8.6 %gather_fusion = s32[2048]{0:T(1024)S(1)} fusion(s32[1024]{0:T(1024)S(1)} %bitcast.61, s32[2048]{0:T(1024)S(1)} %broadcast_clamp_fusion.2), kind=kCustom, calls=%fused_computation | custom fusion | bytes 24576 | tf_op jit(solution)/shard_map/gather | solution.py:112
  23.3 8.1 %gather_fusion.1 = bf16[2048,128]{1,0:T(8,128)(2,1)} fusion(bf16[1024,128]{1,0:T(8,128)(2,1)S(1)} %copy-done.2, s32[2048]{0:T(1024)S(1)} %get-tuple-element.53), kind=kCustom, calls=%fused_computation.1 | custom fusion | bytes 1056768 | tf_op jit(solution)/shard_map/gather | solution.py:116
  33.3 24.9 %all-gather.3.cloned.1.call-done = bf16[8192,128]{1,0:T(8,128)(2,1)} async-done(((bf16[256,128]{1,0:T(8,128)(2,1)}), bf16[8192,128]{1,0:T(8,128)(2,1)}) %all-gather.3.cloned.1.call-update) | async-done | bytes 2097168 | tf_op jit(solution)/shard_map/all_gather | solution.py:96
  61.2 12.1 %gather_fusion.5 = bf16[4096,128]{1,0:T(8,128)(2,1)S(1)} fusion(bf16[1536,128]{1,0:T(8,128)(2,1)S(1)} %constant_dynamic-update-slice_fusion, s32[4096]{0:T(1024)S(1)} %get-tuple-element.38), kind=kCustom, calls=%fused_computation.5 | custom fusion | bytes 2113536 | tf_op jit(solution)/shard_map/gather | solution.py:38
  73.3 12.1 %gather_fusion.4 = bf16[4096,128]{1,0:T(8,128)(2,1)S(1)} fusion(bf16[1536,128]{1,0:T(8,128)(2,1)S(1)} %constant_dynamic-update-slice_fusion, s32[4096]{0:T(1024)S(1)} %get-tuple-element.51), kind=kCustom, calls=%fused_computation.4 | custom fusion | bytes 2113536 | tf_op jit(solution)/shard_map/gather | solution.py:38
  94.9 22.8 %scatter_custom_fusion.1 = f32[1024,128]{1,0:T(8,128)S(1)} fusion(s32[4096]{0:T(1024)S(1)} %copy-done.39, f32[4096,128]{1,0:T(8,128)} %copy.43, f32[]{:T(128)} %constant.18.clone.1), kind=kCustom, calls=%fused_computation.59 | custom fusion | flops 524288 | bytes 524800 | tf_op jit(solution)/shard_map/scatter-add | solution.py:47
  120.8 8.0 %gather_fusion.6 = bf16[2048,128]{1,0:T(8,128)(2,1)} fusion(bf16[1024,128]{1,0:T(8,128)(2,1)S(1)} %copy.44, s32[2048]{0:T(1024)S(1)} %get-tuple-element.53), kind=kCustom, calls=%fused_computation.6 | custom fusion | bytes 1056768 | tf_op jit(solution)/shard_map/gather | solution.py:115
  131.1 13.1 %all_to_all.15 = bf16[4,512,128]{2,1,0:T(8,128)(2,1)} all-to-all(bf16[4,512,128]{2,1,0:T(8,128)(2,1)S(1)} %get-tuple-element.40), channel_id=1, replica_groups=mesh['group'=4,'dom'=32] {'group'}, dimensions={0} | all-to-all | bytes 1048576 | tf_op jit(solution)/shard_map/all_to_all | solution.py:118
  144.2 4.1 all-to-all-start
  152.2 12.1 %scatter_custom_fusion.2 = f32[256,128]{1,0:T(8,128)S(1)} fusion(s32[2048]{0:T(1024)S(1)} %bitcast.73, bf16[2048,128]{1,0:T(8,128)(2,1)} %bitcast.65, f32[]{:T(128)} %constant.18.clone.1), kind=kCustom, calls=%fused_computation.37 | custom fusion | flops 524288 | bytes 655364 | tf_op jit(solution)/shard_map/scatter-add | solution.py:122
  164.3 12.3 %scatter_custom_fusion = f32[256,128]{1,0:T(8,128)} fusion(f32[256,128]{1,0:T(8,128)} %convert_element_type.94, s32[2048]{0:T(1024)} %bitcast.74, bf16[2048,128]{1,0:T(8,128)(2,1)} %bitcast.16), kind=kCustom, calls=%fused_computation.39 | custom fusion | flops 524288 | bytes 655360 | tf_op jit(solution)/shard_map/scatter-add | solution.py:125
  181.1 8.9 %gather_fusion.7 = bf16[2048,128]{1,0:T(8,128)(2,1)} fusion(bf16[256,128]{1,0:T(8,128)(2,1)S(1)} %slice_multiply_fusion, s32[2048]{0:T(1024)} %get-tuple-element.52), kind=kCustom, calls=%fused_computation.7 | custom fusion | bytes 1056768 | tf_op jit(solution)/shard_map/gather | solution.py:143
  190.0 4.3 all-to-all-start.2
  197.1 4.6 all-to-all-done.2
  204.1 13.2 %scatter_fusion = f32[1024,128]{1,0:T(8,128)S(1)} fusion(f32[1024,128]{1,0:T(8,128)S(1)} %convert_element_type.93, s32[2048]{0:T(1024)S(1)} %copy-done.27, f32[2048,128]{1,0:T(8,128)} %bitcast.62), kind=kCustom, calls=%fused_computation.12 | custom fusion | flops 262144 | bytes 3153920 | tf_op jit(solution)/shard_map/scatter-add | solution.py:150
  224.6 14.1 %gather_fusion.8 = f32[4096,128]{1,0:T(8,128)} fusion(f32[1024,128]{1,0:T(8,128)S(1)} %slice.56, s32[4096]{0:T(1024)S(1)} %copy-done.29), kind=kCustom, calls=%fused_computation.8 | custom fusion | bytes 4210688 | tf_op jit(solution)/shard_map/gather | solution.py:157
  238.6 3.0 copy.48
  251.2 3.6 fusion.45
  254.8 20.9 %scatter_custom_fusion.4 = f32[1536,128]{1,0:T(8,128)S(1)} fusion(s32[4096]{0:T(1024)} %param.28, f32[4096,384]{1,0:T(8,128)} %fusion.45, f32[]{:T(128)} %constant.18.clone.1), kind=kCustom, calls=%fused_computation.23 | custom fusion | flops 524288 | bytes 2884096 | tf_op jit(solution)/shard_map/scatter-add | solution.py:162
  275.7 4.6 scatter_custom_fusion.6
  280.4 3.7 convert_element_type.117
  287.8 24.6 %scatter_custom_fusion.5 = f32[1024,128]{1,0:T(8,128)} fusion(f32[1024,128]{1,0:T(8,128)} %slice_add_fusion, s32[4096]{0:T(1024)} %param.29, f32[4096,384]{1,0:T(8,128)} %fusion.45), kind=kCustom, calls=%fused_computation.21 | custom fusion | flops 524288 | bytes 2621440 | tf_op jit(solution)/shard_map/scatter-add | solution.py:165
  318.1 80.2 %all-reduce.3.cloned.1.call-done = (f32[384,128]{1,0:T(8,128)}, f32[128,128]{1,0:T(8,128)}, f32[256,128]{1,0:T(8,128)}, f32[128,128]{1,0:T(8,128)}, f32[256,128]{1,0:T(8,128)}, /*index=5*/f32[128,128]{1,0:T(8,128)}) async-done(((f32[384,128]{1,0:T(8,128)}, f32[128,128]{1,0:T(8,128)}, f32[256,128]{1,0:T(8,128)}, f32[128,128]{1,0:T(8,128)}, f32[256,128]{1,0:T(8,128)}, /*index=5*/f32[128,128]{1,0:T(8,128)}), ...) | async-done | bytes 655376 | tf_op jit(solution)/shard_map/psum | solution.py:175
  407.5 69.2 %reduce-scatter.2.cloned.1.call-done = bf16[256,128]{1,0:T(8,128)(2,1)} async-done(((bf16[8192,128]{1,0:T(8,128)(2,1)}), bf16[256,128]{1,0:T(8,128)(2,1)}) %reduce-scatter.2.cloned.1.call-update) | async-done | bytes 65552 | tf_op jit(solution)/shard_map/reduce_scatter | solution.py:171
  (188 shorter events, 78.4 us)
Async XLA Ops:
  7.2 79.8 %copy-start = (bf16[384,128]{1,0:T(8,128)(2,1)S(1)}, bf16[384,128]{1,0:T(8,128)(2,1)}, u32[]{:S(2)}) copy-start(bf16[384,128]{1,0:T(8,128)(2,1)} %param.22) | copy-start | bytes 294916
  7.2 6.5 %copy-start.1 = (s32[1,1024]{1,0:T(1,128)S(1)}, s32[1,1024]{1,0:T(1,128)}, u32[]{:S(2)}) copy-start(s32[1,1024]{1,0:T(1,128)} %param.32) | copy-start | bytes 12292
  7.2 51.0 %all-gather.3.cloned.1.call-start = ((), (), s32[]{:S(2)}) async-start(), calls=%async_computation.5 | async-start | bytes 2162688 | tf_op jit(solution)/shard_map/all_gather | solution.py:96
  13.7 8.7 %copy-start.35 = (s32[1,4,512]{2,1,0:T(4,128)S(1)}, s32[1,4,512]{2,1,0:T(4,128)}, u32[]{:S(2)}) copy-start(s32[1,4,512]{2,1,0:T(4,128)} %param.34) | copy-start | bytes 24580
  13.7 8.9 %copy-start.40 = (s32[1,32,16]{1,2,0:T(8,128)S(1)}, s32[1,32,16]{1,2,0:T(8,128)}, u32[]{:S(2)}) copy-start(s32[1,32,16]{1,2,0:T(8,128)} %param.31) | copy-start | bytes 6148
  13.7 9.6 %copy-start.2 = (bf16[1024,128]{1,0:T(8,128)(2,1)S(1)}, bf16[1024,128]{1,0:T(8,128)(2,1)}, u32[]{:S(2)}) copy-start(bf16[1024,128]{1,0:T(8,128)(2,1)} %param.35) | copy-start | bytes 786436
  22.3 9.1 %copy-start.26 = (s32[2048]{0:T(1024)}, s32[2048]{0:T(1024)S(1)}, u32[]{:S(2)}) copy-start(s32[2048]{0:T(1024)S(1)} %gather_fusion) | copy-start | bytes 24580
  23.3 8.7 %copy-start.9 = (bf16[1024,128]{1,0:T(8,128)(2,1)S(1)}, bf16[1024,128]{1,0:T(8,128)(2,1)}, u32[]{:S(2)}) copy-start(bf16[1024,128]{1,0:T(8,128)(2,1)} %param.19) | copy-start | bytes 786436
  23.3 8.7 %copy-start.42 = (s32[1,4]{1,0:T(1,128)S(1)}, s32[1,4]{1,0:T(1,128)}, u32[]{:S(2)}) copy-start(s32[1,4]{1,0:T(1,128)} %param.33) | copy-start | bytes 52
  23.3 9.4 %copy-start.38 = (s32[4096]{0:T(1024)S(1)}, s32[4096]{0:T(1024)}, u32[]{:S(2)}) copy-start(s32[4096]{0:T(1024)} %param.28) | copy-start | bytes 49156
  23.3 9.4 %copy-start.39 = (s32[4096]{0:T(1024)S(1)}, s32[4096]{0:T(1024)}, u32[]{:S(2)}) copy-start(s32[4096]{0:T(1024)} %param.29) | copy-start | bytes 49156
  120.8 8.0 %copy-start.37 = (bf16[4,512]{1,0:T(4,128)(2,1)S(1)}, bf16[4,512]{1,0:T(4,128)(2,1)}, u32[]{:S(2)}) copy-start(bf16[4,512]{1,0:T(4,128)(2,1)} %get-tuple-element.42) | copy-start | bytes 12292
  128.7 19.6 %copy-start.36 = (s32[1,4,512]{2,1,0:T(4,128)S(1)}, s32[1,4,512]{2,1,0:T(4,128)}, u32[]{:S(2)}) copy-start(s32[1,4,512]{2,1,0:T(4,128)} %param.34) | copy-start | bytes 24580
  144.2 20.2 %all-to-all-start = ((bf16[4,512,128]{2,1,0:T(8,128)(2,1)}), bf16[4,512,128]{2,1,0:T(8,128)(2,1)}, u32[]{:S(2)}, u32[]{:S(2)}) async-start(bf16[4,512,128]{2,1,0:T(8,128)(2,1)} %get-tuple-element.39), calls=%async_computation | async-start | bytes 1048576 | tf_op jit(solution)/shard_map/all_to_all | solution.py:119
  148.4 28.2 %copy-start.22 = (bf16[256,128]{1,0:T(8,128)(2,1)S(1)}, bf16[256,128]{1,0:T(8,128)(2,1)}, u32[]{:S(2)}) copy-start(bf16[256,128]{1,0:T(8,128)(2,1)} %param.21) | copy-start | bytes 196612
  148.4 3.8 copy-start.41
  181.1 13.3 %copy-start.23 = (bf16[256,128]{1,0:T(8,128)(2,1)S(1)}, bf16[256,128]{1,0:T(8,128)(2,1)}, u32[]{:S(2)}) copy-start(bf16[256,128]{1,0:T(8,128)(2,1)} %param.21) | copy-start | bytes 196612
  181.1 20.6 %copy-start.32 = (f32[4,512]{1,0:T(4,128)S(1)}, f32[4,512]{1,0:T(4,128)}, u32[]{:S(2)}) copy-start(f32[4,512]{1,0:T(4,128)} %get-tuple-element.41) | copy-start | bytes 24580
  190.0 14.1 %copy-start.27 = (s32[2048]{0:T(1024)S(1)}, s32[2048]{0:T(1024)}, u32[]{:S(2)}) copy-start(s32[2048]{0:T(1024)} %copy-done.26) | copy-start | bytes 24580
  190.0 11.7 %all-to-all-start.2 = ((bf16[4,512,128]{2,1,0:T(8,128)(2,1)}), bf16[4,512,128]{2,1,0:T(8,128)(2,1)}, u32[]{:S(2)}, u32[]{:S(2)}) async-start(bf16[4,512,128]{2,1,0:T(8,128)(2,1)} %bitcast.63), calls=%async_computation.2 | async-start | bytes 1048576 | tf_op jit(solution)/shard_map/all_to_all | solution.py:142
  194.3 204.0 %all-reduce.3.cloned.1.call-start = ((), (), s32[]{:S(2)}) async-start(), calls=%async_computation.6 | async-start | bytes 1310720 | tf_op jit(solution)/shard_map/psum | solution.py:175
  250.9 225.8 %reduce-scatter.2.cloned.1.call-start = ((), (), s32[]{:S(2)}) async-start(), calls=%async_computation.4 | async-start | bytes 2162688 | tf_op jit(solution)/shard_map/reduce_scatter | solution.py:171
  286.9 25.5 %slice-start = ((f32[4096,384]{1,0:T(8,128)}), f32[4096,128]{1,0:T(8,128)S(1)}, s32[]{:S(2)}) async-start(f32[4096,384]{1,0:T(8,128)} %fusion.45), calls=%async_computation.7 | async-start | bytes 4194304 | tf_op jit(solution)/shard_map/slice | solution.py:161
  316.3 162.3 %copy-start.13 = (f32[1024,128]{1,0:T(8,128)S(1)}, f32[1024,128]{1,0:T(8,128)}, u32[]{:S(2)}) copy-start(f32[1024,128]{1,0:T(8,128)} %scatter_custom_fusion.5) | copy-start | bytes 1572868
  (27 other events, 47.7 us)
Sparse Core Ops, SparseCore 0:
  10.9 47.3 all-gather.2
  251.0 147.2 all-reduce.2
  401.9 74.8 reduce-scatter.1
where the time goes:
time: 488 us; the launch traced here: 486 us
  waiting for transfers between devices  179 us (37%)
  other arithmetic  149 us (31%)
  local copies, waits for them, and re-layouts  101 us (21%)
  matrix products  20.9 us (4%)
  between operations  14.5 us (3%)
  blocking collectives  13.1 us (3%)
  starting transfers between devices  8.77 us (2%)
    psum x1, waiting for transfers between devices, local(): lax.psum((grad_w_one, grad_w_two, grad_v_one, grad_v_two, grad_c_one, gra...  80.2 us
    reduce_scatter x1, waiting for transfers between devices, local(): lax.psum_scatter(gathered_grad.astype(jnp.bfloat16), 'dom', scatter_dimen...  69.2 us
    all_gather x1, waiting for transfers between devices, local(): published = lax.all_gather(shared, 'dom', axis=0, tiled=True)  24.9 us
    scatter-add x1, other arithmetic, local(): jax.ops.segment_sum(stacked_grad[:, latent:2 * latent], edge_target, num_...  24.6 us
    gather x2, local copies, waits for them, and re-layouts, edge_forward(): stacked = jnp.concatenate([lookup[source], lookup[target], edges], axis=1)  24.3 us
    scatter-add x1, other arithmetic, node_forward(): jax.ops.segment_sum(norm_rows(message), target, num_segments=row_count)  22.8 us
    scatter-add x1, other arithmetic, local(): jax.ops.segment_sum(stacked_grad[:, :latent], edge_source, num_segments=l...  20.9 us
    gather x2, local copies, waits for them, and re-layouts, local(): node_grad_join[:, latent:][edge_target]  17.1 us
  transfers between devices with their start and end apart: 5, of which 4 were waited for; matrix products, arithmetic and copies ran while one was open for 24% of the time, Pallas kernels for 0%

commit v1 on v0

v1 whole, which is shorter than its diff:
```python
import functools

import jax
import jax.numpy as jnp
from jax import lax
from jax.experimental import pallas as pl
from jax.experimental.pallas import tpu as pltpu
from jax.sharding import PartitionSpec as P

NORM_EPSILON = 1e-05
POOL_SHARE = 0.25
BF = jnp.bfloat16
F32 = jnp.float32
I32 = jnp.int32
LANES = 128
VMEM_BYTES = 48 * 1024 * 1024


def nn(a, b):
    return lax.dot_general(a, b, (((1,), (0,)), ((), ())), preferred_element_type=F32)


def nt(a, b):
    return lax.dot_general(a, b, (((1,), (1,)), ((), ())), preferred_element_type=F32)


def tn(a, b):
    return lax.dot_general(a, b, (((0,), (0,)), ((), ())), preferred_element_type=F32)


def as_hit(mask):
    return jnp.where(mask, 1.0, 0.0).astype(BF)


def hit_rows(index_row, count, base=0):
    width = index_row.shape[1]
    return as_hit(lax.broadcasted_iota(I32, (count, width), 0) == index_row - base)


def spread_column(index_row):
    width = index_row.shape[1]
    return jnp.transpose(jnp.broadcast_to(index_row, (LANES, width)))


def hit_columns(index_column, count, base=0):
    lane = lax.broadcasted_iota(I32, index_column.shape, 1)
    return jnp.concatenate(
        [as_hit(lane == index_column - (base + LANES * j)) for j in range(count // LANES)], axis=1
    )


def split_wide(values):
    high = values.astype(BF)
    low = (values - high.astype(F32)).astype(BF)
    return jnp.concatenate([high, low], axis=1)


def fold_wide(values):
    return values[:, :LANES] + values[:, LANES:]


def times_transposed(values, weights):
    return nt(split_wide(values), jnp.concatenate([weights, weights], axis=1))


def mean_lanes(values):
    return jnp.mean(values, axis=-1, keepdims=True)


def norm_parts(values):
    centred = values - mean_lanes(values)
    inv_std = lax.rsqrt(mean_lanes(centred * centred) + NORM_EPSILON)
    return centred * inv_std, inv_std


def norm_back(normed, inv_std, grad_in):
    return inv_std * (grad_in - mean_lanes(grad_in) - normed * mean_lanes(grad_in * normed))


def sigmoid(values):
    return 1.0 / (1.0 + jnp.exp(-values))


def slope(values, sig):
    return sig * (1.0 + values * (1.0 - sig))


def share_kernel(boundary_ref, wanted_ref, nodes_ref, out_ref):
    rows = nodes_ref.shape[0]
    border = boundary_ref.shape[1]
    shared = nn(hit_columns(spread_column(boundary_ref[...]), rows), nodes_ref[...]).astype(BF)
    out_ref[...] = nn(hit_columns(spread_column(wanted_ref[...]), border), shared).astype(BF)


def route_kernel(count_ref, slot_ref, order_ref, cot_ref, pool_ref, back_ref, cot_pool_ref):
    groups, capacity = slot_ref.shape
    rows = order_ref.shape[1]
    coarse = pool_ref.shape[0] // groups
    place = lax.broadcasted_iota(I32, (8, rows), 1)
    goal = jnp.zeros((8, rows), I32)
    start = 0
    for k in range(groups):
        count = count_ref[0, k]
        line = jnp.concatenate(
            [slot_ref[k : k + 1, :], jnp.zeros((1, rows - capacity), I32)], axis=1
        )
        line = pltpu.roll(jnp.broadcast_to(line, (8, rows)), start, 1)
        inside = (place >= start) & (place < start + count)
        goal = jnp.where(inside, line + k * coarse, goal)
        start = start + count
    to_coarse = hit_rows(goal[0:1, :], groups * coarse)
    to_fine = hit_rows(order_ref[...], rows)
    pool = nt(to_coarse, to_fine).astype(BF)
    pool_ref[...] = pool
    back_ref[...] = nt(to_fine, to_coarse).astype(BF)
    cot_pool_ref[...] = nn(pool, cot_ref[...]).astype(BF)


def edge_first_kernel(source_ref, target_ref, nodes_ref, edges_ref, w_ref, src_ref, tgt_ref, pre_ref):
    rows = nodes_ref.shape[0]
    nodes = nodes_ref[...]
    src = nn(hit_columns(spread_column(source_ref[...]), rows), nodes).astype(BF)
    tgt = nn(hit_columns(spread_column(target_ref[...]), rows), nodes).astype(BF)
    src_ref[...] = src
    tgt_ref[...] = tgt
    pre_ref[...] = nn(jnp.concatenate([src, tgt, edges_ref[...]], axis=1), w_ref[...])


def edge_second_kernel(
    source_ref, target_ref, pre_in_ref, src_in_ref, ghosts_ref, w1_ref, w2_ref,
    nodes_ref, v1_ref, v2_ref, pool_ref, cot_pool_ref,
    pre_ref, src_ref, summed_ref, send_ref, total,
):
    step = pl.program_id(0)
    rows = nodes_ref.shape[0]
    ghost_count = ghosts_ref.shape[0]

    @pl.when(step == 0)
    def _():
        total[...] = jnp.zeros_like(total)

    found = nn(
        hit_columns(spread_column(source_ref[...]), ghost_count, rows), ghosts_ref[...]
    ).astype(BF)
    src_ref[...] = src_in_ref[...] + found
    pre = pre_in_ref[...] + nn(found, w1_ref[:LANES, :])
    pre_ref[...] = pre
    hidden = (pre * sigmoid(pre)).astype(BF)
    message, _ = norm_parts(nn(hidden, w2_ref[...]))
    total[...] += nn(hit_rows(target_ref[...], rows), split_wide(message))

    @pl.when(step == pl.num_programs(0) - 1)
    def _():
        summed = fold_wide(total[...]).astype(BF)
        summed_ref[...] = summed
        nodes = nodes_ref[...]
        pre_node = nn(jnp.concatenate([nodes, summed], axis=1), v1_ref[...])
        hidden_node = (pre_node * sigmoid(pre_node)).astype(BF)
        normed, _ = norm_parts(nn(hidden_node, v2_ref[...]))
        updated = (nodes.astype(F32) + normed).astype(BF)
        pooled = nn(pool_ref[...], updated).astype(BF)
        groups = send_ref.shape[0]
        coarse = send_ref.shape[1] // 2
        for k in range(groups):
            send_ref[k, :coarse, :] = pooled[k * coarse : (k + 1) * coarse, :]
            send_ref[k, coarse:, :] = cot_pool_ref[k * coarse : (k + 1) * coarse, :]


def coarse_kernel(
    got_ref, feat_ref, cot_ref, w1_ref, w2_ref, grad_ref, back_ref, g1_ref, g2_ref
):
    groups = got_ref.shape[0]
    coarse = feat_ref.shape[0]
    got = got_ref[0].astype(F32)
    for k in range(1, groups):
        got = got + got_ref[k].astype(F32)
    pooled = (got[:coarse] * POOL_SHARE).astype(BF)
    cot = cot_ref[...].astype(F32)
    grad_out = (cot + got[coarse:]).astype(BF)
    joined = jnp.concatenate([feat_ref[...], pooled], axis=1)
    pre = nn(joined, w1_ref[...])
    sig = sigmoid(pre)
    hidden = (pre * sig).astype(BF)
    g2_ref[...] = tn(hidden, grad_out)
    grad_pre = (nt(grad_out, w2_ref[...]) * slope(pre, sig)).astype(BF)
    g1_ref[...] = tn(joined, grad_pre)
    grad_in = nt(grad_pre, w1_ref[...])
    grad_ref[...] = cot + grad_in[:, :LANES]
    back = (grad_in[:, LANES:] * POOL_SHARE).astype(BF)
    for k in range(groups):
        back_ref[k] = back


def edge_back_kernel(
    target_ref, pre_ref, src_ref, tgt_ref, edges_ref, cot_ref, w1_ref, w2_ref,
    gp_ref, back_ref, node_cot_ref, nodes_ref, summed_ref, v1_ref, v2_ref, c1_ref, c2_ref,
    grad_pre_ref, local_ref, pack_ref, wide, gw1, gw2, gv1, gv2,
):
    step = pl.program_id(0)
    rows = nodes_ref.shape[0]

    @pl.when(step == 0)
    def _():
        gw1[...] = jnp.zeros_like(gw1)
        gw2[...] = jnp.zeros_like(gw2)
        updated_grad = node_cot_ref[...].astype(F32) + nn(back_ref[...], gp_ref[...])
        joined = jnp.concatenate([nodes_ref[...], summed_ref[...]], axis=1)
        pre = nn(joined, v1_ref[...])
        sig = sigmoid(pre)
        hidden = (pre * sig).astype(BF)
        normed, inv_std = norm_parts(nn(hidden, v2_ref[...]))
        grad_norm = norm_back(normed, inv_std, updated_grad).astype(BF)
        gv2[...] = tn(hidden, grad_norm)
        grad_pre = (nt(grad_norm, v2_ref[...]) * slope(pre, sig)).astype(BF)
        gv1[...] = tn(joined, grad_pre)
        grad_in = nt(grad_pre, v1_ref[...])
        local_ref[...] = updated_grad + grad_in[:, :LANES]
        wide[...] = split_wide(grad_in[:, LANES:])

    from_node = fold_wide(nn(hit_columns(spread_column(target_ref[...]), rows), wide[...]))
    message_grad = cot_ref[...].astype(F32) + from_node
    pre = pre_ref[...]
    sig = sigmoid(pre)
    hidden = (pre * sig).astype(BF)
    normed, inv_std = norm_parts(nn(hidden, w2_ref[...]))
    grad_norm = norm_back(normed, inv_std, message_grad).astype(BF)
    gw2[...] += tn(hidden, grad_norm)
    grad_pre = (nt(grad_norm, w2_ref[...]) * slope(pre, sig)).astype(BF)
    grad_pre_ref[...] = grad_pre
    stacked = jnp.concatenate([src_ref[...], tgt_ref[...], edges_ref[...]], axis=1)
    gw1[...] += tn(stacked, grad_pre)

    @pl.when(step == pl.num_programs(0) - 1)
    def _():
        place = 0
        for part in (gw1, gw2, gv1, gv2, c1_ref, c2_ref):
            size = part.shape[0]
            pack_ref[place : place + size, :] = part[...].astype(BF)
            place += size
        pack_ref[place:, :] = jnp.zeros((pack_ref.shape[0] - place, LANES), BF)


def ghost_back_kernel(source_ref, grad_pre_ref, w1_ref, out_ref, total, *, rows):
    step = pl.program_id(0)

    @pl.when(step == 0)
    def _():
        total[...] = jnp.zeros_like(total)

    total[...] += nn(hit_rows(source_ref[...], total.shape[0], rows), grad_pre_ref[...])

    @pl.when(step == pl.num_programs(0) - 1)
    def _():
        out_ref[...] = times_transposed(total[...], w1_ref[:LANES, :]).astype(BF)


def own_back_kernel(
    source_ref, target_ref, grad_pre_ref, cot_ref, local_ref, w1_ref,
    out_ref, edges_ref, by_source, by_target,
):
    step = pl.program_id(0)
    rows = by_source.shape[0]

    @pl.when(step == 0)
    def _():
        by_source[...] = jnp.zeros_like(by_source)
        by_target[...] = jnp.zeros_like(by_target)

    grad_pre = grad_pre_ref[...]
    by_source[...] += nn(hit_rows(source_ref[...], rows), grad_pre)
    by_target[...] += nn(hit_rows(target_ref[...], rows), grad_pre)
    edges_ref[...] = cot_ref[...].astype(F32) + nt(grad_pre, w1_ref[2 * LANES :, :])

    @pl.when(step == pl.num_programs(0) - 1)
    def _():
        out_ref[...] = (
            local_ref[...]
            + times_transposed(by_source[...], w1_ref[:LANES, :])
            + times_transposed(by_target[...], w1_ref[LANES : 2 * LANES, :])
        )


def add_back_kernel(boundary_ref, wanted_ref, got_ref, local_ref, out_ref):
    rows = local_ref.shape[0]
    border = boundary_ref.shape[1]
    border_grad = nn(hit_rows(wanted_ref[...], border), got_ref[...])
    out_ref[...] = local_ref[...] + fold_wide(
        nn(hit_rows(boundary_ref[...], rows), split_wide(border_grad))
    )


def add_parts_kernel(got_ref, out_ref):
    parts = got_ref.shape[0]
    total = got_ref[0].astype(F32)
    for k in range(1, parts):
        total = total + got_ref[k].astype(F32)
    total = total.astype(BF)
    for k in range(parts):
        out_ref[k] = total


def scale_kernel(pack_ref, *out_refs, scales):
    place = 0
    for out_ref, scale in zip(out_refs, scales):
        size = out_ref.shape[0]
        out_ref[...] = pack_ref[place : place + size, :].astype(F32) * scale
        place += size


def whole(shape):
    zeros = (0,) * len(shape)
    return pl.BlockSpec(shape, lambda *_: zeros)


def call(kernel, out_shapes, *args, flops=0, bytes_accessed=0, in_specs=None, out_specs=None,
         grid=None, scratch=(), name=None):
    single = not isinstance(out_shapes, (list, tuple))
    extra = {}
    if grid is not None:
        extra["grid"] = grid
    if in_specs is not None:
        extra["in_specs"] = in_specs
    if out_specs is not None:
        extra["out_specs"] = out_specs
    return pl.pallas_call(
        kernel,
        out_shape=out_shapes if single else list(out_shapes),
        scratch_shapes=list(scratch),
        compiler_params=pltpu.CompilerParams(vmem_limit_bytes=VMEM_BYTES),
        cost_estimate=pl.CostEstimate(
            flops=flops, bytes_accessed=bytes_accessed, transcendentals=0
        ),
        name=name,
        **extra,
    )(*args)


def local(
    node_features, edge_features, coarse_features,
    edge_w_one, edge_w_two, node_w_one, node_w_two, coarse_w_one, coarse_w_two,
    edge_source, edge_target, boundary, ghost_pos, restr_order, restr_count, coarse_slot,
    node_cotangent, edge_cotangent, coarse_cotangent,
):
    rows, latent = node_features.shape
    edges = edge_features.shape[0]
    coarse = coarse_features.shape[0]
    groups = lax.axis_size("group")
    domains = lax.axis_size("dom")
    parts = groups * domains
    slots = ghost_pos.shape[2]
    ghosts = domains * slots
    shape = jax.ShapeDtypeStruct
    block = 512
    grid = (edges // block,)
    index_spec = pl.BlockSpec((1, block), lambda i: (0, i))
    edge_spec = pl.BlockSpec((block, latent), lambda i: (i, 0))
    exchange = functools.partial(lax.all_to_all, split_axis=0, concat_axis=0, tiled=True)

    source = edge_source.reshape(1, edges)
    target = edge_target.reshape(1, edges)
    asked = exchange(ghost_pos.reshape(domains, slots), "dom").reshape(1, ghosts)
    coarse_to = exchange(coarse_slot.reshape(groups, -1), "group")

    share = call(
        share_kernel, shape((ghosts, latent), BF), boundary, asked, node_features,
        flops=10**9, bytes_accessed=10**6, name="share",
    )
    ghost_rows = exchange(share.reshape(domains, slots, latent), "dom").reshape(ghosts, latent)

    src_own, tgt_rows, pre_part = call(
        edge_first_kernel,
        [shape((edges, latent), BF), shape((edges, latent), BF), shape((edges, latent), F32)],
        source, target, node_features, edge_features, edge_w_one,
        grid=grid,
        in_specs=[index_spec, index_spec, whole((rows, latent)), edge_spec, whole((3 * latent, latent))],
        out_specs=[edge_spec, edge_spec, edge_spec],
        flops=5 * 10**9, bytes_accessed=6 * 10**6, name="edge_first",
    )
    pool, back, cot_pool = call(
        route_kernel,
        [shape((groups * coarse, rows), BF), shape((rows, groups * coarse), BF),
         shape((groups * coarse, latent), BF)],
        restr_count, coarse_to, restr_order, node_cotangent,
        in_specs=[pl.BlockSpec(memory_space=pltpu.SMEM)] + [pl.BlockSpec(memory_space=pltpu.VMEM)] * 3,
        flops=4 * 10**9, bytes_accessed=4 * 10**6, name="route",
    )
    pre, src_rows, summed, send = call(
        edge_second_kernel,
        [shape((edges, latent), F32), shape((edges, latent), BF), shape((rows, latent), BF),
         shape((groups, 2 * coarse, latent), BF)],
        source, target, pre_part, src_own, ghost_rows, edge_w_one, edge_w_two,
        node_features, node_w_one, node_w_two, pool, cot_pool,
        grid=grid,
        in_specs=[index_spec, index_spec, edge_spec, edge_spec, whole((ghosts, latent)),
                  whole((3 * latent, latent)), whole((latent, latent)), whole((rows, latent)),
                  whole((2 * latent, latent)), whole((latent, latent)),
                  whole((groups * coarse, rows)), whole((groups * coarse, latent))],
        out_specs=[edge_spec, edge_spec, whole((rows, latent)), whole((groups, 2 * coarse, latent))],
        scratch=[pltpu.VMEM((rows, 2 * latent), F32)],
        flops=5 * 10**9, bytes_accessed=8 * 10**6, name="edge_second",
    )
    got = exchange(send, "group")
    grad_coarse, coarse_back, grad_c_one, grad_c_two = call(
        coarse_kernel,
        [shape((coarse, latent), F32), shape((groups, coarse, latent), BF),
         shape((2 * latent, latent), F32), shape((latent, latent), F32)],
        got, coarse_features, coarse_cotangent, coarse_w_one, coarse_w_two,
        flops=10**8, bytes_accessed=10**6, name="coarse",
    )
    returned = exchange(coarse_back, "group").reshape(groups * coarse, latent)
    pack_rows = parts * 16
    grad_pre, node_local, pack = call(
        edge_back_kernel,
        [shape((edges, latent), BF), shape((rows, latent), F32), shape((pack_rows, latent), BF)],
        target, pre, src_rows, tgt_rows, edge_features, edge_cotangent, edge_w_one, edge_w_two,
        returned, back, node_cotangent, node_features, summed, node_w_one, node_w_two,
        grad_c_one, grad_c_two,
        grid=grid,
        in_specs=[index_spec, edge_spec, edge_spec, edge_spec, edge_spec, edge_spec,
                  whole((3 * latent, latent)), whole((latent, latent)),
                  whole((groups * coarse, latent)), whole((rows, groups * coarse)),
                  whole((rows, latent)), whole((rows, latent)), whole((rows, latent)),
                  whole((2 * latent, latent)), whole((latent, latent)),
                  whole((2 * latent, latent)), whole((latent, latent))],
        out_specs=[edge_spec, whole((rows, latent)), whole((pack_rows, latent))],
        scratch=[pltpu.VMEM((rows, 2 * latent), BF), pltpu.VMEM((3 * latent, latent), F32),
                 pltpu.VMEM((latent, latent), F32), pltpu.VMEM((2 * latent, latent), F32),
                 pltpu.VMEM((latent, latent), F32)],
        flops=6 * 10**9, bytes_accessed=10**7, name="edge_back",
    )
    pack_got = exchange(pack.reshape(parts, 16, latent), ("group", "dom"))
    ghost_grad = call(
        functools.partial(ghost_back_kernel, rows=rows), shape((ghosts, latent), BF),
        source, grad_pre, edge_w_one,
        grid=grid,
        in_specs=[index_spec, edge_spec, whole((3 * latent, latent))],
        out_specs=whole((ghosts, latent)),
        scratch=[pltpu.VMEM((ghosts, latent), F32)],
        flops=10**9, bytes_accessed=10**6, name="ghost_back",
    )
    ghost_got = exchange(ghost_grad.reshape(domains, slots, latent), "dom").reshape(ghosts, latent)
    own_local, grad_edges = call(
        own_back_kernel,
        [shape((rows, latent), F32), shape((edges, latent), F32)],
        source, target, grad_pre, edge_cotangent, node_local, edge_w_one,
        grid=grid,
        in_specs=[index_spec, index_spec, edge_spec, edge_spec, whole((rows, latent)),
                  whole((3 * latent, latent))],
        out_specs=[whole((rows, latent)), edge_spec],
        scratch=[pltpu.VMEM((rows, latent), F32), pltpu.VMEM((rows, latent), F32)],
        flops=4 * 10**9, bytes_accessed=5 * 10**6, name="own_back",
    )
    pack_sum = call(
        add_parts_kernel, shape((parts, 16, latent), BF), pack_got,
        flops=10**6, bytes_accessed=10**6, name="add_parts",
    )
    pack_all = exchange(pack_sum, ("group", "dom")).reshape(pack_rows, latent)
    grad_nodes = call(
        add_back_kernel, shape((rows, latent), F32), boundary, asked, ghost_got, own_local,
        flops=10**9, bytes_accessed=10**6, name="add_back",
    )
    edge_scale = (edges * parts) ** (-0.5)
    node_scale = (rows * parts) ** (-0.5)
    coarse_scale = (coarse * parts) ** (-0.5)
    weight_grads = call(
        functools.partial(
            scale_kernel,
            scales=(edge_scale, edge_scale, node_scale, node_scale, coarse_scale, coarse_scale),
        ),
        [shape((size * latent, latent), F32) for size in (3, 1, 2, 1, 2, 1)],
        pack_all,
        flops=10**6, bytes_accessed=10**6, name="scale",
    )
    return (grad_nodes, grad_edges, grad_coarse, *weight_grads)


def solution(mesh):
    rows = P(("group", "dom"), None)
    cube = P(("group", "dom"), None, None)
    line = P(("group", "dom"))
    placed = (
        rows, rows, rows, P(), P(), P(), P(), P(), P(), line, line, rows, cube, rows, rows, cube,
        rows, rows, rows,
    )
    return jax.shard_map(
        local,
        mesh=mesh,
        in_specs=placed,
        out_specs=(rows, rows, rows, P(), P(), P(), P(), P(), P()),
        check_vma=False,
    )
```

time: 488 us -> 158 us (0.32)
  waiting for transfers between devices: 179 us -> 23.4 us
  other arithmetic: 149 us -> 0.69 us
  local copies, waits for them, and re-layouts: 101 us -> 13.5 us
  Pallas kernels: 0 us -> 59 us
  starting transfers between devices: 8.77 us -> 40.2 us
  matrix products: 20.9 us -> 0 us
  between operations: 14.5 us -> 0.94 us
  blocking collectives: 13.1 us -> 19.7 us
    scatter-add x8 -> x0, other arithmetic: 112 us -> none  [the longest x1 24.6 us: local(): jax.ops.segment_sum(stacked_grad[:, latent:2 * latent], edge_target, num_...]
    psum x1 -> x0, waiting for transfers between devices: 80.2 us -> none  [local(): lax.psum((grad_w_one, grad_w_two, grad_v_one, grad_v_two, grad_c_one, gra...]
    gather x11 -> x0, local copies, waits for them, and re-layouts: 80.1 us -> none  [the longest x2 24.3 us: edge_forward(): stacked = jnp.concatenate([lookup[source], lookup[target], edges], axis=1)]
    reduce_scatter x1 -> x0, waiting for transfers between devices: 69.2 us -> none  [local(): lax.psum_scatter(gathered_grad.astype(jnp.bfloat16), 'dom', scatter_dimen...]
    pallas_call x0 -> x11, Pallas kernels: none -> 59 us  [call(): pl.pallas_call(kernel, out_shape=out_shapes if single else list(out_shape...]
    all_to_all x2 -> x6, starting transfers between devices: 8.46 us -> 40.2 us  [the longest x1 9.35 us: local(): pack_got = exchange(pack.reshape(parts, 16, latent), ('group', 'dom'))]
    all_gather x1 -> x0, waiting for transfers between devices: 24.9 us -> none  [local(): published = lax.all_gather(shared, 'dom', axis=0, tiled=True)]
    dot_general x17 -> x0, matrix products: 20.9 us -> none  [the longest x6 7.43 us: outer_sum(): lax.dot_general(first_op, second_op, (((0,), (0,)), ((), ())), preferred_...]
  transfers between devices with their start and end apart: 5 -> 6, of which waited for: 4 -> 4; matrix products, arithmetic and copies ran while one was open for 24% -> 1% of each run, Pallas kernels for 0% -> 17%
where the time goes in v1:
time: 158 us; the launch traced here: 157 us
  Pallas kernels  59 us (37%)
  starting transfers between devices  40.2 us (25%)
  waiting for transfers between devices  23.4 us (15%)
  blocking collectives  19.7 us (12%)
  local copies, waits for them, and re-layouts  13.5 us (9%)
    pallas_call x11, Pallas kernels, call(): pl.pallas_call(kernel, out_shape=out_shapes if single else list(out_shape...  59 us
    unnamed x58, local copies, waits for them, and re-layouts  12.3 us
    all_to_all x1, blocking collectives, local(): got = exchange(send, 'group')  11.8 us
    all_to_all x1, waiting for transfers between devices, local(): pack_got = exchange(pack.reshape(parts, 16, latent), ('group', 'dom'))  10.1 us
    all_to_all x1, starting transfers between devices, local(): pack_got = exchange(pack.reshape(parts, 16, latent), ('group', 'dom'))  9.35 us
    all_to_all x1, starting transfers between devices, local(): exchange(share.reshape(domains, slots, latent), 'dom')  8.81 us
    all_to_all x1, starting transfers between devices, local(): exchange(ghost_pos.reshape(domains, slots), 'dom').reshape(1, ghosts)  8.59 us
    all_to_all x1, blocking collectives, local(): returned = exchange(coarse_back, 'group').reshape(groups * coarse, latent)  7.91 us
  transfers between devices with their start and end apart: 6, of which 4 were waited for; matrix products, arithmetic and copies ran while one was open for 1% of the time, Pallas kernels for 17%

profile of v1, /device:TPU:1, one launch (start us, length us, event | category | flops | bytes accessed | tf_op | source)
XLA Modules:
  0.0 157.4 jit_solution(6192541142498487213)
XLA Ops:
  0.6 1.4 copy.30
  2.0 8.6 %all-to-all-start = ((s32[32,1,16]{2,1,0:T(1,128)}), s32[32,1,16]{2,1,0:T(1,128)S(1)}, u32[]{:S(2)}, u32[]{:S(2)}) async-start(s32[32,1,16]{2,1,0:T(1,128)} %bitcast), calls=%async_computation | async-start | bytes 32768 | tf_op jit(solution)/shard_map/all_to_all | solution.py:361
  15.1 7.3 %edge_first.1 = (bf16[4096,128]{1,0:T(8,128)(2,1)S(1)}, bf16[4096,128]{1,0:T(8,128)(2,1)S(1)}, f32[4096,128]{1,0:T(8,128)S(1)}) custom-call(s32[1,4096]{1,0:T(1,128)S(1)} %bitcast.18, s32[1,4096]{1,0:T(1,128)S(1)} %bitcast.22, bf16[1024,128]{1,0:T(8,128)(2,1)S(1)} %copy-done.6, bf16[4096,128]{1,0:T(8,128)(2,1)S(1)} %copy-done.4, bf16[384,128]{1,0:T(8,128)(2,1)S(1)} %copy-done.9), custom_call_target="tpu_custom_call" | custom-call | flops 5000000000 | bytes 6000000 | tf_op jit(solution)/shard_map/edge_first/pallas_call | solution.py:325
  22.4 1.3 copy-done.23
  25.4 5.0 %all-to-all-start.2 = ((s32[4,1,512]{2,1,0:T(1,128)}), s32[4,1,512]{2,1,0:T(1,128)S(1)}, u32[]{:S(2)}, u32[]{:S(2)}) async-start(s32[4,1,512]{2,1,0:T(1,128)} %all_to_all.34), calls=%async_computation.2 | async-start | bytes 16384 | tf_op jit(solution)/shard_map/all_to_all | solution.py:362
  31.7 1.3 share.1
  33.0 1.5 all-to-all-done.2
  34.6 8.8 %all-to-all-start.1 = ((bf16[32,16,128]{2,1,0:T(8,128)(2,1)}), bf16[32,16,128]{2,1,0:T(8,128)(2,1)S(1)}, u32[]{:S(2)}, u32[]{:S(2)}) async-start(bf16[32,16,128]{2,1,0:T(8,128)(2,1)} %bitcast.3), calls=%async_computation.1 | async-start | bytes 262144 | tf_op jit(solution)/shard_map/all_to_all | solution.py:368
  43.5 5.7 %route.1 = (bf16[1024,1024]{1,0:T(8,128)(2,1)S(1)}, bf16[1024,1024]{1,0:T(8,128)(2,1)S(1)}, bf16[1024,128]{1,0:T(8,128)(2,1)S(1)}) custom-call(s32[1,4]{1,0:T(1,128)S(1)} %copy-done.20, s32[4,512]{1,0:T(4,128)S(1)} %bitcast.17, s32[1,1024]{1,0:T(1,128)S(1)} %copy-done.18, bf16[1024,128]{1,0:T(8,128)(2,1)S(1)} %copy-done.8), custom_call_target="tpu_custom_call" | custom-call | flops 4000000000 | bytes 4000000 | tf_op jit(solution)/shard_map/route/pallas_call | solution.py:325
  49.2 1.3 copy-done.21
  50.5 1.3 copy-done.24
  52.0 14.2 %edge_second.1 = (f32[4096,128]{1,0:T(8,128)S(1)}, bf16[4096,128]{1,0:T(8,128)(2,1)S(1)}, bf16[1024,128]{1,0:T(8,128)(2,1)S(1)}, bf16[4,512,128]{2,1,0:T(8,128)(2,1)S(1)}) custom-call(s32[1,4096]{1,0:T(1,128)S(1)} %bitcast.19, s32[1,4096]{1,0:T(1,128)S(1)} %bitcast.23, f32[4096,128]{1,0:T(8,128)} %copy-done.23, ...), custom_call_target="tpu_custom_call" | custom-call | flops 5000000000 | bytes 8000000 | tf_op jit(solution)/shard_map/edge_second/pallas_call | solution.py:325
  66.2 1.3 copy-done.22
  67.5 11.8 %all_to_all.50.got_ref = bf16[4,512,128]{2,1,0:T(8,128)(2,1)S(1)} all-to-all(bf16[4,512,128]{2,1,0:T(8,128)(2,1)S(1)} %get-tuple-element.41), channel_id=1, replica_groups=mesh['group'=4,'dom'=32] {'group'}, dimensions={0} | all-to-all | bytes 1048576 | tf_op jit(solution)/shard_map/all_to_all | solution.py:402
  80.6 7.9 %all_to_all.51 = bf16[4,256,128]{2,1,0:T(8,128)(2,1)S(1)} all-to-all(bf16[4,256,128]{2,1,0:T(8,128)(2,1)S(1)} %get-tuple-element.42), channel_id=1, replica_groups=mesh['group'=4,'dom'=32] {'group'}, dimensions={0} | all-to-all | bytes 524288 | tf_op jit(solution)/shard_map/all_to_all | solution.py:410
  88.5 15.3 %edge_back.1 = (bf16[4096,128]{1,0:T(8,128)(2,1)S(1)}, f32[1024,128]{1,0:T(8,128)S(1)}, bf16[2048,128]{1,0:T(8,128)(2,1)}) custom-call(s32[1,4096]{1,0:T(1,128)S(1)} %bitcast.24, f32[4096,128]{1,0:T(8,128)} %copy-done.22, bf16[4096,128]{1,0:T(8,128)(2,1)S(1)} %get-tuple-element.39.src_ref, bf16[4096,128]{1,0:T(8,128)(2,1)S(1)} %copy-done.26, ...), custom_call_target="tpu_custom_call" | custom-call | flops 6000000000 | bytes 10000000 | tf_op jit(solution)/shard_map/edge_back/pallas_call | solution.py:325
  103.8 9.3 %all-to-all-start.6 = ((bf16[128,16,128]{2,1,0:T(8,128)(2,1)}), bf16[128,16,128]{2,1,0:T(8,128)(2,1)S(1)}, u32[]{:S(2)}, u32[]{:S(2)}) async-start(bf16[128,16,128]{2,1,0:T(8,128)(2,1)} %bitcast.8), calls=%async_computation.6 | async-start | bytes 1048576 | tf_op jit(solution)/shard_map/all_to_all | solution.py:431
  113.2 3.4 %ghost_back.1 = bf16[512,128]{1,0:T(8,128)(2,1)} custom-call(s32[1,4096]{1,0:T(1,128)S(1)} %bitcast.20, bf16[4096,128]{1,0:T(8,128)(2,1)S(1)} %get-tuple-element.47.grad_pre_ref, bf16[384,128]{1,0:T(8,128)(2,1)S(1)} %copy-done.10), custom_call_target="tpu_custom_call" | custom-call | flops 1000000000 | bytes 1000000 | tf_op jit(solution)/shard_map/ghost_back/pallas_call | solution.py:325
  116.6 10.1 %all-to-all-done.6.got_ref = bf16[128,16,128]{2,1,0:T(8,128)(2,1)S(1)} async-done(((bf16[128,16,128]{2,1,0:T(8,128)(2,1)}), bf16[128,16,128]{2,1,0:T(8,128)(2,1)S(1)}, u32[]{:S(2)}, u32[]{:S(2)}) %all-to-all-start.6) | async-done | bytes 524320 | tf_op jit(solution)/shard_map/all_to_all | solution.py:431
  126.7 4.6 %all-to-all-start.5 = ((bf16[32,16,128]{2,1,0:T(8,128)(2,1)}), bf16[32,16,128]{2,1,0:T(8,128)(2,1)S(1)}, u32[]{:S(2)}, u32[]{:S(2)}) async-start(bf16[32,16,128]{2,1,0:T(8,128)(2,1)} %bitcast.6), calls=%async_computation.5 | async-start | bytes 262144 | tf_op jit(solution)/shard_map/all_to_all | solution.py:441
  132.2 6.8 %all-to-all-done.5 = bf16[32,16,128]{2,1,0:T(8,128)(2,1)S(1)} async-done(((bf16[32,16,128]{2,1,0:T(8,128)(2,1)}), bf16[32,16,128]{2,1,0:T(8,128)(2,1)S(1)}, u32[]{:S(2)}, u32[]{:S(2)}) %all-to-all-start.5) | async-done | bytes 131104 | tf_op jit(solution)/shard_map/all_to_all | solution.py:441
  139.1 3.8 %all-to-all-start.7 = ((bf16[128,16,128]{2,1,0:T(8,128)(2,1)}), bf16[128,16,128]{2,1,0:T(8,128)(2,1)S(1)}, u32[]{:S(2)}, u32[]{:S(2)}) async-start(bf16[128,16,128]{2,1,0:T(8,128)(2,1)} %add_parts.1), calls=%async_computation.7 | async-start | bytes 1048576 | tf_op jit(solution)/shard_map/all_to_all | solution.py:457
  142.9 7.4 %own_back.1 = (f32[1024,128]{1,0:T(8,128)S(1)}, f32[4096,128]{1,0:T(8,128)}) custom-call(s32[1,4096]{1,0:T(1,128)S(1)} %bitcast.21, s32[1,4096]{1,0:T(1,128)S(1)} %bitcast.25, bf16[4096,128]{1,0:T(8,128)(2,1)S(1)} %get-tuple-element.47.grad_pre_ref, bf16[4096,128]{1,0:T(8,128)(2,1)S(1)} %copy-done.5, f32[1024,128]{1,0:T(8,128)S(1)} %get-tuple-element.48.local_ref, ...), custom_call_target="tpu_custom_call" | custom-call | flops 4000000000 | bytes 5000000 | tf_op jit(solution)/shard_map/own_back/pallas_call | solution.py:325
  151.6 4.9 %all-to-all-done.7 = bf16[128,16,128]{2,1,0:T(8,128)(2,1)S(1)} async-done(((bf16[128,16,128]{2,1,0:T(8,128)(2,1)}), bf16[128,16,128]{2,1,0:T(8,128)(2,1)S(1)}, u32[]{:S(2)}, u32[]{:S(2)}) %all-to-all-start.7) | async-done | bytes 524320 | tf_op jit(solution)/shard_map/all_to_all | solution.py:457
  (63 shorter events, 11.9 us)
Async XLA Ops:
  2.0 23.3 %all-to-all-start = ((s32[32,1,16]{2,1,0:T(1,128)}), s32[32,1,16]{2,1,0:T(1,128)S(1)}, u32[]{:S(2)}, u32[]{:S(2)}) async-start(s32[32,1,16]{2,1,0:T(1,128)} %bitcast), calls=%async_computation | async-start | bytes 32768 | tf_op jit(solution)/shard_map/all_to_all | solution.py:361
  15.1 9.6 %copy-start.27 = (s32[1,4,512]{2,1,0:T(4,128)S(1)}, s32[1,4,512]{2,1,0:T(4,128)}, u32[]{:S(2)}) copy-start(s32[1,4,512]{2,1,0:T(4,128)} %param.34) | copy-start | bytes 24580
  15.1 16.6 %copy-start.7 = (bf16[1024,128]{1,0:T(8,128)(2,1)S(1)}, bf16[1024,128]{1,0:T(8,128)(2,1)}, u32[]{:S(2)}) copy-start(bf16[1024,128]{1,0:T(8,128)(2,1)} %nodes_ref.7) | copy-start | bytes 786436
  15.1 16.6 %copy-start.19 = (s32[1,256]{1,0:T(1,128)S(1)}, s32[1,256]{1,0:T(1,128)}, u32[]{:S(2)}) copy-start(s32[1,256]{1,0:T(1,128)} %boundary_ref.3) | copy-start | bytes 3076
  24.7 18.7 %copy-start.8 = (bf16[1024,128]{1,0:T(8,128)(2,1)S(1)}, bf16[1024,128]{1,0:T(8,128)(2,1)}, u32[]{:S(2)}) copy-start(bf16[1024,128]{1,0:T(8,128)(2,1)} %node_cot_ref.1) | copy-start | bytes 786436
  24.7 18.7 %copy-start.18 = (s32[1,1024]{1,0:T(1,128)S(1)}, s32[1,1024]{1,0:T(1,128)}, u32[]{:S(2)}) copy-start(s32[1,1024]{1,0:T(1,128)} %order_ref.1) | copy-start | bytes 12292
  24.7 18.7 %copy-start.20 = (s32[1,4]{1,0:T(1,128)S(1)}, s32[1,4]{1,0:T(1,128)}, u32[]{:S(2)}) copy-start(s32[1,4]{1,0:T(1,128)} %count_ref.1) | copy-start | bytes 52
  25.4 9.2 %all-to-all-start.2 = ((s32[4,1,512]{2,1,0:T(1,128)}), s32[4,1,512]{2,1,0:T(1,128)S(1)}, u32[]{:S(2)}, u32[]{:S(2)}) async-start(s32[4,1,512]{2,1,0:T(1,128)} %all_to_all.34), calls=%async_computation.2 | async-start | bytes 16384 | tf_op jit(solution)/shard_map/all_to_all | solution.py:362
  34.6 17.3 %all-to-all-start.1 = ((bf16[32,16,128]{2,1,0:T(8,128)(2,1)}), bf16[32,16,128]{2,1,0:T(8,128)(2,1)S(1)}, u32[]{:S(2)}, u32[]{:S(2)}) async-start(bf16[32,16,128]{2,1,0:T(8,128)(2,1)} %bitcast.3), calls=%async_computation.1 | async-start | bytes 262144 | tf_op jit(solution)/shard_map/all_to_all | solution.py:368
  43.4 8.5 %copy-start.10 = (bf16[384,128]{1,0:T(8,128)(2,1)S(1)}, bf16[384,128]{1,0:T(8,128)(2,1)}, u32[]{:S(2)}) copy-start(bf16[384,128]{1,0:T(8,128)(2,1)} %w1_ref.9) | copy-start | bytes 294916
  43.4 8.4 %copy-start.11 = (bf16[256,128]{1,0:T(8,128)(2,1)S(1)}, bf16[256,128]{1,0:T(8,128)(2,1)}, u32[]{:S(2)}) copy-start(bf16[256,128]{1,0:T(8,128)(2,1)} %v1_ref.3) | copy-start | bytes 196612
  43.4 8.4 %copy-start.12 = (bf16[128,128]{1,0:T(8,128)(2,1)S(1)}, bf16[128,128]{1,0:T(8,128)(2,1)}, u32[]{:S(2)}) copy-start(bf16[128,128]{1,0:T(8,128)(2,1)} %w2_ref.5) | copy-start | bytes 98308
  43.5 8.4 %copy-start.13 = (bf16[128,128]{1,0:T(8,128)(2,1)S(1)}, bf16[128,128]{1,0:T(8,128)(2,1)}, u32[]{:S(2)}) copy-start(bf16[128,128]{1,0:T(8,128)(2,1)} %v2_ref.3) | copy-start | bytes 98308
  43.5 8.4 %copy-start.15 = (s32[4096]{0:T(1024)S(1)}, s32[4096]{0:T(1024)}, u32[]{:S(2)}) copy-start(s32[4096]{0:T(1024)} %param.28) | copy-start | bytes 49156
  43.5 8.4 %copy-start.17 = (s32[4096]{0:T(1024)S(1)}, s32[4096]{0:T(1024)}, u32[]{:S(2)}) copy-start(s32[4096]{0:T(1024)} %param.29) | copy-start | bytes 49156
  51.9 27.4 %copy-start = (bf16[256,128]{1,0:T(8,128)(2,1)S(1)}, bf16[256,128]{1,0:T(8,128)(2,1)}, u32[]{:S(2)}) copy-start(bf16[256,128]{1,0:T(8,128)(2,1)} %feat_ref.1) | copy-start | bytes 196612
  51.9 27.4 %copy-start.1 = (bf16[256,128]{1,0:T(8,128)(2,1)S(1)}, bf16[256,128]{1,0:T(8,128)(2,1)}, u32[]{:S(2)}) copy-start(bf16[256,128]{1,0:T(8,128)(2,1)} %cot_ref.5) | copy-start | bytes 196612
  51.9 27.4 %copy-start.2 = (bf16[256,128]{1,0:T(8,128)(2,1)S(1)}, bf16[256,128]{1,0:T(8,128)(2,1)}, u32[]{:S(2)}) copy-start(bf16[256,128]{1,0:T(8,128)(2,1)} %w1_ref.6) | copy-start | bytes 196612
  52.0 27.4 %copy-start.3 = (bf16[128,128]{1,0:T(8,128)(2,1)S(1)}, bf16[128,128]{1,0:T(8,128)(2,1)}, u32[]{:S(2)}) copy-start(bf16[128,128]{1,0:T(8,128)(2,1)} %w2_ref.4) | copy-start | bytes 98308
  67.5 21.0 %copy-start.26 = (bf16[4096,128]{1,0:T(8,128)(2,1)S(1)}, bf16[4096,128]{1,0:T(8,128)(2,1)}, u32[]{:S(2)}) copy-start(bf16[4096,128]{1,0:T(8,128)(2,1)} %copy-done.25) | copy-start | bytes 3145732
  103.8 22.9 %all-to-all-start.6 = ((bf16[128,16,128]{2,1,0:T(8,128)(2,1)}), bf16[128,16,128]{2,1,0:T(8,128)(2,1)S(1)}, u32[]{:S(2)}, u32[]{:S(2)}) async-start(bf16[128,16,128]{2,1,0:T(8,128)(2,1)} %bitcast.8), calls=%async_computation.6 | async-start | bytes 1048576 | tf_op jit(solution)/shard_map/all_to_all | solution.py:431
  116.6 26.4 %copy-start.5 = (bf16[4096,128]{1,0:T(8,128)(2,1)S(1)}, bf16[4096,128]{1,0:T(8,128)(2,1)}, u32[]{:S(2)}) copy-start(bf16[4096,128]{1,0:T(8,128)(2,1)} %cot_ref.7) | copy-start | bytes 3145732
  126.7 12.4 %all-to-all-start.5 = ((bf16[32,16,128]{2,1,0:T(8,128)(2,1)}), bf16[32,16,128]{2,1,0:T(8,128)(2,1)S(1)}, u32[]{:S(2)}, u32[]{:S(2)}) async-start(bf16[32,16,128]{2,1,0:T(8,128)(2,1)} %bitcast.6), calls=%async_computation.5 | async-start | bytes 262144 | tf_op jit(solution)/shard_map/all_to_all | solution.py:441
  139.1 17.5 %all-to-all-start.7 = ((bf16[128,16,128]{2,1,0:T(8,128)(2,1)}), bf16[128,16,128]{2,1,0:T(8,128)(2,1)S(1)}, u32[]{:S(2)}, u32[]{:S(2)}) async-start(bf16[128,16,128]{2,1,0:T(8,128)(2,1)} %add_parts.1), calls=%async_computation.7 | async-start | bytes 1048576 | tf_op jit(solution)/shard_map/all_to_all | solution.py:457
  (10 other events, 10.8 us)

commit v2 on v1

v2 whole, which is shorter than its diff:
```python
import functools

import jax
import jax.numpy as jnp
from jax import lax
from jax.experimental import pallas as pl
from jax.experimental.pallas import tpu as pltpu
from jax.sharding import PartitionSpec as P

NORM_EPSILON = 1e-05
POOL_SHARE = 0.25
BF = jnp.bfloat16
F32 = jnp.float32
I32 = jnp.int32
LANES = 128


def nn(a, b):
    return lax.dot_general(a, b, (((1,), (0,)), ((), ())), preferred_element_type=F32)


def nt(a, b):
    return lax.dot_general(a, b, (((1,), (1,)), ((), ())), preferred_element_type=F32)


def tn(a, b):
    return lax.dot_general(a, b, (((0,), (0,)), ((), ())), preferred_element_type=F32)


def as_hit(mask):
    return jnp.where(mask, 1.0, 0.0).astype(BF)


def hit_rows(index_row, count, base=0):
    width = index_row.shape[1]
    return as_hit(lax.broadcasted_iota(I32, (count, width), 0) == index_row - base)


def spread_column(index_row):
    width = index_row.shape[1]
    return jnp.transpose(jnp.broadcast_to(index_row, (LANES, width)))


def hit_columns(index_column, count, base=0):
    lane = lax.broadcasted_iota(I32, index_column.shape, 1)
    return jnp.concatenate(
        [as_hit(lane == index_column - (base + LANES * j)) for j in range(count // LANES)], axis=1
    )


def halves(table):
    half = table.shape[0] // 2
    return jnp.concatenate([table[:half], table[half:]], axis=1)


def pick_rows(index_column, table_halves):
    half = table_halves.shape[0]
    upper = index_column >= half
    wide = nn(hit_columns(jnp.where(upper, index_column - half, index_column), half), table_halves)
    return jnp.where(upper, wide[:, LANES:], wide[:, :LANES])


def sum_rows(index_row, index_column, values, half):
    upper = index_column >= half
    nothing = jnp.zeros_like(values)
    both = jnp.concatenate(
        [jnp.where(upper, nothing, values), jnp.where(upper, values, nothing)], axis=1
    )
    return nn(hit_rows(jnp.where(index_row >= half, index_row - half, index_row), half), both)


def unfold(sums):
    return jnp.concatenate([sums[:, :LANES], sums[:, LANES:]], axis=0)


def split_wide(values):
    high = values.astype(BF)
    low = (values - high.astype(F32)).astype(BF)
    return jnp.concatenate([high, low], axis=1)


def fold_wide(values):
    return values[:, :LANES] + values[:, LANES:]


def times_transposed(values, weights):
    return nt(split_wide(values), jnp.concatenate([weights, weights], axis=1))


def mean_lanes(values):
    return jnp.mean(values, axis=-1, keepdims=True)


def norm_parts(values):
    centred = values - mean_lanes(values)
    inv_std = lax.rsqrt(mean_lanes(centred * centred) + NORM_EPSILON)
    return centred * inv_std, inv_std


def norm_back(normed, inv_std, grad_in):
    return inv_std * (grad_in - mean_lanes(grad_in) - normed * mean_lanes(grad_in * normed))


def sigmoid(values):
    return 1.0 / (1.0 + jnp.exp(-values))


def slope(values, sig):
    return sig * (1.0 + values * (1.0 - sig))


def spread_kernel(wanted_ref, out_ref):
    domains, slots = wanted_ref.shape
    ghosts = out_ref.shape[0]
    first = lax.broadcasted_iota(I32, (ghosts, domains), 0) // slots
    pick = as_hit(first == lax.broadcasted_iota(I32, (ghosts, domains), 1))
    by_owner = nn(pick, wanted_ref[...].astype(F32).astype(BF))
    slot = lax.broadcasted_iota(I32, (ghosts, slots), 0) % slots
    own = jnp.where(slot == lax.broadcasted_iota(I32, (ghosts, slots), 1), by_owner, 0.0).astype(BF)
    out_ref[...] = nn(own, jnp.ones((slots, LANES), BF)).astype(BF)


def share_kernel(boundary_ref, wanted_ref, nodes_ref, out_ref):
    border = boundary_ref.shape[1]
    shared = pick_rows(spread_column(boundary_ref[...]), halves(nodes_ref[...])).astype(BF)
    wanted = wanted_ref[...].astype(F32).astype(I32)
    out_ref[...] = nn(hit_columns(wanted, border), shared).astype(BF)


def route_kernel(group_ref, count_ref, order_ref, *refs, coarse):
    slot_refs, out_ref = refs[:-1], refs[-1]
    groups = len(slot_refs)
    capacity = slot_refs[0].shape[1]
    rows = order_ref.shape[1]
    here = group_ref[0, 0]
    place = lax.broadcasted_iota(I32, (8, rows), 1)
    owner = jnp.zeros((8, rows), I32)
    goal = jnp.zeros((8, rows), I32)
    for ahead, slot_ref in enumerate(slot_refs):
        k = lax.rem(here + ahead, groups)
        start = 0
        for other in range(groups - 1):
            start = start + jnp.where(other < k, count_ref[0, other], 0)
        line = jnp.concatenate(
            [slot_ref[pl.ds(here, 1), :], jnp.zeros((1, rows - capacity), I32)], axis=1
        )
        line = pltpu.roll(jnp.broadcast_to(line, (8, rows)), start, 1)
        inside = (place >= start) & (place < start + count_ref[0, k])
        owner = jnp.where(inside, ahead, owner)
        goal = jnp.where(inside, line, goal)
    digits = jnp.where(lax.broadcasted_iota(I32, (8, rows), 0) == 0, owner, goal)
    by_row = nt(digits.astype(F32).astype(BF), hit_rows(order_ref[...], rows))
    out_ref[...] = (by_row[0:1, :] * coarse + by_row[1:2, :]).astype(I32)


def edge_first_kernel(source_ref, target_ref, nodes_ref, src_ref, tgt_ref):
    nodes = halves(nodes_ref[...])
    src_ref[...] = pick_rows(spread_column(source_ref[...]), nodes).astype(BF)
    tgt_ref[...] = pick_rows(spread_column(target_ref[...]), nodes).astype(BF)


def edge_second_kernel(
    source_ref, target_ref, src_in_ref, tgt_ref, edges_ref, ghosts_ref, w1_ref, w2_ref,
    nodes_ref, v1_ref, v2_ref, goal_ref, node_cot_ref,
    pre_ref, src_ref, summed_ref, *rest,
):
    send_refs, total = rest[:-1], rest[-1]
    step = pl.program_id(0)
    rows = nodes_ref.shape[0]

    @pl.when(step == 0)
    def _():
        total[...] = jnp.zeros_like(total)

    found = pick_rows(spread_column(source_ref[...]) - rows, halves(ghosts_ref[...])).astype(BF)
    src = src_in_ref[...] + found
    src_ref[...] = src
    pre = nn(jnp.concatenate([src, tgt_ref[...], edges_ref[...]], axis=1), w1_ref[...])
    pre_ref[...] = pre
    hidden = (pre * sigmoid(pre)).astype(BF)
    message, _ = norm_parts(nn(hidden, w2_ref[...]))
    target = target_ref[...]
    total[...] += sum_rows(target, spread_column(target), message.astype(BF), rows // 2)

    @pl.when(step == pl.num_programs(0) - 1)
    def _():
        summed = unfold(total[...]).astype(BF)
        summed_ref[...] = summed
        nodes = nodes_ref[...]
        pre_node = nn(jnp.concatenate([nodes, summed], axis=1), v1_ref[...])
        hidden_node = (pre_node * sigmoid(pre_node)).astype(BF)
        normed, _ = norm_parts(nn(hidden_node, v2_ref[...]))
        updated = (nodes.astype(F32) + normed).astype(BF)
        coarse = send_refs[0].shape[0] // 2
        both = jnp.concatenate([updated, node_cot_ref[...]], axis=1)
        pooled = nn(hit_rows(goal_ref[...], len(send_refs) * coarse), both).astype(BF)
        for k, send_ref in enumerate(send_refs):
            send_ref[:coarse, :] = pooled[k * coarse : (k + 1) * coarse, :LANES]
            send_ref[coarse:, :] = pooled[k * coarse : (k + 1) * coarse, LANES:]


def coarse_kernel(feat_ref, cot_ref, w1_ref, w2_ref, *refs):
    got_refs, (grad_ref, back_ref, g1_ref, g2_ref) = refs[:-4], refs[-4:]
    coarse = feat_ref.shape[0]
    got = got_refs[0][...].astype(F32)
    for got_ref in got_refs[1:]:
        got = got + got_ref[...].astype(F32)
    pooled = (got[:coarse] * POOL_SHARE).astype(BF)
    cot = cot_ref[...].astype(F32)
    grad_out = (cot + got[coarse:]).astype(BF)
    joined = jnp.concatenate([feat_ref[...], pooled], axis=1)
    pre = nn(joined, w1_ref[...])
    sig = sigmoid(pre)
    hidden = (pre * sig).astype(BF)
    g2_ref[...] = tn(hidden, grad_out)
    grad_pre = (nt(grad_out, w2_ref[...]) * slope(pre, sig)).astype(BF)
    g1_ref[...] = tn(joined, grad_pre)
    grad_in = nt(grad_pre, w1_ref[...])
    grad_ref[...] = cot + grad_in[:, :LANES]
    back_ref[...] = (grad_in[:, LANES:] * POOL_SHARE).astype(BF)


def edge_back_kernel(
    target_ref, pre_ref, src_ref, tgt_ref, edges_ref, cot_ref, w1_ref, w2_ref,
    goal_ref, node_cot_ref, nodes_ref, summed_ref, v1_ref, v2_ref, c1_ref, c2_ref, *rest,
):
    gp_refs = rest[:-8]
    grad_pre_ref, local_ref, pack_ref, wide, gw1, gw2, gv1, gv2 = rest[-8:]
    step = pl.program_id(0)

    @pl.when(step == 0)
    def _():
        gw1[...] = jnp.zeros_like(gw1)
        gw2[...] = jnp.zeros_like(gw2)
        table = halves(jnp.concatenate([gp_ref[...] for gp_ref in gp_refs], axis=0))
        from_coarse = pick_rows(spread_column(goal_ref[...]), table)
        updated_grad = node_cot_ref[...].astype(F32) + from_coarse
        joined = jnp.concatenate([nodes_ref[...], summed_ref[...]], axis=1)
        pre = nn(joined, v1_ref[...])
        sig = sigmoid(pre)
        hidden = (pre * sig).astype(BF)
        normed, inv_std = norm_parts(nn(hidden, v2_ref[...]))
        grad_norm = norm_back(normed, inv_std, updated_grad).astype(BF)
        gv2[...] = tn(hidden, grad_norm)
        grad_pre = (nt(grad_norm, v2_ref[...]) * slope(pre, sig)).astype(BF)
        gv1[...] = tn(joined, grad_pre)
        grad_in = nt(grad_pre, v1_ref[...])
        local_ref[...] = updated_grad + grad_in[:, :LANES]
        wide[...] = halves(grad_in[:, LANES:].astype(BF))

    from_node = pick_rows(spread_column(target_ref[...]), wide[...])
    message_grad = cot_ref[...].astype(F32) + from_node
    pre = pre_ref[...]
    sig = sigmoid(pre)
    hidden = (pre * sig).astype(BF)
    normed, inv_std = norm_parts(nn(hidden, w2_ref[...]))
    grad_norm = norm_back(normed, inv_std, message_grad).astype(BF)
    gw2[...] += tn(hidden, grad_norm)
    grad_pre = (nt(grad_norm, w2_ref[...]) * slope(pre, sig)).astype(BF)
    grad_pre_ref[...] = grad_pre
    stacked = jnp.concatenate([src_ref[...], tgt_ref[...], edges_ref[...]], axis=1)
    gw1[...] += tn(stacked, grad_pre)

    @pl.when(step == pl.num_programs(0) - 1)
    def _():
        place = 0
        for part in (gw1, gw2, gv1, gv2, c1_ref, c2_ref):
            size = part.shape[0]
            pack_ref[place : place + size, :] = part[...].astype(BF)
            place += size
        pack_ref[place:, :] = jnp.zeros((pack_ref.shape[0] - place, LANES), BF)


def ghost_back_kernel(source_ref, grad_pre_ref, w1_ref, pack_ref, out_ref, total, *, rows):
    step = pl.program_id(0)

    @pl.when(step == 0)
    def _():
        total[...] = jnp.zeros_like(total)

    source = source_ref[...] - rows
    total[...] += sum_rows(source, spread_column(source), grad_pre_ref[...], total.shape[0])

    @pl.when(step == pl.num_programs(0) - 1)
    def _():
        ghost = times_transposed(unfold(total[...]), w1_ref[:LANES, :]).astype(BF)
        domains, both, _ = out_ref.shape
        share = pack_ref.shape[0] // domains
        out_ref[:, :share, :] = pack_ref[...].reshape(domains, share, LANES)
        out_ref[:, share:, :] = ghost.reshape(domains, both - share, LANES)


def own_back_kernel(
    source_ref, target_ref, grad_pre_ref, cot_ref, local_ref, w1_ref,
    out_ref, edges_ref, by_source, by_target,
):
    step = pl.program_id(0)
    half = by_source.shape[0]

    @pl.when(step == 0)
    def _():
        by_source[...] = jnp.zeros_like(by_source)
        by_target[...] = jnp.zeros_like(by_target)

    grad_pre = grad_pre_ref[...]
    source, target = source_ref[...], target_ref[...]
    by_source[...] += sum_rows(source, spread_column(source), grad_pre, half)
    by_target[...] += sum_rows(target, spread_column(target), grad_pre, half)
    edges_ref[...] = cot_ref[...].astype(F32) + nt(grad_pre, w1_ref[2 * LANES :, :])

    @pl.when(step == pl.num_programs(0) - 1)
    def _():
        out_ref[...] = (
            local_ref[...]
            + times_transposed(unfold(by_source[...]), w1_ref[:LANES, :])
            + times_transposed(unfold(by_target[...]), w1_ref[LANES : 2 * LANES, :])
        )


def add_back_kernel(boundary_ref, wanted_ref, got_ref, local_ref, out_ref):
    rows = local_ref.shape[0]
    border = boundary_ref.shape[1]
    wanted = jnp.transpose(wanted_ref[...].astype(F32))[0:1, :].astype(I32)
    slots = wanted.shape[1] // got_ref.shape[0]
    got = got_ref[:, got_ref.shape[1] - slots :, :].reshape(wanted.shape[1], LANES)
    border_grad = nn(hit_rows(wanted, border), got)
    out_ref[...] = local_ref[...] + fold_wide(
        nn(hit_rows(boundary_ref[...], rows), split_wide(border_grad))
    )


def add_parts_kernel(got_ref, out_ref):
    size = out_ref.shape[0]
    total = got_ref[0, :size, :].astype(F32)
    for k in range(1, got_ref.shape[0]):
        total = total + got_ref[k, :size, :].astype(F32)
    out_ref[...] = total


def add_groups_kernel(*refs):
    part_refs, out_ref = refs[:-1], refs[-1]
    total = part_refs[0][...]
    for part_ref in part_refs[1:]:
        total = total + part_ref[...]
    total = total.astype(BF)
    for k in range(out_ref.shape[0]):
        out_ref[k] = total


def scale_kernel(pack_ref, *out_refs, scales):
    place = 0
    for out_ref, scale in zip(out_refs, scales):
        size = out_ref.shape[0]
        out_ref[...] = pack_ref[place : place + size, :].astype(F32) * scale
        place += size


def whole(shape):
    zeros = (0,) * len(shape)
    return pl.BlockSpec(shape, lambda *_: zeros)


def call(kernel, out_shapes, *args, flops=0, bytes_accessed=0, in_specs=None, out_specs=None,
         grid=None, scratch=(), name=None, vmem=40):
    single = not isinstance(out_shapes, (list, tuple))
    extra = {}
    if grid is not None:
        extra["grid"] = grid
    if in_specs is not None:
        extra["in_specs"] = in_specs
    if out_specs is not None:
        extra["out_specs"] = out_specs
    return pl.pallas_call(
        kernel,
        out_shape=out_shapes if single else list(out_shapes),
        scratch_shapes=list(scratch),
        compiler_params=pltpu.CompilerParams(vmem_limit_bytes=vmem * 2**20),
        cost_estimate=pl.CostEstimate(
            flops=flops, bytes_accessed=bytes_accessed, transcendentals=0
        ),
        name=name,
        **extra,
    )(*args)


def local(
    node_features, edge_features, coarse_features,
    edge_w_one, edge_w_two, node_w_one, node_w_two, coarse_w_one, coarse_w_two,
    edge_source, edge_target, boundary, ghost_pos, restr_order, restr_count, coarse_slot,
    node_cotangent, edge_cotangent, coarse_cotangent,
):
    rows, latent = node_features.shape
    edges = edge_features.shape[0]
    coarse = coarse_features.shape[0]
    groups = lax.axis_size("group")
    domains = lax.axis_size("dom")
    parts = groups * domains
    slots = ghost_pos.shape[2]
    ghosts = domains * slots
    shape = jax.ShapeDtypeStruct
    block = 1024
    grid = (edges // block,)
    index_spec = pl.BlockSpec((1, block), lambda i: (0, i))
    edge_spec = pl.BlockSpec((block, latent), lambda i: (i, 0))
    exchange = functools.partial(lax.all_to_all, split_axis=0, concat_axis=0, tiled=True)

    def turned(step):
        return [(k, (k - step) % groups) for k in range(groups)]

    source = edge_source.reshape(1, edges)
    target = edge_target.reshape(1, edges)
    spread = call(
        spread_kernel, shape((ghosts, latent), BF), ghost_pos.reshape(domains, slots),
        flops=10**6, bytes_accessed=10**5, name="spread", vmem=8,
    )
    asked = exchange(spread.reshape(domains, slots, latent), "dom").reshape(ghosts, latent)
    slot_list = coarse_slot.reshape(groups, -1)
    here = lax.axis_index("group").astype(I32).reshape(1, 1)

    src_own, tgt_rows = call(
        edge_first_kernel,
        [shape((edges, latent), BF), shape((edges, latent), BF)],
        source, target, node_features,
        grid=grid,
        in_specs=[index_spec, index_spec, whole((rows, latent))],
        out_specs=[edge_spec, edge_spec],
        flops=4 * 10**9, bytes_accessed=3 * 10**6, name="edge_first", vmem=61,
    )
    asked, src_own, tgt_rows = lax.optimization_barrier((asked, src_own, tgt_rows))
    share = call(
        share_kernel, shape((ghosts, latent), BF), boundary, asked, node_features,
        flops=10**9, bytes_accessed=10**6, name="share", vmem=16,
    )
    share, slot_list = lax.optimization_barrier((share, slot_list))
    slot_lists = [slot_list] + [
        lax.ppermute(slot_list, "group", turned(ahead)) for ahead in range(1, groups)
    ]
    ghost_rows = exchange(share.reshape(domains, slots, latent), "dom").reshape(ghosts, latent)
    goal = call(
        functools.partial(route_kernel, coarse=coarse), shape((1, rows), I32),
        here, restr_count, restr_order, *slot_lists,
        in_specs=[pl.BlockSpec(memory_space=pltpu.SMEM)] * 2
        + [pl.BlockSpec(memory_space=pltpu.VMEM)] * (1 + groups),
        flops=10**9, bytes_accessed=10**6, name="route", vmem=16,
    )
    pre, src_rows, summed, *send = call(
        edge_second_kernel,
        [shape((edges, latent), F32), shape((edges, latent), BF), shape((rows, latent), BF)]
        + [shape((2 * coarse, latent), BF)] * groups,
        source, target, src_own, tgt_rows, edge_features, ghost_rows, edge_w_one, edge_w_two,
        node_features, node_w_one, node_w_two, goal, node_cotangent,
        grid=grid,
        in_specs=[index_spec, index_spec, edge_spec, edge_spec, edge_spec, whole((ghosts, latent)),
                  whole((3 * latent, latent)), whole((latent, latent)), whole((rows, latent)),
                  whole((2 * latent, latent)), whole((latent, latent)),
                  whole((1, rows)), whole((rows, latent))],
        out_specs=[edge_spec, edge_spec, whole((rows, latent))]
        + [whole((2 * coarse, latent))] * groups,
        scratch=[pltpu.VMEM((rows // 2, 2 * latent), F32)],
        flops=5 * 10**9, bytes_accessed=8 * 10**6, name="edge_second",
    )
    got = [send[0]] + [
        lax.ppermute(send[ahead], "group", turned(-ahead)) for ahead in range(1, groups)
    ]
    grad_coarse, coarse_back, grad_c_one, grad_c_two = call(
        coarse_kernel,
        [shape((coarse, latent), F32), shape((coarse, latent), BF),
         shape((2 * latent, latent), F32), shape((latent, latent), F32)],
        coarse_features, coarse_cotangent, coarse_w_one, coarse_w_two, *got,
        flops=10**8, bytes_accessed=10**6, name="coarse", vmem=16,
    )
    returned = [coarse_back] + [
        lax.ppermute(coarse_back, "group", turned(ahead)) for ahead in range(1, groups)
    ]
    share_rows = 48
    pack_rows = domains * share_rows
    grad_pre, node_local, pack = call(
        edge_back_kernel,
        [shape((edges, latent), BF), shape((rows, latent), F32), shape((pack_rows, latent), BF)],
        target, pre, src_rows, tgt_rows, edge_features, edge_cotangent, edge_w_one, edge_w_two,
        goal, node_cotangent, node_features, summed, node_w_one, node_w_two,
        grad_c_one, grad_c_two, *returned,
        grid=grid,
        in_specs=[index_spec, edge_spec, edge_spec, edge_spec, edge_spec, edge_spec,
                  whole((3 * latent, latent)), whole((latent, latent)),
                  whole((1, rows)),
                  whole((rows, latent)), whole((rows, latent)), whole((rows, latent)),
                  whole((2 * latent, latent)), whole((latent, latent)),
                  whole((2 * latent, latent)), whole((latent, latent))]
        + [whole((coarse, latent))] * groups,
        out_specs=[edge_spec, whole((rows, latent)), whole((pack_rows, latent))],
        scratch=[pltpu.VMEM((rows // 2, 2 * latent), BF), pltpu.VMEM((3 * latent, latent), F32),
                 pltpu.VMEM((latent, latent), F32), pltpu.VMEM((2 * latent, latent), F32),
                 pltpu.VMEM((latent, latent), F32)],
        flops=6 * 10**9, bytes_accessed=10**7, name="edge_back",
    )
    joint_shape = (domains, share_rows + slots, latent)
    joint = call(
        functools.partial(ghost_back_kernel, rows=rows), shape(joint_shape, BF),
        source, grad_pre, edge_w_one, pack,
        grid=grid,
        in_specs=[index_spec, edge_spec, whole((3 * latent, latent)), whole((pack_rows, latent))],
        out_specs=whole(joint_shape),
        scratch=[pltpu.VMEM((ghosts // 2, 2 * latent), F32)],
        flops=10**9, bytes_accessed=10**6, name="ghost_back", vmem=24,
    )
    own_local, grad_edges = call(
        own_back_kernel,
        [shape((rows, latent), F32), shape((edges, latent), F32)],
        source, target, grad_pre, edge_cotangent, node_local, edge_w_one,
        grid=grid,
        in_specs=[index_spec, index_spec, edge_spec, edge_spec, whole((rows, latent)),
                  whole((3 * latent, latent))],
        out_specs=[whole((rows, latent)), edge_spec],
        scratch=[pltpu.VMEM((rows // 2, 2 * latent), F32)] * 2,
        flops=4 * 10**9, bytes_accessed=5 * 10**6, name="own_back",
    )
    joint_got, own_local = lax.optimization_barrier((exchange(joint, "dom"), own_local))
    part_sum = call(
        add_parts_kernel, shape((share_rows, latent), F32), joint_got,
        flops=10**6, bytes_accessed=10**6, name="add_parts", vmem=16,
    )
    part_sums = [part_sum] + [
        lax.ppermute(part_sum, "group", turned(ahead)) for ahead in range(1, groups)
    ]
    pack_sum = call(
        add_groups_kernel, shape((domains, share_rows, latent), BF), *part_sums,
        flops=10**6, bytes_accessed=10**6, name="add_groups", vmem=16,
    )
    pack_all = exchange(pack_sum, "dom").reshape(pack_rows, latent)
    grad_nodes = call(
        add_back_kernel, shape((rows, latent), F32), boundary, asked, joint_got, own_local,
        flops=10**9, bytes_accessed=10**6, name="add_back", vmem=16,
    )
    edge_scale = (edges * parts) ** (-0.5)
    node_scale = (rows * parts) ** (-0.5)
    coarse_scale = (coarse * parts) ** (-0.5)
    weight_grads = call(
        functools.partial(
            scale_kernel,
            scales=(edge_scale, edge_scale, node_scale, node_scale, coarse_scale, coarse_scale),
        ),
        [shape((size * latent, latent), F32) for size in (3, 1, 2, 1, 2, 1)],
        pack_all,
        flops=10**6, bytes_accessed=10**6, name="scale", vmem=16,
    )
    return (grad_nodes, grad_edges, grad_coarse, *weight_grads)


def solution(mesh):
    rows = P(("group", "dom"), None)
    cube = P(("group", "dom"), None, None)
    line = P(("group", "dom"))
    placed = (
        rows, rows, rows, P(), P(), P(), P(), P(), P(), line, line, rows, cube, rows, rows, cube,
        rows, rows, rows,
    )
    return jax.shard_map(
        local,
        mesh=mesh,
        in_specs=placed,
        out_specs=(rows, rows, rows, P(), P(), P(), P(), P(), P()),
        check_vma=False,
    )
```

time: 158 us -> 120 us (0.76)
  Pallas kernels: 59 us -> 37.8 us
  blocking collectives: 19.7 us -> 0 us
  starting transfers between devices: 40.2 us -> 47.5 us
  local copies, waits for them, and re-layouts: 13.5 us -> 9.15 us
    pallas_call x11 -> x13, Pallas kernels: 59 us -> 37.8 us  [call(): pl.pallas_call(kernel, out_shape=out_shapes if single else list(out_shape...]
    all_to_all x2 -> x0, blocking collectives: 19.7 us -> none  [the longest x1 11.8 us: local(): got = exchange(send, 'group')]
    ppermute x0 -> x12, starting transfers between devices: none -> 18.1 us  [the longest x3 5.74 us: local(): lax.ppermute(slot_list, 'group', turned(ahead))]
    ppermute x0 -> x12, waiting for transfers between devices: none -> 10.3 us  [the longest x3 4.18 us: local(): lax.ppermute(send[ahead], 'group', turned(-ahead))]
    all_to_all x5 -> x3, waiting for transfers between devices: 23.4 us -> 14 us  [the longest x1 7.92 us: local(): pack_all = exchange(pack_sum, 'dom').reshape(pack_rows, latent)]
    all_to_all x5 -> x3, starting transfers between devices: 31.4 us -> 24.4 us  [the longest x1 10.4 us: local(): exchange(joint, 'dom')]
    all_to_all x1, starting transfers between devices: 8.81 us -> 4.92 us  [local(): exchange(share.reshape(domains, slots, latent), 'dom')]
    unnamed x58 -> x55, local copies, waits for them, and re-layouts: 12.3 us -> 9.15 us
  transfers between devices with their start and end apart: 6 -> 16, of which waited for: 4 -> 12; matrix products, arithmetic and copies ran while one was open for 1% -> 0% of each run, Pallas kernels for 17% -> 11%
where the time goes in v2:
time: 120 us
  starting transfers between devices  47.5 us (40%)
  Pallas kernels  37.8 us (31%)
  waiting for transfers between devices  24.3 us (20%)
  local copies, waits for them, and re-layouts  9.15 us (8%)
    pallas_call x13, Pallas kernels, call(): pl.pallas_call(kernel, out_shape=out_shapes if single else list(out_shape...  37.8 us
    all_to_all x1, starting transfers between devices, local(): exchange(joint, 'dom')  10.4 us
    unnamed x55, local copies, waits for them, and re-layouts  9.15 us
    all_to_all x1, starting transfers between devices, local(): exchange(spread.reshape(domains, slots, latent), 'dom')  8.59 us
    all_to_all x1, waiting for transfers between devices, local(): pack_all = exchange(pack_sum, 'dom').reshape(pack_rows, latent)  7.92 us
    ppermute x3, starting transfers between devices, local(): lax.ppermute(slot_list, 'group', turned(ahead))  5.74 us
    all_to_all x1, starting transfers between devices, local(): pack_all = exchange(pack_sum, 'dom').reshape(pack_rows, latent)  5.46 us
    all_to_all x1, starting transfers between devices, local(): exchange(share.reshape(domains, slots, latent), 'dom')  4.92 us
  transfers between devices with their start and end apart: 16, of which 12 were waited for; matrix products, arithmetic and copies ran while one was open for 0% of the time, Pallas kernels for 11%

profile of v2, /device:TPU:1, one launch (start us, length us, event | category | flops | bytes accessed | tf_op | source)
XLA Modules:
  0.0 119.7 jit_solution(11342449517417441679)
XLA Ops:
  2.4 8.6 %all-to-all-start = ((bf16[32,16,128]{2,1,0:T(8,128)(2,1)}), bf16[32,16,128]{2,1,0:T(8,128)(2,1)S(1)}, u32[]{:S(2)}, u32[]{:S(2)}) async-start(bf16[32,16,128]{2,1,0:T(8,128)(2,1)} %bitcast.1), calls=%async_computation | async-start | bytes 262144 | tf_op jit(solution)/shard_map/all_to_all | solution.py:416
  11.0 5.0 %edge_first.1 = (bf16[4096,128]{1,0:T(8,128)(2,1)}, bf16[4096,128]{1,0:T(8,128)(2,1)}) custom-call(s32[1,4096]{1,0:T(1,128)} %bitcast.15, s32[1,4096]{1,0:T(1,128)} %bitcast.19, bf16[1024,128]{1,0:T(8,128)(2,1)} %nodes_ref.7), custom_call_target="tpu_custom_call" | custom-call | flops 4000000000 | bytes 3000000 | tf_op jit(solution)/shard_map/edge_first/pallas_call | solution.py:373
  16.1 2.6 %all-to-all-done = bf16[32,16,128]{2,1,0:T(8,128)(2,1)S(1)} async-done(((bf16[32,16,128]{2,1,0:T(8,128)(2,1)}), bf16[32,16,128]{2,1,0:T(8,128)(2,1)S(1)}, u32[]{:S(2)}, u32[]{:S(2)}) %all-to-all-start) | async-done | bytes 131104 | tf_op jit(solution)/shard_map/all_to_all | solution.py:416
  20.0 4.9 %all-to-all-start.1 = ((bf16[32,16,128]{2,1,0:T(8,128)(2,1)}), bf16[32,16,128]{2,1,0:T(8,128)(2,1)S(1)}, u32[]{:S(2)}, u32[]{:S(2)}) async-start(bf16[32,16,128]{2,1,0:T(8,128)(2,1)} %bitcast.6), calls=%async_computation.1 | async-start | bytes 262144 | tf_op jit(solution)/shard_map/all_to_all | solution.py:438
  24.9 1.7 %collective-permute-start.2 = (s32[4,512]{1,0:T(4,128)S(1)}, s32[4,512]{1,0:T(4,128)S(1)}, u32[]{:S(2)}, u32[]{:S(2)}) collective-permute-start(s32[4,512]{1,0:T(4,128)S(1)} %bitcast.23), channel_id=1, source_target_pairs={{0,32},{32,64},{64,96},{96,0},{1,33},{33,65},{65,97},{97,1},{2,34}... | collective-permute-start | bytes 24584 | tf_op jit(solution)/shard_map/ppermute | solution.py:436
  26.6 3.3 %collective-permute-start.1 = (s32[4,512]{1,0:T(4,128)S(1)}, s32[4,512]{1,0:T(4,128)S(1)}, u32[]{:S(2)}, u32[]{:S(2)}) collective-permute-start(s32[4,512]{1,0:T(4,128)S(1)} %bitcast.24), channel_id=1, source_target_pairs={{0,64},{32,96},{64,0},{96,32},{1,65},{33,97},{65,1},{97,33},{2,66}... | collective-permute-start | bytes 24584 | tf_op jit(solution)/shard_map/ppermute | solution.py:436
  31.3 1.3 %collective-permute-done.refs_1_ = s32[4,512]{1,0:T(4,128)S(1)} collective-permute-done((s32[4,512]{1,0:T(4,128)S(1)}, s32[4,512]{1,0:T(4,128)S(1)}, u32[]{:S(2)}, u32[]{:S(2)}) %collective-permute-start) | collective-permute-done | bytes 8224 | tf_op jit(solution)/shard_map/ppermute | solution.py:436
  32.6 1.3 %route.1.goal_ref = s32[1,1024]{1,0:T(1,128)S(1)} custom-call(s32[1,1]{1,0:T(1,128)} %bitcast.8.group_ref, s32[1,4]{1,0:T(1,128)S(1)} %copy-done.17, s32[1,1024]{1,0:T(1,128)S(1)} %copy-done.15, s32[4,512]{1,0:T(4,128)S(1)} %bitcast.26, s32[4,512]{1,0:T(4,128)S(1)} %collective-permute-done.refs_1_, s32[4,512]{1,0:T(4,128)S(1)} %collective-permute-done.1.refs_2_, ...), custom_call_target="tpu_custom_call" | custom-call | flops 1000000000 | bytes 1000000 | tf_op jit(solution)/shard_map/route/pallas_call | solution.py:373
  36.5 8.8 %edge_second.1 = (f32[4096,128]{1,0:T(8,128)S(1)}, bf16[4096,128]{1,0:T(8,128)(2,1)S(1)}, bf16[1024,128]{1,0:T(8,128)(2,1)S(1)}, bf16[512,128]{1,0:T(8,128)(2,1)...) custom-call(s32[1,4096]{1,0:T(1,128)S(1)} %bitcast.16, ...), custom_call_target="tpu_custom_call" | custom-call | flops 5000000000 | bytes 8000000 | tf_op jit(solution)/shard_map/edge_second/pallas_call | solution.py:373
  45.7 3.3 %collective-permute-start.4 = (bf16[512,128]{1,0:T(8,128)(2,1)S(1)}, bf16[512,128]{1,0:T(8,128)(2,1)S(1)}, u32[]{:S(2)}, u32[]{:S(2)}) collective-permute-start(bf16[512,128]{1,0:T(8,128)(2,1)S(1)} %get-tuple-element.52), channel_id=1, source_target_pairs={{0,64},{32,96},{64,0},{96,32},{1,65},{33,97},{65,1},{97,33},{2,66}... | collective-permute-start | bytes 393224 | tf_op jit(solution)/shard_map/ppermute | solution.py:463
  50.4 3.4 %collective-permute-done.4.refs_2_ = bf16[512,128]{1,0:T(8,128)(2,1)S(1)} collective-permute-done((bf16[512,128]{1,0:T(8,128)(2,1)S(1)}, bf16[512,128]{1,0:T(8,128)(2,1)S(1)}, u32[]{:S(2)}, u32[]{:S(2)}) %collective-permute-start.4) | collective-permute-done | bytes 131104 | tf_op jit(solution)/shard_map/ppermute | solution.py:463
  53.9 1.3 %coarse.1 = (f32[256,128]{1,0:T(8,128)}, bf16[256,128]{1,0:T(8,128)(2,1)S(1)}, f32[256,128]{1,0:T(8,128)S(1)}, f32[128,128]{1,0:T(8,128)S(1)}) custom-call(bf16[256,128]{1,0:T(8,128)(2,1)S(1)} %copy-done, bf16[256,128]{1,0:T(8,128)(2,1)S(1)} %copy-done.1, bf16[256,128]{1,0:T(8,128)(2,1)S(1)} %copy-done.2, bf16[128,128]{1,0:T(8,128)(2,1)S(1)} %copy-done.3, ...), custom_call_target="tpu_custom_call" | custom-call | flops 100000000 | bytes 1000000 | tf_op jit(solution)/shard_map/coarse/pallas_call | solution.py:373
  55.2 2.1 %collective-permute-start.8 = (bf16[256,128]{1,0:T(8,128)(2,1)S(1)}, bf16[256,128]{1,0:T(8,128)(2,1)S(1)}, u32[]{:S(2)}, u32[]{:S(2)}) collective-permute-start(bf16[256,128]{1,0:T(8,128)(2,1)S(1)} %get-tuple-element.56.rest_0_), channel_id=1, source_target_pairs={{0,32},{32,64},{64,96},{96,0},{1,33},{33,65},{65,97},{97,1},{2,34}... | collective-permute-start | bytes 196616 | tf_op jit(solution)/shard_map/ppermute | solution.py:473
  57.8 1.9 %collective-permute-start.6 = (bf16[256,128]{1,0:T(8,128)(2,1)S(1)}, bf16[256,128]{1,0:T(8,128)(2,1)S(1)}, u32[]{:S(2)}, u32[]{:S(2)}) collective-permute-start(bf16[256,128]{1,0:T(8,128)(2,1)S(1)} %get-tuple-element.56.rest_0_), channel_id=1, source_target_pairs={{0,96},{32,0},{64,32},{96,64},{1,97},{33,1},{65,33},{97,65},{2,98}... | collective-permute-start | bytes 196616 | tf_op jit(solution)/shard_map/ppermute | solution.py:473
  59.7 2.2 %collective-permute-done.7.rest_2_ = bf16[256,128]{1,0:T(8,128)(2,1)S(1)} collective-permute-done((bf16[256,128]{1,0:T(8,128)(2,1)S(1)}, bf16[256,128]{1,0:T(8,128)(2,1)S(1)}, u32[]{:S(2)}, u32[]{:S(2)}) %collective-permute-start.7) | collective-permute-done | bytes 65568 | tf_op jit(solution)/shard_map/ppermute | solution.py:473
  61.9 8.3 %edge_back.1 = (bf16[4096,128]{1,0:T(8,128)(2,1)S(1)}, f32[1024,128]{1,0:T(8,128)S(1)}, bf16[1536,128]{1,0:T(8,128)(2,1)S(1)}) custom-call(s32[1,4096]{1,0:T(1,128)S(1)} %bitcast.21, f32[4096,128]{1,0:T(8,128)S(1)} %get-tuple-element.47.pre_ref, bf16[4096,128]{1,0:T(8,128)(2,1)S(1)} %get-tuple-element.48.src_ref, bf16[4096,128]{1,0:T(8,128)(2,1)S(1)} %copy-done.23, ...), custom_call_target="tpu_custom_call" | custom-call | flops 6000000000 | bytes 10000000 | tf_op jit(solution)/shard_map/edge_back/pallas_call | solution.py:373
  71.1 2.8 %ghost_back.1 = bf16[32,64,128]{2,1,0:T(8,128)(2,1)} custom-call(s32[1,4096]{1,0:T(1,128)S(1)} %bitcast.17, bf16[4096,128]{1,0:T(8,128)(2,1)S(1)} %get-tuple-element.57.grad_pre_ref, bf16[384,128]{1,0:T(8,128)(2,1)S(1)} %copy-done.8, bf16[1536,128]{1,0:T(8,128)(2,1)S(1)} %get-tuple-element.58.pack_ref), custom_call_target="tpu_custom_call" | custom-call | flops 1000000000 | bytes 1000000 | tf_op jit(solution)/shard_map/ghost_back/pallas_call | solution.py:373
  74.8 10.4 %all-to-all-start.2 = ((bf16[32,64,128]{2,1,0:T(8,128)(2,1)}), bf16[32,64,128]{2,1,0:T(8,128)(2,1)S(1)}, u32[]{:S(2)}, u32[]{:S(2)}) async-start(bf16[32,64,128]{2,1,0:T(8,128)(2,1)} %ghost_back.1), calls=%async_computation.2 | async-start | bytes 1048576 | tf_op jit(solution)/shard_map/all_to_all | solution.py:518
  87.5 5.1 %own_back.1 = (f32[1024,128]{1,0:T(8,128)S(1)}, f32[4096,128]{1,0:T(8,128)}) custom-call(s32[1,4096]{1,0:T(1,128)S(1)} %bitcast.18, s32[1,4096]{1,0:T(1,128)S(1)} %bitcast.22, bf16[4096,128]{1,0:T(8,128)(2,1)S(1)} %copy-done.19, bf16[4096,128]{1,0:T(8,128)(2,1)S(1)} %copy-done.5, f32[1024,128]{1,0:T(8,128)S(1)} %copy-done.26, bf16[384,128]{1,0:T(8,128)(2,1)S(1)} %copy-done.8), custom_call_target="tpu_custom_call" | custom-call | flops 4000000000 | bytes 5000000 | tf_op jit(solution)/shard_map/own_back/pallas_call | solution.py:373
  93.4 3.5 %all-to-all-done.2.got_ref = bf16[32,64,128]{2,1,0:T(8,128)(2,1)S(1)} async-done(((bf16[32,64,128]{2,1,0:T(8,128)(2,1)}), bf16[32,64,128]{2,1,0:T(8,128)(2,1)S(1)}, u32[]{:S(2)}, u32[]{:S(2)}) %all-to-all-start.2) | async-done | bytes 524320 | tf_op jit(solution)/shard_map/all_to_all | solution.py:518
  97.0 2.4 %collective-permute-start.10 = (f32[48,128]{1,0:T(8,128)S(1)}, f32[48,128]{1,0:T(8,128)S(1)}, u32[]{:S(2)}, u32[]{:S(2)}) collective-permute-start(f32[48,128]{1,0:T(8,128)S(1)} %add_parts.1.refs_0_), channel_id=1, source_target_pairs={{0,64},{32,96},{64,0},{96,32},{1,65},{33,97},{65,1},{97,33},{2,66}... | collective-permute-start | bytes 73736 | tf_op jit(solution)/shard_map/ppermute | solution.py:524
  103.0 5.5 %all-to-all-start.3 = ((bf16[32,48,128]{2,1,0:T(8,128)(2,1)}), bf16[32,48,128]{2,1,0:T(8,128)(2,1)S(1)}, u32[]{:S(2)}, u32[]{:S(2)}) async-start(bf16[32,48,128]{2,1,0:T(8,128)(2,1)} %add_groups.1), calls=%async_computation.3 | async-start | bytes 786432 | tf_op jit(solution)/shard_map/all_to_all | solution.py:530
  109.6 1.3 %add_back.1 = f32[1024,128]{1,0:T(8,128)} custom-call(s32[1,256]{1,0:T(1,128)S(1)} %copy-done.16, bf16[512,128]{1,0:T(8,128)(2,1)S(1)} %bitcast.12, bf16[32,64,128]{2,1,0:T(8,128)(2,1)S(1)} %all-to-all-done.2.got_ref, f32[1024,128]{1,0:T(8,128)S(1)} %copy-done.21), custom_call_target="tpu_custom_call" | custom-call | flops 1000000000 | bytes 1000000 | tf_op jit(solution)/shard_map/add_back/pallas_call | solution.py:373
  110.9 7.9 %all-to-all-done.3 = bf16[32,48,128]{2,1,0:T(8,128)(2,1)S(1)} async-done(((bf16[32,48,128]{2,1,0:T(8,128)(2,1)}), bf16[32,48,128]{2,1,0:T(8,128)(2,1)S(1)}, u32[]{:S(2)}, u32[]{:S(2)}) %all-to-all-start.3) | async-done | bytes 393248 | tf_op jit(solution)/shard_map/all_to_all | solution.py:530
  (76 shorter events, 19.9 us)
Async XLA Ops:
  2.4 16.3 %all-to-all-start = ((bf16[32,16,128]{2,1,0:T(8,128)(2,1)}), bf16[32,16,128]{2,1,0:T(8,128)(2,1)S(1)}, u32[]{:S(2)}, u32[]{:S(2)}) async-start(bf16[32,16,128]{2,1,0:T(8,128)(2,1)} %bitcast.1), calls=%async_computation | async-start | bytes 262144 | tf_op jit(solution)/shard_map/all_to_all | solution.py:416
  16.0 16.6 %copy-start.15 = (s32[1,1024]{1,0:T(1,128)S(1)}, s32[1,1024]{1,0:T(1,128)}, u32[]{:S(2)}) copy-start(s32[1,1024]{1,0:T(1,128)} %order_ref.1) | copy-start | bytes 12292
  16.0 16.6 %copy-start.17 = (s32[1,4]{1,0:T(1,128)S(1)}, s32[1,4]{1,0:T(1,128)}, u32[]{:S(2)}) copy-start(s32[1,4]{1,0:T(1,128)} %count_ref.1) | copy-start | bytes 52
  20.0 13.9 %all-to-all-start.1 = ((bf16[32,16,128]{2,1,0:T(8,128)(2,1)}), bf16[32,16,128]{2,1,0:T(8,128)(2,1)S(1)}, u32[]{:S(2)}, u32[]{:S(2)}) async-start(bf16[32,16,128]{2,1,0:T(8,128)(2,1)} %bitcast.6), calls=%async_computation.1 | async-start | bytes 262144 | tf_op jit(solution)/shard_map/all_to_all | solution.py:438
  24.9 5.7 %collective-permute-start.2 = (s32[4,512]{1,0:T(4,128)S(1)}, s32[4,512]{1,0:T(4,128)S(1)}, u32[]{:S(2)}, u32[]{:S(2)}) collective-permute-start(s32[4,512]{1,0:T(4,128)S(1)} %bitcast.23), channel_id=1, source_target_pairs={{0,32},{32,64},{64,96},{96,0},{1,33},{33,65},{65,97},{97,1},{2,34}... | collective-permute-start | bytes 24584 | tf_op jit(solution)/shard_map/ppermute | solution.py:436
  26.6 4.7 %collective-permute-start.1 = (s32[4,512]{1,0:T(4,128)S(1)}, s32[4,512]{1,0:T(4,128)S(1)}, u32[]{:S(2)}, u32[]{:S(2)}) collective-permute-start(s32[4,512]{1,0:T(4,128)S(1)} %bitcast.24), channel_id=1, source_target_pairs={{0,64},{32,96},{64,0},{96,32},{1,65},{33,97},{65,1},{97,33},{2,66}... | collective-permute-start | bytes 24584 | tf_op jit(solution)/shard_map/ppermute | solution.py:436
  29.9 2.7 %collective-permute-start = (s32[4,512]{1,0:T(4,128)S(1)}, s32[4,512]{1,0:T(4,128)S(1)}, u32[]{:S(2)}, u32[]{:S(2)}) collective-permute-start(s32[4,512]{1,0:T(4,128)S(1)} %bitcast.25), channel_id=1, source_target_pairs={{0,96},{32,0},{64,32},{96,64},{1,97},{33,1},{65,33},{97,65},{2,98}... | collective-permute-start | bytes 24584 | tf_op jit(solution)/shard_map/ppermute | solution.py:436
  36.4 17.5 %copy-start = (bf16[256,128]{1,0:T(8,128)(2,1)S(1)}, bf16[256,128]{1,0:T(8,128)(2,1)}, u32[]{:S(2)}) copy-start(bf16[256,128]{1,0:T(8,128)(2,1)} %feat_ref.1) | copy-start | bytes 196612
  36.4 17.5 %copy-start.1 = (bf16[256,128]{1,0:T(8,128)(2,1)S(1)}, bf16[256,128]{1,0:T(8,128)(2,1)}, u32[]{:S(2)}) copy-start(bf16[256,128]{1,0:T(8,128)(2,1)} %cot_ref.3) | copy-start | bytes 196612
  36.4 17.5 %copy-start.2 = (bf16[256,128]{1,0:T(8,128)(2,1)S(1)}, bf16[256,128]{1,0:T(8,128)(2,1)}, u32[]{:S(2)}) copy-start(bf16[256,128]{1,0:T(8,128)(2,1)} %w1_ref.6) | copy-start | bytes 196612
  36.4 17.5 %copy-start.3 = (bf16[128,128]{1,0:T(8,128)(2,1)S(1)}, bf16[128,128]{1,0:T(8,128)(2,1)}, u32[]{:S(2)}) copy-start(bf16[128,128]{1,0:T(8,128)(2,1)} %w2_ref.4) | copy-start | bytes 98308
  36.4 25.5 %copy-start.5 = (bf16[4096,128]{1,0:T(8,128)(2,1)S(1)}, bf16[4096,128]{1,0:T(8,128)(2,1)}, u32[]{:S(2)}) copy-start(bf16[4096,128]{1,0:T(8,128)(2,1)} %cot_ref.5) | copy-start | bytes 3145732
  36.5 25.5 %copy-start.23 = (bf16[4096,128]{1,0:T(8,128)(2,1)S(1)}, bf16[4096,128]{1,0:T(8,128)(2,1)}, u32[]{:S(2)}) copy-start(bf16[4096,128]{1,0:T(8,128)(2,1)} %get-tuple-element.44.tgt_ref) | copy-start | bytes 3145732
  45.3 5.1 %collective-permute-start.3 = (bf16[512,128]{1,0:T(8,128)(2,1)S(1)}, bf16[512,128]{1,0:T(8,128)(2,1)S(1)}, u32[]{:S(2)}, u32[]{:S(2)}) collective-permute-start(bf16[512,128]{1,0:T(8,128)(2,1)S(1)} %get-tuple-element.51), channel_id=1, source_target_pairs={{0,32},{32,64},{64,96},{96,0},{1,33},{33,65},{65,97},{97,1},{2,34}... | collective-permute-start | bytes 393224 | tf_op jit(solution)/shard_map/ppermute | solution.py:463
  45.7 8.1 %collective-permute-start.4 = (bf16[512,128]{1,0:T(8,128)(2,1)S(1)}, bf16[512,128]{1,0:T(8,128)(2,1)S(1)}, u32[]{:S(2)}, u32[]{:S(2)}) collective-permute-start(bf16[512,128]{1,0:T(8,128)(2,1)S(1)} %get-tuple-element.52), channel_id=1, source_target_pairs={{0,64},{32,96},{64,0},{96,32},{1,65},{33,97},{65,1},{97,33},{2,66}... | collective-permute-start | bytes 393224 | tf_op jit(solution)/shard_map/ppermute | solution.py:463
  49.0 4.9 %collective-permute-start.5 = (bf16[512,128]{1,0:T(8,128)(2,1)S(1)}, bf16[512,128]{1,0:T(8,128)(2,1)S(1)}, u32[]{:S(2)}, u32[]{:S(2)}) collective-permute-start(bf16[512,128]{1,0:T(8,128)(2,1)S(1)} %get-tuple-element.53), channel_id=1, source_target_pairs={{0,96},{32,0},{64,32},{96,64},{1,97},{33,1},{65,33},{97,65},{2,98}... | collective-permute-start | bytes 393224 | tf_op jit(solution)/shard_map/ppermute | solution.py:463
  55.2 4.5 %collective-permute-start.8 = (bf16[256,128]{1,0:T(8,128)(2,1)S(1)}, bf16[256,128]{1,0:T(8,128)(2,1)S(1)}, u32[]{:S(2)}, u32[]{:S(2)}) collective-permute-start(bf16[256,128]{1,0:T(8,128)(2,1)S(1)} %get-tuple-element.56.rest_0_), channel_id=1, source_target_pairs={{0,32},{32,64},{64,96},{96,0},{1,33},{33,65},{65,97},{97,1},{2,34}... | collective-permute-start | bytes 196616 | tf_op jit(solution)/shard_map/ppermute | solution.py:473
  57.3 4.6 %collective-permute-start.7 = (bf16[256,128]{1,0:T(8,128)(2,1)S(1)}, bf16[256,128]{1,0:T(8,128)(2,1)S(1)}, u32[]{:S(2)}, u32[]{:S(2)}) collective-permute-start(bf16[256,128]{1,0:T(8,128)(2,1)S(1)} %get-tuple-element.56.rest_0_), channel_id=1, source_target_pairs={{0,64},{32,96},{64,0},{96,32},{1,65},{33,97},{65,1},{97,33},{2,66}... | collective-permute-start | bytes 196616 | tf_op jit(solution)/shard_map/ppermute | solution.py:473
  57.8 4.1 %collective-permute-start.6 = (bf16[256,128]{1,0:T(8,128)(2,1)S(1)}, bf16[256,128]{1,0:T(8,128)(2,1)S(1)}, u32[]{:S(2)}, u32[]{:S(2)}) collective-permute-start(bf16[256,128]{1,0:T(8,128)(2,1)S(1)} %get-tuple-element.56.rest_0_), channel_id=1, source_target_pairs={{0,96},{32,0},{64,32},{96,64},{1,97},{33,1},{65,33},{97,65},{2,98}... | collective-permute-start | bytes 196616 | tf_op jit(solution)/shard_map/ppermute | solution.py:473
  74.8 22.0 %all-to-all-start.2 = ((bf16[32,64,128]{2,1,0:T(8,128)(2,1)}), bf16[32,64,128]{2,1,0:T(8,128)(2,1)S(1)}, u32[]{:S(2)}, u32[]{:S(2)}) async-start(bf16[32,64,128]{2,1,0:T(8,128)(2,1)} %ghost_back.1), calls=%async_computation.2 | async-start | bytes 1048576 | tf_op jit(solution)/shard_map/all_to_all | solution.py:518
  96.9 4.0 %collective-permute-start.11 = (f32[48,128]{1,0:T(8,128)S(1)}, f32[48,128]{1,0:T(8,128)S(1)}, u32[]{:S(2)}, u32[]{:S(2)}) collective-permute-start(f32[48,128]{1,0:T(8,128)S(1)} %add_parts.1.refs_0_), channel_id=1, source_target_pairs={{0,32},{32,64},{64,96},{96,0},{1,33},{33,65},{65,97},{97,1},{2,34}... | collective-permute-start | bytes 73736 | tf_op jit(solution)/shard_map/ppermute | solution.py:524
  97.0 4.4 %collective-permute-start.10 = (f32[48,128]{1,0:T(8,128)S(1)}, f32[48,128]{1,0:T(8,128)S(1)}, u32[]{:S(2)}, u32[]{:S(2)}) collective-permute-start(f32[48,128]{1,0:T(8,128)S(1)} %add_parts.1.refs_0_), channel_id=1, source_target_pairs={{0,64},{32,96},{64,0},{96,32},{1,65},{33,97},{65,1},{97,33},{2,66}... | collective-permute-start | bytes 73736 | tf_op jit(solution)/shard_map/ppermute | solution.py:524
  99.4 2.8 %collective-permute-start.9 = (f32[48,128]{1,0:T(8,128)S(1)}, f32[48,128]{1,0:T(8,128)S(1)}, u32[]{:S(2)}, u32[]{:S(2)}) collective-permute-start(f32[48,128]{1,0:T(8,128)S(1)} %add_parts.1.refs_0_), channel_id=1, source_target_pairs={{0,96},{32,0},{64,32},{96,64},{1,97},{33,1},{65,33},{97,65},{2,98}... | collective-permute-start | bytes 73736 | tf_op jit(solution)/shard_map/ppermute | solution.py:524
  103.0 15.8 %all-to-all-start.3 = ((bf16[32,48,128]{2,1,0:T(8,128)(2,1)}), bf16[32,48,128]{2,1,0:T(8,128)(2,1)S(1)}, u32[]{:S(2)}, u32[]{:S(2)}) async-start(bf16[32,48,128]{2,1,0:T(8,128)(2,1)} %add_groups.1), calls=%async_computation.3 | async-start | bytes 786432 | tf_op jit(solution)/shard_map/all_to_all | solution.py:530
  (19 other events, 144.5 us)

commit v3 on v2

--- a/solution.py
+++ b/solution.py
@@ -13,6 +13,8 @@
 F32 = jnp.float32
 I32 = jnp.int32
 LANES = 128
+SECOND_SUB = 512
+BACK_SUB = 2048
 
 
 def nn(a, b):
@@ -172,15 +174,22 @@
     def _():
         total[...] = jnp.zeros_like(total)
 
-    found = pick_rows(spread_column(source_ref[...]) - rows, halves(ghosts_ref[...])).astype(BF)
-    src = src_in_ref[...] + found
-    src_ref[...] = src
-    pre = nn(jnp.concatenate([src, tgt_ref[...], edges_ref[...]], axis=1), w1_ref[...])
-    pre_ref[...] = pre
-    hidden = (pre * sigmoid(pre)).astype(BF)
-    message, _ = norm_parts(nn(hidden, w2_ref[...]))
+    ghosts = halves(ghosts_ref[...])
+    from_ghost = spread_column(source_ref[...]) - rows
     target = target_ref[...]
-    total[...] += sum_rows(target, spread_column(target), message.astype(BF), rows // 2)
+    messages = []
+    for part in range(0, target.shape[1], SECOND_SUB):
+        here = slice(part, part + SECOND_SUB)
+        src = src_in_ref[here, :] + pick_rows(from_ghost[here], ghosts).astype(BF)
+        src_ref[here, :] = src
+        pre = nn(jnp.concatenate([src, tgt_ref[here, :], edges_ref[here, :]], axis=1), w1_ref[...])
+        pre_ref[here, :] = pre
+        hidden = (pre * sigmoid(pre)).astype(BF)
+        message, _ = norm_parts(nn(hidden, w2_ref[...]))
+        messages.append(message.astype(BF))
+    total[...] += sum_rows(
+        target, spread_column(target), jnp.concatenate(messages, axis=0), rows // 2
+    )
 
     @pl.when(step == pl.num_programs(0) - 1)
     def _():
@@ -221,15 +230,17 @@
 
 
 def edge_back_kernel(
-    target_ref, pre_ref, src_ref, tgt_ref, edges_ref, cot_ref, w1_ref, w2_ref,
+    source_ref, target_ref, pre_ref, src_ref, tgt_ref, edges_ref, cot_ref, w1_ref, w2_ref,
     goal_ref, node_cot_ref, nodes_ref, summed_ref, v1_ref, v2_ref, c1_ref, c2_ref, *rest,
 ):
-    gp_refs = rest[:-8]
-    grad_pre_ref, local_ref, pack_ref, wide, gw1, gw2, gv1, gv2 = rest[-8:]
+    gp_refs = rest[:-10]
+    grad_pre_ref, local_ref, joint_ref, wide, gw1, gw2, gv1, gv2, by_ghost, pack_ref = rest[-10:]
     step = pl.program_id(0)
+    rows = nodes_ref.shape[0]
 
     @pl.when(step == 0)
     def _():
+        by_ghost[...] = jnp.zeros_like(by_ghost)
         gw1[...] = jnp.zeros_like(gw1)
         gw2[...] = jnp.zeros_like(gw2)
         table = halves(jnp.concatenate([gp_ref[...] for gp_ref in gp_refs], axis=0))
@@ -248,18 +259,27 @@
         local_ref[...] = updated_grad + grad_in[:, :LANES]
         wide[...] = halves(grad_in[:, LANES:].astype(BF))
 
-    from_node = pick_rows(spread_column(target_ref[...]), wide[...])
-    message_grad = cot_ref[...].astype(F32) + from_node
-    pre = pre_ref[...]
-    sig = sigmoid(pre)
-    hidden = (pre * sig).astype(BF)
-    normed, inv_std = norm_parts(nn(hidden, w2_ref[...]))
-    grad_norm = norm_back(normed, inv_std, message_grad).astype(BF)
-    gw2[...] += tn(hidden, grad_norm)
-    grad_pre = (nt(grad_norm, w2_ref[...]) * slope(pre, sig)).astype(BF)
+    target = spread_column(target_ref[...])
+    hiddens, grad_norms, grad_pres = [], [], []
+    for part in range(0, target.shape[0], BACK_SUB):
+        here = slice(part, part + BACK_SUB)
+        message_grad = cot_ref[here, :].astype(F32) + pick_rows(target[here], wide[...])
+        pre = pre_ref[here, :]
+        sig = sigmoid(pre)
+        hidden = (pre * sig).astype(BF)
+        normed, inv_std = norm_parts(nn(hidden, w2_ref[...]))
+        grad_norm = norm_back(normed, inv_std, message_grad).astype(BF)
+        grad_pre = (nt(grad_norm, w2_ref[...]) * slope(pre, sig)).astype(BF)
+        hiddens.append(hidden)
+        grad_norms.append(grad_norm)
+        grad_pres.append(grad_pre)
+    grad_pre = jnp.concatenate(grad_pres, axis=0)
     grad_pre_ref[...] = grad_pre
+    gw2[...] += tn(jnp.concatenate(hiddens, axis=0), jnp.concatenate(grad_norms, axis=0))
     stacked = jnp.concatenate([src_ref[...], tgt_ref[...], edges_ref[...]], axis=1)
     gw1[...] += tn(stacked, grad_pre)
+    source = source_ref[...] - rows
+    by_ghost[...] += sum_rows(source, spread_column(source), grad_pre, by_ghost.shape[0])
 
     @pl.when(step == pl.num_programs(0) - 1)
     def _():
@@ -269,25 +289,11 @@
             pack_ref[place : place + size, :] = part[...].astype(BF)
             place += size
         pack_ref[place:, :] = jnp.zeros((pack_ref.shape[0] - place, LANES), BF)
-
-
-def ghost_back_kernel(source_ref, grad_pre_ref, w1_ref, pack_ref, out_ref, total, *, rows):
-    step = pl.program_id(0)
-
-    @pl.when(step == 0)
-    def _():
-        total[...] = jnp.zeros_like(total)
-
-    source = source_ref[...] - rows
-    total[...] += sum_rows(source, spread_column(source), grad_pre_ref[...], total.shape[0])
-
-    @pl.when(step == pl.num_programs(0) - 1)
-    def _():
-        ghost = times_transposed(unfold(total[...]), w1_ref[:LANES, :]).astype(BF)
-        domains, both, _ = out_ref.shape
+        ghost = times_transposed(unfold(by_ghost[...]), w1_ref[:LANES, :]).astype(BF)
+        domains, both, _ = joint_ref.shape
         share = pack_ref.shape[0] // domains
-        out_ref[:, :share, :] = pack_ref[...].reshape(domains, share, LANES)
-        out_ref[:, share:, :] = ghost.reshape(domains, both - share, LANES)
+        joint_ref[:, :share, :] = pack_ref[...].reshape(domains, share, LANES)
+        joint_ref[:, share:, :] = ghost.reshape(domains, both - share, LANES)
 
 
 def own_back_kernel(
@@ -398,10 +404,14 @@
     slots = ghost_pos.shape[2]
     ghosts = domains * slots
     shape = jax.ShapeDtypeStruct
-    block = 1024
-    grid = (edges // block,)
-    index_spec = pl.BlockSpec((1, block), lambda i: (0, i))
-    edge_spec = pl.BlockSpec((block, latent), lambda i: (i, 0))
+
+    def edge_blocks(block):
+        return (
+            (edges // block,),
+            pl.BlockSpec((1, block), lambda i: (0, i)),
+            pl.BlockSpec((block, latent), lambda i: (i, 0)),
+        )
+
     exchange = functools.partial(lax.all_to_all, split_axis=0, concat_axis=0, tiled=True)
 
     def turned(step):
@@ -417,6 +427,7 @@
     slot_list = coarse_slot.reshape(groups, -1)
     here = lax.axis_index("group").astype(I32).reshape(1, 1)
 
+    grid, index_spec, edge_spec = edge_blocks(2048)
     src_own, tgt_rows = call(
         edge_first_kernel,
         [shape((edges, latent), BF), shape((edges, latent), BF)],
@@ -443,6 +454,7 @@
         + [pl.BlockSpec(memory_space=pltpu.VMEM)] * (1 + groups),
         flops=10**9, bytes_accessed=10**6, name="route", vmem=16,
     )
+    grid, index_spec, edge_spec = edge_blocks(4096)
     pre, src_rows, summed, *send = call(
         edge_second_kernel,
         [shape((edges, latent), F32), shape((edges, latent), BF), shape((rows, latent), BF)]
@@ -474,36 +486,30 @@
     ]
     share_rows = 48
     pack_rows = domains * share_rows
-    grad_pre, node_local, pack = call(
+    grid, index_spec, edge_spec = edge_blocks(4096)
+    joint_shape = (domains, share_rows + slots, latent)
+    grad_pre, node_local, joint = call(
         edge_back_kernel,
-        [shape((edges, latent), BF), shape((rows, latent), F32), shape((pack_rows, latent), BF)],
-        target, pre, src_rows, tgt_rows, edge_features, edge_cotangent, edge_w_one, edge_w_two,
+        [shape((edges, latent), BF), shape((rows, latent), F32), shape(joint_shape, BF)],
+        source, target, pre, src_rows, tgt_rows, edge_features, edge_cotangent, edge_w_one, edge_w_two,
         goal, node_cotangent, node_features, summed, node_w_one, node_w_two,
         grad_c_one, grad_c_two, *returned,
         grid=grid,
-        in_specs=[index_spec, edge_spec, edge_spec, edge_spec, edge_spec, edge_spec,
+        in_specs=[index_spec, index_spec, edge_spec, edge_spec, edge_spec, edge_spec, edge_spec,
                   whole((3 * latent, latent)), whole((latent, latent)),
                   whole((1, rows)),
                   whole((rows, latent)), whole((rows, latent)), whole((rows, latent)),
                   whole((2 * latent, latent)), whole((latent, latent)),
                   whole((2 * latent, latent)), whole((latent, latent))]
         + [whole((coarse, latent))] * groups,
-        out_specs=[edge_spec, whole((rows, latent)), whole((pack_rows, latent))],
+        out_specs=[edge_spec, whole((rows, latent)), whole(joint_shape)],
         scratch=[pltpu.VMEM((rows // 2, 2 * latent), BF), pltpu.VMEM((3 * latent, latent), F32),
                  pltpu.VMEM((latent, latent), F32), pltpu.VMEM((2 * latent, latent), F32),
-                 pltpu.VMEM((latent, latent), F32)],
+                 pltpu.VMEM((latent, latent), F32), pltpu.VMEM((ghosts // 2, 2 * latent), F32),
+                 pltpu.VMEM((pack_rows, latent), BF)],
         flops=6 * 10**9, bytes_accessed=10**7, name="edge_back",
     )
-    joint_shape = (domains, share_rows + slots, latent)
-    joint = call(
-        functools.partial(ghost_back_kernel, rows=rows), shape(joint_shape, BF),
-        source, grad_pre, edge_w_one, pack,
-        grid=grid,
-        in_specs=[index_spec, edge_spec, whole((3 * latent, latent)), whole((pack_rows, latent))],
-        out_specs=whole(joint_shape),
-        scratch=[pltpu.VMEM((ghosts // 2, 2 * latent), F32)],
-        flops=10**9, bytes_accessed=10**6, name="ghost_back", vmem=24,
-    )
+    grid, index_spec, edge_spec = edge_blocks(4096)
     own_local, grad_edges = call(
         own_back_kernel,
         [shape((rows, latent), F32), shape((edges, latent), F32)],

time: 120 us -> 114 us (0.950)
  Pallas kernels: 37.8 us -> 31.3 us
  waiting for transfers between devices: 24.3 us -> 26.7 us
  local copies, waits for them, and re-layouts: 9.15 us -> 7.34 us
    pallas_call x13 -> x12, Pallas kernels: 37.8 us -> 31.3 us  [call(): pl.pallas_call(kernel, out_shape=out_shapes if single else list(out_shape...]
    unnamed x55 -> x51, local copies, waits for them, and re-layouts: 9.15 us -> 7.34 us
where the time goes in v3:
time: 114 us; the launch traced here: 113 us
  starting transfers between devices  47 us (41%)
  Pallas kernels  31.3 us (27%)
  waiting for transfers between devices  26.7 us (23%)
  local copies, waits for them, and re-layouts  7.34 us (6%)
    pallas_call x12, Pallas kernels, call(): pl.pallas_call(kernel, out_shape=out_shapes if single else list(out_shape...  31.3 us
    all_to_all x1, starting transfers between devices, local(): exchange(joint, 'dom')  10.4 us
    all_to_all x1, waiting for transfers between devices, local(): pack_all = exchange(pack_sum, 'dom').reshape(pack_rows, latent)  8.96 us
    all_to_all x1, starting transfers between devices, local(): exchange(spread.reshape(domains, slots, latent), 'dom')  8.59 us
    unnamed x51, local copies, waits for them, and re-layouts  7.34 us
    ppermute x3, starting transfers between devices, local(): lax.ppermute(slot_list, 'group', turned(ahead))  5.74 us
    all_to_all x1, starting transfers between devices, local(): pack_all = exchange(pack_sum, 'dom').reshape(pack_rows, latent)  5.16 us
    all_to_all x1, starting transfers between devices, local(): exchange(share.reshape(domains, slots, latent), 'dom')  4.76 us
  transfers between devices with their start and end apart: 16, of which 12 were waited for; matrix products, arithmetic and copies ran while one was open for 0% of the time, Pallas kernels for 11%

profile of v3, /device:TPU:1, one launch (start us, length us, event | category | flops | bytes accessed | tf_op | source)
XLA Modules:
  0.0 113.3 jit_solution(8997363817424243872)
XLA Ops:
  2.4 8.6 %all-to-all-start = ((bf16[32,16,128]{2,1,0:T(8,128)(2,1)}), bf16[32,16,128]{2,1,0:T(8,128)(2,1)S(1)}, u32[]{:S(2)}, u32[]{:S(2)}) async-start(bf16[32,16,128]{2,1,0:T(8,128)(2,1)} %bitcast.1), calls=%async_computation | async-start | bytes 262144 | tf_op jit(solution)/shard_map/all_to_all | solution.py:426
  11.0 4.9 %edge_first.1 = (bf16[4096,128]{1,0:T(8,128)(2,1)}, bf16[4096,128]{1,0:T(8,128)(2,1)}) custom-call(s32[1,4096]{1,0:T(1,128)} %bitcast.15, s32[1,4096]{1,0:T(1,128)} %bitcast.19, bf16[1024,128]{1,0:T(8,128)(2,1)} %nodes_ref.7), custom_call_target="tpu_custom_call" | custom-call | flops 4000000000 | bytes 3000000 | tf_op jit(solution)/shard_map/edge_first/pallas_call | solution.py:379
  15.9 2.8 %all-to-all-done = bf16[32,16,128]{2,1,0:T(8,128)(2,1)S(1)} async-done(((bf16[32,16,128]{2,1,0:T(8,128)(2,1)}), bf16[32,16,128]{2,1,0:T(8,128)(2,1)S(1)}, u32[]{:S(2)}, u32[]{:S(2)}) %all-to-all-start) | async-done | bytes 131104 | tf_op jit(solution)/shard_map/all_to_all | solution.py:426
  18.7 1.2 %share.1 = bf16[512,128]{1,0:T(8,128)(2,1)} custom-call(s32[1,256]{1,0:T(1,128)S(1)} %copy-done.16, bf16[512,128]{1,0:T(8,128)(2,1)S(1)} %bitcast.11, bf16[1024,128]{1,0:T(8,128)(2,1)S(1)} %copy-done.6), custom_call_target="tpu_custom_call" | custom-call | flops 1000000000 | bytes 1000000 | tf_op jit(solution)/shard_map/share/pallas_call | solution.py:379
  20.0 4.8 %all-to-all-start.1 = ((bf16[32,16,128]{2,1,0:T(8,128)(2,1)}), bf16[32,16,128]{2,1,0:T(8,128)(2,1)S(1)}, u32[]{:S(2)}, u32[]{:S(2)}) async-start(bf16[32,16,128]{2,1,0:T(8,128)(2,1)} %bitcast.6), calls=%async_computation.1 | async-start | bytes 262144 | tf_op jit(solution)/shard_map/all_to_all | solution.py:449
  24.8 1.7 %collective-permute-start.2 = (s32[4,512]{1,0:T(4,128)S(1)}, s32[4,512]{1,0:T(4,128)S(1)}, u32[]{:S(2)}, u32[]{:S(2)}) collective-permute-start(s32[4,512]{1,0:T(4,128)S(1)} %bitcast.23), channel_id=1, source_target_pairs={{0,32},{32,64},{64,96},{96,0},{1,33},{33,65},{65,97},{97,1},{2,34}... | collective-permute-start | bytes 24584 | tf_op jit(solution)/shard_map/ppermute | solution.py:447
  26.5 3.3 %collective-permute-start.1 = (s32[4,512]{1,0:T(4,128)S(1)}, s32[4,512]{1,0:T(4,128)S(1)}, u32[]{:S(2)}, u32[]{:S(2)}) collective-permute-start(s32[4,512]{1,0:T(4,128)S(1)} %bitcast.24), channel_id=1, source_target_pairs={{0,64},{32,96},{64,0},{96,32},{1,65},{33,97},{65,1},{97,33},{2,66}... | collective-permute-start | bytes 24584 | tf_op jit(solution)/shard_map/ppermute | solution.py:447
  31.2 1.3 %collective-permute-done.refs_1_ = s32[4,512]{1,0:T(4,128)S(1)} collective-permute-done((s32[4,512]{1,0:T(4,128)S(1)}, s32[4,512]{1,0:T(4,128)S(1)}, u32[]{:S(2)}, u32[]{:S(2)}) %collective-permute-start) | collective-permute-done | bytes 8224 | tf_op jit(solution)/shard_map/ppermute | solution.py:447
  32.5 1.3 %route.1.goal_ref = s32[1,1024]{1,0:T(1,128)S(1)} custom-call(s32[1,1]{1,0:T(1,128)} %bitcast.8.group_ref, s32[1,4]{1,0:T(1,128)S(1)} %copy-done.17, s32[1,1024]{1,0:T(1,128)S(1)} %copy-done.15, s32[4,512]{1,0:T(4,128)S(1)} %bitcast.26, s32[4,512]{1,0:T(4,128)S(1)} %collective-permute-done.refs_1_, s32[4,512]{1,0:T(4,128)S(1)} %collective-permute-done.1.refs_2_, ...), custom_call_target="tpu_custom_call" | custom-call | flops 1000000000 | bytes 1000000 | tf_op jit(solution)/shard_map/route/pallas_call | solution.py:379
  36.3 6.0 %edge_second.1 = (f32[4096,128]{1,0:T(8,128)S(1)}, bf16[4096,128]{1,0:T(8,128)(2,1)S(1)}, bf16[1024,128]{1,0:T(8,128)(2,1)S(1)}, bf16[512,128]{1,0:T(8,128)(2,1)...) custom-call(s32[1,4096]{1,0:T(1,128)S(1)} %bitcast.16, ...), custom_call_target="tpu_custom_call" | custom-call | flops 5000000000 | bytes 8000000 | tf_op jit(solution)/shard_map/edge_second/pallas_call | solution.py:379
  42.7 3.3 %collective-permute-start.4 = (bf16[512,128]{1,0:T(8,128)(2,1)S(1)}, bf16[512,128]{1,0:T(8,128)(2,1)S(1)}, u32[]{:S(2)}, u32[]{:S(2)}) collective-permute-start(bf16[512,128]{1,0:T(8,128)(2,1)S(1)} %get-tuple-element.52), channel_id=1, source_target_pairs={{0,64},{32,96},{64,0},{96,32},{1,65},{33,97},{65,1},{97,33},{2,66}... | collective-permute-start | bytes 393224 | tf_op jit(solution)/shard_map/ppermute | solution.py:475
  47.4 3.4 %collective-permute-done.4.refs_2_ = bf16[512,128]{1,0:T(8,128)(2,1)S(1)} collective-permute-done((bf16[512,128]{1,0:T(8,128)(2,1)S(1)}, bf16[512,128]{1,0:T(8,128)(2,1)S(1)}, u32[]{:S(2)}, u32[]{:S(2)}) %collective-permute-start.4) | collective-permute-done | bytes 131104 | tf_op jit(solution)/shard_map/ppermute | solution.py:475
  50.9 1.3 %coarse.1 = (f32[256,128]{1,0:T(8,128)}, bf16[256,128]{1,0:T(8,128)(2,1)S(1)}, f32[256,128]{1,0:T(8,128)S(1)}, f32[128,128]{1,0:T(8,128)S(1)}) custom-call(bf16[256,128]{1,0:T(8,128)(2,1)S(1)} %copy-done, bf16[256,128]{1,0:T(8,128)(2,1)S(1)} %copy-done.1, bf16[256,128]{1,0:T(8,128)(2,1)S(1)} %copy-done.2, bf16[128,128]{1,0:T(8,128)(2,1)S(1)} %copy-done.3, ...), custom_call_target="tpu_custom_call" | custom-call | flops 100000000 | bytes 1000000 | tf_op jit(solution)/shard_map/coarse/pallas_call | solution.py:379
  52.2 2.1 %collective-permute-start.8 = (bf16[256,128]{1,0:T(8,128)(2,1)S(1)}, bf16[256,128]{1,0:T(8,128)(2,1)S(1)}, u32[]{:S(2)}, u32[]{:S(2)}) collective-permute-start(bf16[256,128]{1,0:T(8,128)(2,1)S(1)} %get-tuple-element.56.rest_0_), channel_id=1, source_target_pairs={{0,32},{32,64},{64,96},{96,0},{1,33},{33,65},{65,97},{97,1},{2,34}... | collective-permute-start | bytes 196616 | tf_op jit(solution)/shard_map/ppermute | solution.py:485
  54.9 1.9 %collective-permute-start.6 = (bf16[256,128]{1,0:T(8,128)(2,1)S(1)}, bf16[256,128]{1,0:T(8,128)(2,1)S(1)}, u32[]{:S(2)}, u32[]{:S(2)}) collective-permute-start(bf16[256,128]{1,0:T(8,128)(2,1)S(1)} %get-tuple-element.56.rest_0_), channel_id=1, source_target_pairs={{0,96},{32,0},{64,32},{96,64},{1,97},{33,1},{65,33},{97,65},{2,98}... | collective-permute-start | bytes 196616 | tf_op jit(solution)/shard_map/ppermute | solution.py:485
  56.7 2.2 %collective-permute-done.7.rest_2_ = bf16[256,128]{1,0:T(8,128)(2,1)S(1)} collective-permute-done((bf16[256,128]{1,0:T(8,128)(2,1)S(1)}, bf16[256,128]{1,0:T(8,128)(2,1)S(1)}, u32[]{:S(2)}, u32[]{:S(2)}) %collective-permute-start.7) | collective-permute-done | bytes 65568 | tf_op jit(solution)/shard_map/ppermute | solution.py:485
  58.9 8.0 %edge_back.1 = (bf16[4096,128]{1,0:T(8,128)(2,1)S(1)}, f32[1024,128]{1,0:T(8,128)S(1)}, bf16[32,64,128]{2,1,0:T(8,128)(2,1)}) custom-call(s32[1,4096]{1,0:T(1,128)S(1)} %bitcast.17, s32[1,4096]{1,0:T(1,128)S(1)} %bitcast.21, f32[4096,128]{1,0:T(8,128)S(1)} %get-tuple-element.47.pre_ref, bf16[4096,128]{1,0:T(8,128)(2,1)S(1)} %get-tuple-element.48.src_ref, ...), custom_call_target="tpu_custom_call" | custom-call | flops 6000000000 | bytes 10000000 | tf_op jit(solution)/shard_map/edge_back/pallas_call | solution.py:379
  68.7 10.4 %all-to-all-start.2 = ((bf16[32,64,128]{2,1,0:T(8,128)(2,1)}), bf16[32,64,128]{2,1,0:T(8,128)(2,1)S(1)}, u32[]{:S(2)}, u32[]{:S(2)}) async-start(bf16[32,64,128]{2,1,0:T(8,128)(2,1)} %get-tuple-element.57), calls=%async_computation.2 | async-start | bytes 1048576 | tf_op jit(solution)/shard_map/all_to_all | solution.py:524
  81.4 4.7 %own_back.1 = (f32[1024,128]{1,0:T(8,128)S(1)}, f32[4096,128]{1,0:T(8,128)}) custom-call(s32[1,4096]{1,0:T(1,128)S(1)} %bitcast.18, s32[1,4096]{1,0:T(1,128)S(1)} %bitcast.22, bf16[4096,128]{1,0:T(8,128)(2,1)S(1)} %copy-done.19, bf16[4096,128]{1,0:T(8,128)(2,1)S(1)} %copy-done.5, f32[1024,128]{1,0:T(8,128)S(1)} %copy-done.24, bf16[384,128]{1,0:T(8,128)(2,1)S(1)} %copy-done.8), custom_call_target="tpu_custom_call" | custom-call | flops 4000000000 | bytes 5000000 | tf_op jit(solution)/shard_map/own_back/pallas_call | solution.py:379
  86.1 4.6 %all-to-all-done.2.got_ref = bf16[32,64,128]{2,1,0:T(8,128)(2,1)S(1)} async-done(((bf16[32,64,128]{2,1,0:T(8,128)(2,1)}), bf16[32,64,128]{2,1,0:T(8,128)(2,1)S(1)}, u32[]{:S(2)}, u32[]{:S(2)}) %all-to-all-start.2) | async-done | bytes 524320 | tf_op jit(solution)/shard_map/all_to_all | solution.py:524
  90.9 2.4 %collective-permute-start.10 = (f32[48,128]{1,0:T(8,128)S(1)}, f32[48,128]{1,0:T(8,128)S(1)}, u32[]{:S(2)}, u32[]{:S(2)}) collective-permute-start(f32[48,128]{1,0:T(8,128)S(1)} %add_parts.1.refs_0_), channel_id=1, source_target_pairs={{0,64},{32,96},{64,0},{96,32},{1,65},{33,97},{65,1},{97,33},{2,66}... | collective-permute-start | bytes 73736 | tf_op jit(solution)/shard_map/ppermute | solution.py:530
  96.9 5.2 %all-to-all-start.3 = ((bf16[32,48,128]{2,1,0:T(8,128)(2,1)}), bf16[32,48,128]{2,1,0:T(8,128)(2,1)S(1)}, u32[]{:S(2)}, u32[]{:S(2)}) async-start(bf16[32,48,128]{2,1,0:T(8,128)(2,1)} %add_groups.1), calls=%async_computation.3 | async-start | bytes 786432 | tf_op jit(solution)/shard_map/all_to_all | solution.py:536
  102.1 1.3 %add_back.1 = f32[1024,128]{1,0:T(8,128)} custom-call(s32[1,256]{1,0:T(1,128)S(1)} %copy-done.16, bf16[512,128]{1,0:T(8,128)(2,1)S(1)} %bitcast.12, bf16[32,64,128]{2,1,0:T(8,128)(2,1)S(1)} %all-to-all-done.2.got_ref, f32[1024,128]{1,0:T(8,128)S(1)} %get-tuple-element.62.local_ref), custom_call_target="tpu_custom_call" | custom-call | flops 1000000000 | bytes 1000000 | tf_op jit(solution)/shard_map/add_back/pallas_call | solution.py:379
  103.4 9.0 %all-to-all-done.3 = bf16[32,48,128]{2,1,0:T(8,128)(2,1)S(1)} async-done(((bf16[32,48,128]{2,1,0:T(8,128)(2,1)}), bf16[32,48,128]{2,1,0:T(8,128)(2,1)S(1)}, u32[]{:S(2)}, u32[]{:S(2)}) %all-to-all-start.3) | async-done | bytes 393248 | tf_op jit(solution)/shard_map/all_to_all | solution.py:536
  (71 shorter events, 16.8 us)
Async XLA Ops:
  2.4 16.3 %all-to-all-start = ((bf16[32,16,128]{2,1,0:T(8,128)(2,1)}), bf16[32,16,128]{2,1,0:T(8,128)(2,1)S(1)}, u32[]{:S(2)}, u32[]{:S(2)}) async-start(bf16[32,16,128]{2,1,0:T(8,128)(2,1)} %bitcast.1), calls=%async_computation | async-start | bytes 262144 | tf_op jit(solution)/shard_map/all_to_all | solution.py:426
  15.9 16.6 %copy-start.15 = (s32[1,1024]{1,0:T(1,128)S(1)}, s32[1,1024]{1,0:T(1,128)}, u32[]{:S(2)}) copy-start(s32[1,1024]{1,0:T(1,128)} %order_ref.1) | copy-start | bytes 12292
  15.9 16.6 %copy-start.17 = (s32[1,4]{1,0:T(1,128)S(1)}, s32[1,4]{1,0:T(1,128)}, u32[]{:S(2)}) copy-start(s32[1,4]{1,0:T(1,128)} %count_ref.1) | copy-start | bytes 52
  20.0 13.7 %all-to-all-start.1 = ((bf16[32,16,128]{2,1,0:T(8,128)(2,1)}), bf16[32,16,128]{2,1,0:T(8,128)(2,1)S(1)}, u32[]{:S(2)}, u32[]{:S(2)}) async-start(bf16[32,16,128]{2,1,0:T(8,128)(2,1)} %bitcast.6), calls=%async_computation.1 | async-start | bytes 262144 | tf_op jit(solution)/shard_map/all_to_all | solution.py:449
  24.8 5.7 %collective-permute-start.2 = (s32[4,512]{1,0:T(4,128)S(1)}, s32[4,512]{1,0:T(4,128)S(1)}, u32[]{:S(2)}, u32[]{:S(2)}) collective-permute-start(s32[4,512]{1,0:T(4,128)S(1)} %bitcast.23), channel_id=1, source_target_pairs={{0,32},{32,64},{64,96},{96,0},{1,33},{33,65},{65,97},{97,1},{2,34}... | collective-permute-start | bytes 24584 | tf_op jit(solution)/shard_map/ppermute | solution.py:447
  26.5 4.7 %collective-permute-start.1 = (s32[4,512]{1,0:T(4,128)S(1)}, s32[4,512]{1,0:T(4,128)S(1)}, u32[]{:S(2)}, u32[]{:S(2)}) collective-permute-start(s32[4,512]{1,0:T(4,128)S(1)} %bitcast.24), channel_id=1, source_target_pairs={{0,64},{32,96},{64,0},{96,32},{1,65},{33,97},{65,1},{97,33},{2,66}... | collective-permute-start | bytes 24584 | tf_op jit(solution)/shard_map/ppermute | solution.py:447
  29.8 2.7 %collective-permute-start = (s32[4,512]{1,0:T(4,128)S(1)}, s32[4,512]{1,0:T(4,128)S(1)}, u32[]{:S(2)}, u32[]{:S(2)}) collective-permute-start(s32[4,512]{1,0:T(4,128)S(1)} %bitcast.25), channel_id=1, source_target_pairs={{0,96},{32,0},{64,32},{96,64},{1,97},{33,1},{65,33},{97,65},{2,98}... | collective-permute-start | bytes 24584 | tf_op jit(solution)/shard_map/ppermute | solution.py:447
  36.3 14.6 %copy-start = (bf16[256,128]{1,0:T(8,128)(2,1)S(1)}, bf16[256,128]{1,0:T(8,128)(2,1)}, u32[]{:S(2)}) copy-start(bf16[256,128]{1,0:T(8,128)(2,1)} %feat_ref.1) | copy-start | bytes 196612
  36.3 14.6 %copy-start.1 = (bf16[256,128]{1,0:T(8,128)(2,1)S(1)}, bf16[256,128]{1,0:T(8,128)(2,1)}, u32[]{:S(2)}) copy-start(bf16[256,128]{1,0:T(8,128)(2,1)} %cot_ref.3) | copy-start | bytes 196612
  36.3 14.6 %copy-start.2 = (bf16[256,128]{1,0:T(8,128)(2,1)S(1)}, bf16[256,128]{1,0:T(8,128)(2,1)}, u32[]{:S(2)}) copy-start(bf16[256,128]{1,0:T(8,128)(2,1)} %w1_ref.5) | copy-start | bytes 196612
  36.3 14.6 %copy-start.3 = (bf16[128,128]{1,0:T(8,128)(2,1)S(1)}, bf16[128,128]{1,0:T(8,128)(2,1)}, u32[]{:S(2)}) copy-start(bf16[128,128]{1,0:T(8,128)(2,1)} %w2_ref.4) | copy-start | bytes 98308
  36.3 22.7 %copy-start.5 = (bf16[4096,128]{1,0:T(8,128)(2,1)S(1)}, bf16[4096,128]{1,0:T(8,128)(2,1)}, u32[]{:S(2)}) copy-start(bf16[4096,128]{1,0:T(8,128)(2,1)} %cot_ref.5) | copy-start | bytes 3145732
  36.3 22.7 %copy-start.21 = (bf16[4096,128]{1,0:T(8,128)(2,1)S(1)}, bf16[4096,128]{1,0:T(8,128)(2,1)}, u32[]{:S(2)}) copy-start(bf16[4096,128]{1,0:T(8,128)(2,1)} %get-tuple-element.44.tgt_ref) | copy-start | bytes 3145732
  42.3 5.1 %collective-permute-start.3 = (bf16[512,128]{1,0:T(8,128)(2,1)S(1)}, bf16[512,128]{1,0:T(8,128)(2,1)S(1)}, u32[]{:S(2)}, u32[]{:S(2)}) collective-permute-start(bf16[512,128]{1,0:T(8,128)(2,1)S(1)} %get-tuple-element.51), channel_id=1, source_target_pairs={{0,32},{32,64},{64,96},{96,0},{1,33},{33,65},{65,97},{97,1},{2,34}... | collective-permute-start | bytes 393224 | tf_op jit(solution)/shard_map/ppermute | solution.py:475
  42.7 8.1 %collective-permute-start.4 = (bf16[512,128]{1,0:T(8,128)(2,1)S(1)}, bf16[512,128]{1,0:T(8,128)(2,1)S(1)}, u32[]{:S(2)}, u32[]{:S(2)}) collective-permute-start(bf16[512,128]{1,0:T(8,128)(2,1)S(1)} %get-tuple-element.52), channel_id=1, source_target_pairs={{0,64},{32,96},{64,0},{96,32},{1,65},{33,97},{65,1},{97,33},{2,66}... | collective-permute-start | bytes 393224 | tf_op jit(solution)/shard_map/ppermute | solution.py:475
  46.0 4.9 %collective-permute-start.5 = (bf16[512,128]{1,0:T(8,128)(2,1)S(1)}, bf16[512,128]{1,0:T(8,128)(2,1)S(1)}, u32[]{:S(2)}, u32[]{:S(2)}) collective-permute-start(bf16[512,128]{1,0:T(8,128)(2,1)S(1)} %get-tuple-element.53), channel_id=1, source_target_pairs={{0,96},{32,0},{64,32},{96,64},{1,97},{33,1},{65,33},{97,65},{2,98}... | collective-permute-start | bytes 393224 | tf_op jit(solution)/shard_map/ppermute | solution.py:475
  52.2 4.5 %collective-permute-start.8 = (bf16[256,128]{1,0:T(8,128)(2,1)S(1)}, bf16[256,128]{1,0:T(8,128)(2,1)S(1)}, u32[]{:S(2)}, u32[]{:S(2)}) collective-permute-start(bf16[256,128]{1,0:T(8,128)(2,1)S(1)} %get-tuple-element.56.rest_0_), channel_id=1, source_target_pairs={{0,32},{32,64},{64,96},{96,0},{1,33},{33,65},{65,97},{97,1},{2,34}... | collective-permute-start | bytes 196616 | tf_op jit(solution)/shard_map/ppermute | solution.py:485
  54.3 4.6 %collective-permute-start.7 = (bf16[256,128]{1,0:T(8,128)(2,1)S(1)}, bf16[256,128]{1,0:T(8,128)(2,1)S(1)}, u32[]{:S(2)}, u32[]{:S(2)}) collective-permute-start(bf16[256,128]{1,0:T(8,128)(2,1)S(1)} %get-tuple-element.56.rest_0_), channel_id=1, source_target_pairs={{0,64},{32,96},{64,0},{96,32},{1,65},{33,97},{65,1},{97,33},{2,66}... | collective-permute-start | bytes 196616 | tf_op jit(solution)/shard_map/ppermute | solution.py:485
  54.9 4.1 %collective-permute-start.6 = (bf16[256,128]{1,0:T(8,128)(2,1)S(1)}, bf16[256,128]{1,0:T(8,128)(2,1)S(1)}, u32[]{:S(2)}, u32[]{:S(2)}) collective-permute-start(bf16[256,128]{1,0:T(8,128)(2,1)S(1)} %get-tuple-element.56.rest_0_), channel_id=1, source_target_pairs={{0,96},{32,0},{64,32},{96,64},{1,97},{33,1},{65,33},{97,65},{2,98}... | collective-permute-start | bytes 196616 | tf_op jit(solution)/shard_map/ppermute | solution.py:485
  68.7 22.1 %all-to-all-start.2 = ((bf16[32,64,128]{2,1,0:T(8,128)(2,1)}), bf16[32,64,128]{2,1,0:T(8,128)(2,1)S(1)}, u32[]{:S(2)}, u32[]{:S(2)}) async-start(bf16[32,64,128]{2,1,0:T(8,128)(2,1)} %get-tuple-element.57), calls=%async_computation.2 | async-start | bytes 1048576 | tf_op jit(solution)/shard_map/all_to_all | solution.py:524
  90.8 4.0 %collective-permute-start.11 = (f32[48,128]{1,0:T(8,128)S(1)}, f32[48,128]{1,0:T(8,128)S(1)}, u32[]{:S(2)}, u32[]{:S(2)}) collective-permute-start(f32[48,128]{1,0:T(8,128)S(1)} %add_parts.1.refs_0_), channel_id=1, source_target_pairs={{0,32},{32,64},{64,96},{96,0},{1,33},{33,65},{65,97},{97,1},{2,34}... | collective-permute-start | bytes 73736 | tf_op jit(solution)/shard_map/ppermute | solution.py:530
  90.9 4.4 %collective-permute-start.10 = (f32[48,128]{1,0:T(8,128)S(1)}, f32[48,128]{1,0:T(8,128)S(1)}, u32[]{:S(2)}, u32[]{:S(2)}) collective-permute-start(f32[48,128]{1,0:T(8,128)S(1)} %add_parts.1.refs_0_), channel_id=1, source_target_pairs={{0,64},{32,96},{64,0},{96,32},{1,65},{33,97},{65,1},{97,33},{2,66}... | collective-permute-start | bytes 73736 | tf_op jit(solution)/shard_map/ppermute | solution.py:530
  93.3 2.8 %collective-permute-start.9 = (f32[48,128]{1,0:T(8,128)S(1)}, f32[48,128]{1,0:T(8,128)S(1)}, u32[]{:S(2)}, u32[]{:S(2)}) collective-permute-start(f32[48,128]{1,0:T(8,128)S(1)} %add_parts.1.refs_0_), channel_id=1, source_target_pairs={{0,96},{32,0},{64,32},{96,64},{1,97},{33,1},{65,33},{97,65},{2,98}... | collective-permute-start | bytes 73736 | tf_op jit(solution)/shard_map/ppermute | solution.py:530
  96.9 15.5 %all-to-all-start.3 = ((bf16[32,48,128]{2,1,0:T(8,128)(2,1)}), bf16[32,48,128]{2,1,0:T(8,128)(2,1)S(1)}, u32[]{:S(2)}, u32[]{:S(2)}) async-start(bf16[32,48,128]{2,1,0:T(8,128)(2,1)} %add_groups.1), calls=%async_computation.3 | async-start | bytes 786432 | tf_op jit(solution)/shard_map/all_to_all | solution.py:536
  (17 other events, 141.4 us)

commit v4 on v3

--- a/solution.py
+++ b/solution.py
@@ -112,11 +112,11 @@
 
 
 def spread_kernel(wanted_ref, out_ref):
-    domains, slots = wanted_ref.shape
+    _, domains, slots = wanted_ref.shape
     ghosts = out_ref.shape[0]
     first = lax.broadcasted_iota(I32, (ghosts, domains), 0) // slots
     pick = as_hit(first == lax.broadcasted_iota(I32, (ghosts, domains), 1))
-    by_owner = nn(pick, wanted_ref[...].astype(F32).astype(BF))
+    by_owner = nn(pick, wanted_ref[0].astype(F32).astype(BF))
     slot = lax.broadcasted_iota(I32, (ghosts, slots), 0) % slots
     own = jnp.where(slot == lax.broadcasted_iota(I32, (ghosts, slots), 1), by_owner, 0.0).astype(BF)
     out_ref[...] = nn(own, jnp.ones((slots, LANES), BF)).astype(BF)
@@ -129,9 +129,10 @@
     out_ref[...] = nn(hit_columns(wanted, border), shared).astype(BF)
 
 
-def route_kernel(group_ref, count_ref, order_ref, *refs, coarse):
-    slot_refs, out_ref = refs[:-1], refs[-1]
-    groups = len(slot_refs)
+def pool_kernel(group_ref, count_ref, order_ref, updated_ref, node_cot_ref, *refs):
+    groups = (len(refs) - 1) // 2
+    slot_refs, out_ref, send_refs = refs[:groups], refs[groups], refs[groups + 1 :]
+    coarse = send_refs[0].shape[0] // 2
     capacity = slot_refs[0].shape[1]
     rows = order_ref.shape[1]
     here = group_ref[0, 0]
@@ -152,21 +153,26 @@
         goal = jnp.where(inside, line, goal)
     digits = jnp.where(lax.broadcasted_iota(I32, (8, rows), 0) == 0, owner, goal)
     by_row = nt(digits.astype(F32).astype(BF), hit_rows(order_ref[...], rows))
-    out_ref[...] = (by_row[0:1, :] * coarse + by_row[1:2, :]).astype(I32)
-
-
-def edge_first_kernel(source_ref, target_ref, nodes_ref, src_ref, tgt_ref):
+    goal = (by_row[0:1, :] * coarse + by_row[1:2, :]).astype(I32)
+    out_ref[...] = goal
+    both = jnp.concatenate([updated_ref[...], node_cot_ref[...]], axis=1)
+    pooled = nn(hit_rows(goal, groups * coarse), both).astype(BF)
+    for k, send_ref in enumerate(send_refs):
+        send_ref[:coarse, :] = pooled[k * coarse : (k + 1) * coarse, :LANES]
+        send_ref[coarse:, :] = pooled[k * coarse : (k + 1) * coarse, LANES:]
+
+
+def edge_first_kernel(source_ref, target_ref, nodes_ref, out_ref):
     nodes = halves(nodes_ref[...])
-    src_ref[...] = pick_rows(spread_column(source_ref[...]), nodes).astype(BF)
-    tgt_ref[...] = pick_rows(spread_column(target_ref[...]), nodes).astype(BF)
+    out_ref[0] = pick_rows(spread_column(source_ref[...]), nodes).astype(BF)
+    out_ref[1] = pick_rows(spread_column(target_ref[...]), nodes).astype(BF)
 
 
 def edge_second_kernel(
-    source_ref, target_ref, src_in_ref, tgt_ref, edges_ref, ghosts_ref, w1_ref, w2_ref,
-    nodes_ref, v1_ref, v2_ref, goal_ref, node_cot_ref,
-    pre_ref, src_ref, summed_ref, *rest,
+    source_ref, target_ref, own_ref, edges_ref, ghosts_ref, w1_ref, w2_ref,
+    nodes_ref, v1_ref, v2_ref,
+    pre_ref, src_ref, summed_ref, updated_ref, total,
 ):
-    send_refs, total = rest[:-1], rest[-1]
     step = pl.program_id(0)
     rows = nodes_ref.shape[0]
 
@@ -180,9 +186,10 @@
     messages = []
     for part in range(0, target.shape[1], SECOND_SUB):
         here = slice(part, part + SECOND_SUB)
-        src = src_in_ref[here, :] + pick_rows(from_ghost[here], ghosts).astype(BF)
+        src = own_ref[0, here, :] + pick_rows(from_ghost[here], ghosts).astype(BF)
         src_ref[here, :] = src
-        pre = nn(jnp.concatenate([src, tgt_ref[here, :], edges_ref[here, :]], axis=1), w1_ref[...])
+        stacked = jnp.concatenate([src, own_ref[1, here, :], edges_ref[here, :]], axis=1)
+        pre = nn(stacked, w1_ref[...])
         pre_ref[here, :] = pre
         hidden = (pre * sigmoid(pre)).astype(BF)
         message, _ = norm_parts(nn(hidden, w2_ref[...]))
@@ -199,13 +206,7 @@
         pre_node = nn(jnp.concatenate([nodes, summed], axis=1), v1_ref[...])
         hidden_node = (pre_node * sigmoid(pre_node)).astype(BF)
         normed, _ = norm_parts(nn(hidden_node, v2_ref[...]))
-        updated = (nodes.astype(F32) + normed).astype(BF)
-        coarse = send_refs[0].shape[0] // 2
-        both = jnp.concatenate([updated, node_cot_ref[...]], axis=1)
-        pooled = nn(hit_rows(goal_ref[...], len(send_refs) * coarse), both).astype(BF)
-        for k, send_ref in enumerate(send_refs):
-            send_ref[:coarse, :] = pooled[k * coarse : (k + 1) * coarse, :LANES]
-            send_ref[coarse:, :] = pooled[k * coarse : (k + 1) * coarse, LANES:]
+        updated_ref[...] = (nodes.astype(F32) + normed).astype(BF)
 
 
 def coarse_kernel(feat_ref, cot_ref, w1_ref, w2_ref, *refs):
@@ -276,7 +277,7 @@
     grad_pre = jnp.concatenate(grad_pres, axis=0)
     grad_pre_ref[...] = grad_pre
     gw2[...] += tn(jnp.concatenate(hiddens, axis=0), jnp.concatenate(grad_norms, axis=0))
-    stacked = jnp.concatenate([src_ref[...], tgt_ref[...], edges_ref[...]], axis=1)
+    stacked = jnp.concatenate([src_ref[...], tgt_ref[0], edges_ref[...]], axis=1)
     gw1[...] += tn(stacked, grad_pre)
     source = source_ref[...] - rows
     by_ghost[...] += sum_rows(source, spread_column(source), grad_pre, by_ghost.shape[0])
@@ -420,24 +421,23 @@
     source = edge_source.reshape(1, edges)
     target = edge_target.reshape(1, edges)
     spread = call(
-        spread_kernel, shape((ghosts, latent), BF), ghost_pos.reshape(domains, slots),
+        spread_kernel, shape((ghosts, latent), BF), ghost_pos,
         flops=10**6, bytes_accessed=10**5, name="spread", vmem=8,
     )
     asked = exchange(spread.reshape(domains, slots, latent), "dom").reshape(ghosts, latent)
     slot_list = coarse_slot.reshape(groups, -1)
     here = lax.axis_index("group").astype(I32).reshape(1, 1)
 
-    grid, index_spec, edge_spec = edge_blocks(2048)
-    src_own, tgt_rows = call(
-        edge_first_kernel,
-        [shape((edges, latent), BF), shape((edges, latent), BF)],
-        source, target, node_features,
+    grid_block = 2048
+    grid, index_spec, edge_spec = edge_blocks(grid_block)
+    own_rows = call(
+        edge_first_kernel, shape((2, edges, latent), BF), source, target, node_features,
         grid=grid,
         in_specs=[index_spec, index_spec, whole((rows, latent))],
-        out_specs=[edge_spec, edge_spec],
+        out_specs=pl.BlockSpec((2, grid_block, latent), lambda i: (0, i, 0)),
         flops=4 * 10**9, bytes_accessed=3 * 10**6, name="edge_first", vmem=61,
     )
-    asked, src_own, tgt_rows = lax.optimization_barrier((asked, src_own, tgt_rows))
+    asked, own_rows = lax.optimization_barrier((asked, own_rows))
     share = call(
         share_kernel, shape((ghosts, latent), BF), boundary, asked, node_features,
         flops=10**9, bytes_accessed=10**6, name="share", vmem=16,
@@ -447,29 +447,27 @@
         lax.ppermute(slot_list, "group", turned(ahead)) for ahead in range(1, groups)
     ]
     ghost_rows = exchange(share.reshape(domains, slots, latent), "dom").reshape(ghosts, latent)
-    goal = call(
-        functools.partial(route_kernel, coarse=coarse), shape((1, rows), I32),
-        here, restr_count, restr_order, *slot_lists,
-        in_specs=[pl.BlockSpec(memory_space=pltpu.SMEM)] * 2
-        + [pl.BlockSpec(memory_space=pltpu.VMEM)] * (1 + groups),
-        flops=10**9, bytes_accessed=10**6, name="route", vmem=16,
-    )
     grid, index_spec, edge_spec = edge_blocks(4096)
-    pre, src_rows, summed, *send = call(
+    pre, src_rows, summed, updated = call(
         edge_second_kernel,
-        [shape((edges, latent), F32), shape((edges, latent), BF), shape((rows, latent), BF)]
-        + [shape((2 * coarse, latent), BF)] * groups,
-        source, target, src_own, tgt_rows, edge_features, ghost_rows, edge_w_one, edge_w_two,
-        node_features, node_w_one, node_w_two, goal, node_cotangent,
+        [shape((edges, latent), F32), shape((edges, latent), BF), shape((rows, latent), BF),
+         shape((rows, latent), BF)],
+        source, target, own_rows, edge_features, ghost_rows, edge_w_one, edge_w_two,
+        node_features, node_w_one, node_w_two,
         grid=grid,
-        in_specs=[index_spec, index_spec, edge_spec, edge_spec, edge_spec, whole((ghosts, latent)),
-                  whole((3 * latent, latent)), whole((latent, latent)), whole((rows, latent)),
-                  whole((2 * latent, latent)), whole((latent, latent)),
-                  whole((1, rows)), whole((rows, latent))],
-        out_specs=[edge_spec, edge_spec, whole((rows, latent))]
-        + [whole((2 * coarse, latent))] * groups,
+        in_specs=[index_spec, index_spec, whole((2, edges, latent)), edge_spec,
+                  whole((ghosts, latent)), whole((3 * latent, latent)), whole((latent, latent)),
+                  whole((rows, latent)), whole((2 * latent, latent)), whole((latent, latent))],
+        out_specs=[edge_spec, edge_spec, whole((rows, latent)), whole((rows, latent))],
         scratch=[pltpu.VMEM((rows // 2, 2 * latent), F32)],
         flops=5 * 10**9, bytes_accessed=8 * 10**6, name="edge_second",
+    )
+    goal, *send = call(
+        pool_kernel, [shape((1, rows), I32)] + [shape((2 * coarse, latent), BF)] * groups,
+        here, restr_count, restr_order, updated, node_cotangent, *slot_lists,
+        in_specs=[pl.BlockSpec(memory_space=pltpu.SMEM)] * 2
+        + [pl.BlockSpec(memory_space=pltpu.VMEM)] * (3 + groups),
+        flops=10**9, bytes_accessed=10**6, name="pool", vmem=16,
     )
     got = [send[0]] + [
         lax.ppermute(send[ahead], "group", turned(-ahead)) for ahead in range(1, groups)
@@ -491,11 +489,12 @@
     grad_pre, node_local, joint = call(
         edge_back_kernel,
         [shape((edges, latent), BF), shape((rows, latent), F32), shape(joint_shape, BF)],
-        source, target, pre, src_rows, tgt_rows, edge_features, edge_cotangent, edge_w_one, edge_w_two,
+        source, target, pre, src_rows, own_rows, edge_features, edge_cotangent, edge_w_one, edge_w_two,
         goal, node_cotangent, node_features, summed, node_w_one, node_w_two,
         grad_c_one, grad_c_two, *returned,
         grid=grid,
-        in_specs=[index_spec, index_spec, edge_spec, edge_spec, edge_spec, edge_spec, edge_spec,
+        in_specs=[index_spec, index_spec, edge_spec, edge_spec,
+                  pl.BlockSpec((1, edges, latent), lambda i: (1, 0, 0)), edge_spec, edge_spec,
                   whole((3 * latent, latent)), whole((latent, latent)),
                   whole((1, rows)),
                   whole((rows, latent)), whole((rows, latent)), whole((rows, latent)),

time: 114 us -> 111 us (0.974)
  starting transfers between devices: 47 us -> 42.9 us
  waiting for transfers between devices: 26.7 us -> 29.5 us
    all_to_all x1, starting transfers between devices: 10.4 us -> 5.86 us  [local(): exchange(joint, 'dom')]
    all_to_all x1, waiting for transfers between devices: 0.01 us -> 1.95 us  [local(): exchange(share.reshape(domains, slots, latent), 'dom')]
    ppermute x3, waiting for transfers between devices: 1.95 us -> 0.01 us  [local(): lax.ppermute(slot_list, 'group', turned(ahead))]
    ppermute x3, starting transfers between devices: 4.44 us -> 5.72 us  [local(): lax.ppermute(send[ahead], 'group', turned(-ahead))]
    ppermute x3, waiting for transfers between devices: 2.23 us -> 3.42 us  [local(): lax.ppermute(coarse_back, 'group', turned(ahead))]
    unnamed x51 -> x47, local copies, waits for them, and re-layouts: 7.34 us -> 6.48 us
  transfers between devices with their start and end apart: 16 -> 16, of which waited for: 12 -> 12; matrix products, arithmetic and copies ran while one was open for 0% -> 0% of each run, Pallas kernels for 11% -> 14%
where the time goes in v4:
time: 111 us; the launch traced here: 110 us
  starting transfers between devices  42.9 us (39%)
  Pallas kernels  30.6 us (28%)
  waiting for transfers between devices  29.5 us (27%)
  local copies, waits for them, and re-layouts  6.48 us (6%)
    pallas_call x12, Pallas kernels, call(): pl.pallas_call(kernel, out_shape=out_shapes if single else list(out_shape...  30.6 us
    all_to_all x1, waiting for transfers between devices, local(): pack_all = exchange(pack_sum, 'dom').reshape(pack_rows, latent)  8.95 us
    all_to_all x1, starting transfers between devices, local(): exchange(spread.reshape(domains, slots, latent), 'dom')  8.59 us
    unnamed x47, local copies, waits for them, and re-layouts  6.48 us
    all_to_all x1, starting transfers between devices, local(): exchange(joint, 'dom')  5.86 us
    ppermute x3, starting transfers between devices, local(): lax.ppermute(slot_list, 'group', turned(ahead))  5.74 us
    ppermute x3, starting transfers between devices, local(): lax.ppermute(send[ahead], 'group', turned(-ahead))  5.72 us
    ppermute x3, waiting for transfers between devices, local(): lax.ppermute(send[ahead], 'group', turned(-ahead))  5.32 us
  transfers between devices with their start and end apart: 16, of which 12 were waited for; matrix products, arithmetic and copies ran while one was open for 0% of the time, Pallas kernels for 14%

profile of v4, /device:TPU:1, one launch (start us, length us, event | category | flops | bytes accessed | tf_op | source)
XLA Modules:
  0.0 110.4 jit_solution(2649540225238950829)
XLA Ops:
  2.4 8.6 %all-to-all-start = ((bf16[32,16,128]{2,1,0:T(8,128)(2,1)}), bf16[32,16,128]{2,1,0:T(8,128)(2,1)S(1)}, u32[]{:S(2)}, u32[]{:S(2)}) async-start(bf16[32,16,128]{2,1,0:T(8,128)(2,1)} %bitcast), calls=%async_computation | async-start | bytes 262144 | tf_op jit(solution)/shard_map/all_to_all | solution.py:427
  11.0 4.8 %edge_first.1.own_ref.tgt_ref = bf16[2,4096,128]{2,1,0:T(8,128)(2,1)} custom-call(s32[1,4096]{1,0:T(1,128)} %bitcast.13, s32[1,4096]{1,0:T(1,128)} %bitcast.17, bf16[1024,128]{1,0:T(8,128)(2,1)} %nodes_ref.7), custom_call_target="tpu_custom_call" | custom-call | flops 4000000000 | bytes 3000000 | tf_op jit(solution)/shard_map/edge_first/pallas_call | solution.py:380
  15.9 2.8 %all-to-all-done = bf16[32,16,128]{2,1,0:T(8,128)(2,1)S(1)} async-done(((bf16[32,16,128]{2,1,0:T(8,128)(2,1)}), bf16[32,16,128]{2,1,0:T(8,128)(2,1)S(1)}, u32[]{:S(2)}, u32[]{:S(2)}) %all-to-all-start) | async-done | bytes 131104 | tf_op jit(solution)/shard_map/all_to_all | solution.py:427
  19.9 4.6 %all-to-all-start.1 = ((bf16[32,16,128]{2,1,0:T(8,128)(2,1)}), bf16[32,16,128]{2,1,0:T(8,128)(2,1)S(1)}, u32[]{:S(2)}, u32[]{:S(2)}) async-start(bf16[32,16,128]{2,1,0:T(8,128)(2,1)} %bitcast.5), calls=%async_computation.1 | async-start | bytes 262144 | tf_op jit(solution)/shard_map/all_to_all | solution.py:449
  24.6 1.7 %collective-permute-start.2 = (s32[4,512]{1,0:T(4,128)S(1)}, s32[4,512]{1,0:T(4,128)S(1)}, u32[]{:S(2)}, u32[]{:S(2)}) collective-permute-start(s32[4,512]{1,0:T(4,128)S(1)} %bitcast.21), channel_id=1, source_target_pairs={{0,32},{32,64},{64,96},{96,0},{1,33},{33,65},{65,97},{97,1},{2,34}... | collective-permute-start | bytes 24584 | tf_op jit(solution)/shard_map/ppermute | solution.py:447
  26.3 3.3 %collective-permute-start.1 = (s32[4,512]{1,0:T(4,128)S(1)}, s32[4,512]{1,0:T(4,128)S(1)}, u32[]{:S(2)}, u32[]{:S(2)}) collective-permute-start(s32[4,512]{1,0:T(4,128)S(1)} %bitcast.22), channel_id=1, source_target_pairs={{0,64},{32,96},{64,0},{96,32},{1,65},{33,97},{65,1},{97,33},{2,66}... | collective-permute-start | bytes 24584 | tf_op jit(solution)/shard_map/ppermute | solution.py:447
  30.3 2.0 %all-to-all-done.1 = bf16[32,16,128]{2,1,0:T(8,128)(2,1)S(1)} async-done(((bf16[32,16,128]{2,1,0:T(8,128)(2,1)}), bf16[32,16,128]{2,1,0:T(8,128)(2,1)S(1)}, u32[]{:S(2)}, u32[]{:S(2)}) %all-to-all-start.1) | async-done | bytes 131104 | tf_op jit(solution)/shard_map/all_to_all | solution.py:449
  32.3 1.6 %copy-done.18 = bf16[2,4096,128]{2,1,0:T(8,128)(2,1)S(1)} copy-done((bf16[2,4096,128]{2,1,0:T(8,128)(2,1)S(1)}, bf16[2,4096,128]{2,1,0:T(8,128)(2,1)}, u32[]{:S(2)}) %copy-start.18) | copy-done | bytes 2097176
  33.9 4.7 %edge_second.1 = (f32[4096,128]{1,0:T(8,128)S(1)}, bf16[4096,128]{1,0:T(8,128)(2,1)S(1)}, bf16[1024,128]{1,0:T(8,128)(2,1)S(1)}, bf16[1024,128]{1,0:T(8,128)(2,1)S(1)}) custom-call(s32[1,4096]{1,0:T(1,128)S(1)} %bitcast.14, s32[1,4096]{1,0:T(1,128)S(1)} %bitcast.18, bf16[2,4096,128]{2,1,0:T(8,128)(2,1)S(1)} %copy-done.18, bf16[4096,128]{1,0:T(8,128)(2,1)S(1)} %copy-done.4, ...), custom_call_target="tpu_custom_call" | custom-call | flops 5000000000 | bytes 8000000 | tf_op jit(solution)/shard_map/edge_second/pallas_call | solution.py:380
  38.8 1.9 %pool.1 = (s32[1,1024]{1,0:T(1,128)S(1)}, bf16[512,128]{1,0:T(8,128)(2,1)S(1)}, bf16[512,128]{1,0:T(8,128)(2,1)S(1)}, bf16[512,128]{1,0:T(8,128)(2,1)S(1)}, bf16[512,128]{1,0:T(8,128)(2,1)S(1)}) custom-call(s32[1,1]{1,0:T(1,128)} %bitcast.7.group_ref, s32[1,4]{1,0:T(1,128)S(1)} %copy-done.17, s32[1,1024]{1,0:T(1,128)S(1)} %copy-done.15, ...), custom_call_target="tpu_custom_call" | custom-call | flops 1000000000 | bytes 1000000 | tf_op jit(solution)/shard_map/pool/pallas_call | solution.py:380
  40.7 1.7 %collective-permute-start.3 = (bf16[512,128]{1,0:T(8,128)(2,1)S(1)}, bf16[512,128]{1,0:T(8,128)(2,1)S(1)}, u32[]{:S(2)}, u32[]{:S(2)}) collective-permute-start(bf16[512,128]{1,0:T(8,128)(2,1)S(1)} %get-tuple-element.49), channel_id=1, source_target_pairs={{0,32},{32,64},{64,96},{96,0},{1,33},{33,65},{65,97},{97,1},{2,34}... | collective-permute-start | bytes 393224 | tf_op jit(solution)/shard_map/ppermute | solution.py:473
  42.4 3.3 %collective-permute-start.4 = (bf16[512,128]{1,0:T(8,128)(2,1)S(1)}, bf16[512,128]{1,0:T(8,128)(2,1)S(1)}, u32[]{:S(2)}, u32[]{:S(2)}) collective-permute-start(bf16[512,128]{1,0:T(8,128)(2,1)S(1)} %get-tuple-element.50), channel_id=1, source_target_pairs={{0,64},{32,96},{64,0},{96,32},{1,65},{33,97},{65,1},{97,33},{2,66}... | collective-permute-start | bytes 393224 | tf_op jit(solution)/shard_map/ppermute | solution.py:473
  46.4 1.6 %collective-permute-done.3.refs_1_ = bf16[512,128]{1,0:T(8,128)(2,1)S(1)} collective-permute-done((bf16[512,128]{1,0:T(8,128)(2,1)S(1)}, bf16[512,128]{1,0:T(8,128)(2,1)S(1)}, u32[]{:S(2)}, u32[]{:S(2)}) %collective-permute-start.3) | collective-permute-done | bytes 131104 | tf_op jit(solution)/shard_map/ppermute | solution.py:473
  48.1 3.7 %collective-permute-done.4.refs_2_ = bf16[512,128]{1,0:T(8,128)(2,1)S(1)} collective-permute-done((bf16[512,128]{1,0:T(8,128)(2,1)S(1)}, bf16[512,128]{1,0:T(8,128)(2,1)S(1)}, u32[]{:S(2)}, u32[]{:S(2)}) %collective-permute-start.4) | collective-permute-done | bytes 131104 | tf_op jit(solution)/shard_map/ppermute | solution.py:473
  54.3 2.0 %collective-permute-start.7 = (bf16[256,128]{1,0:T(8,128)(2,1)S(1)}, bf16[256,128]{1,0:T(8,128)(2,1)S(1)}, u32[]{:S(2)}, u32[]{:S(2)}) collective-permute-start(bf16[256,128]{1,0:T(8,128)(2,1)S(1)} %get-tuple-element.54.rest_0_), channel_id=1, source_target_pairs={{0,64},{32,96},{64,0},{96,32},{1,65},{33,97},{65,1},{97,33},{2,66}... | collective-permute-start | bytes 196616 | tf_op jit(solution)/shard_map/ppermute | solution.py:483
  57.4 1.9 %collective-permute-done.7.rest_2_ = bf16[256,128]{1,0:T(8,128)(2,1)S(1)} collective-permute-done((bf16[256,128]{1,0:T(8,128)(2,1)S(1)}, bf16[256,128]{1,0:T(8,128)(2,1)S(1)}, u32[]{:S(2)}, u32[]{:S(2)}) %collective-permute-start.7) | collective-permute-done | bytes 65568 | tf_op jit(solution)/shard_map/ppermute | solution.py:483
  60.2 7.8 %edge_back.1 = (bf16[4096,128]{1,0:T(8,128)(2,1)S(1)}, f32[1024,128]{1,0:T(8,128)S(1)}, bf16[32,64,128]{2,1,0:T(8,128)(2,1)}) custom-call(s32[1,4096]{1,0:T(1,128)S(1)} %bitcast.15, s32[1,4096]{1,0:T(1,128)S(1)} %bitcast.19, f32[4096,128]{1,0:T(8,128)S(1)} %get-tuple-element.42.pre_ref, bf16[4096,128]{1,0:T(8,128)(2,1)S(1)} %get-tuple-element.43.src_ref, ...), custom_call_target="tpu_custom_call" | custom-call | flops 6000000000 | bytes 10000000 | tf_op jit(solution)/shard_map/edge_back/pallas_call | solution.py:380
  69.8 5.9 %all-to-all-start.2 = ((bf16[32,64,128]{2,1,0:T(8,128)(2,1)}), bf16[32,64,128]{2,1,0:T(8,128)(2,1)S(1)}, u32[]{:S(2)}, u32[]{:S(2)}) async-start(bf16[32,64,128]{2,1,0:T(8,128)(2,1)} %get-tuple-element.55), calls=%async_computation.2 | async-start | bytes 1048576 | tf_op jit(solution)/shard_map/all_to_all | solution.py:523
  77.9 4.7 %own_back.1 = (f32[1024,128]{1,0:T(8,128)S(1)}, f32[4096,128]{1,0:T(8,128)}) custom-call(s32[1,4096]{1,0:T(1,128)S(1)} %bitcast.16, s32[1,4096]{1,0:T(1,128)S(1)} %bitcast.20, bf16[4096,128]{1,0:T(8,128)(2,1)S(1)} %copy-done.20, bf16[4096,128]{1,0:T(8,128)(2,1)S(1)} %copy-done.5, f32[1024,128]{1,0:T(8,128)S(1)} %copy-done.22, bf16[384,128]{1,0:T(8,128)(2,1)S(1)} %copy-done.8), custom_call_target="tpu_custom_call" | custom-call | flops 4000000000 | bytes 5000000 | tf_op jit(solution)/shard_map/own_back/pallas_call | solution.py:380
  82.7 4.6 %all-to-all-done.2.got_ref = bf16[32,64,128]{2,1,0:T(8,128)(2,1)S(1)} async-done(((bf16[32,64,128]{2,1,0:T(8,128)(2,1)}), bf16[32,64,128]{2,1,0:T(8,128)(2,1)S(1)}, u32[]{:S(2)}, u32[]{:S(2)}) %all-to-all-start.2) | async-done | bytes 524320 | tf_op jit(solution)/shard_map/all_to_all | solution.py:523
  87.7 2.9 %collective-permute-start.10 = (f32[48,128]{1,0:T(8,128)S(1)}, f32[48,128]{1,0:T(8,128)S(1)}, u32[]{:S(2)}, u32[]{:S(2)}) collective-permute-start(f32[48,128]{1,0:T(8,128)S(1)} %add_parts.1.refs_0_), channel_id=1, source_target_pairs={{0,64},{32,96},{64,0},{96,32},{1,65},{33,97},{65,1},{97,33},{2,66}... | collective-permute-start | bytes 73736 | tf_op jit(solution)/shard_map/ppermute | solution.py:529
  94.0 5.3 %all-to-all-start.3 = ((bf16[32,48,128]{2,1,0:T(8,128)(2,1)}), bf16[32,48,128]{2,1,0:T(8,128)(2,1)S(1)}, u32[]{:S(2)}, u32[]{:S(2)}) async-start(bf16[32,48,128]{2,1,0:T(8,128)(2,1)} %add_groups.1), calls=%async_computation.3 | async-start | bytes 786432 | tf_op jit(solution)/shard_map/all_to_all | solution.py:535
  99.3 1.4 %add_back.1 = f32[1024,128]{1,0:T(8,128)} custom-call(s32[1,256]{1,0:T(1,128)S(1)} %copy-done.16, bf16[512,128]{1,0:T(8,128)(2,1)S(1)} %bitcast.11, bf16[32,64,128]{2,1,0:T(8,128)(2,1)S(1)} %all-to-all-done.2.got_ref, f32[1024,128]{1,0:T(8,128)S(1)} %get-tuple-element.60.local_ref), custom_call_target="tpu_custom_call" | custom-call | flops 1000000000 | bytes 1000000 | tf_op jit(solution)/shard_map/add_back/pallas_call | solution.py:380
  100.6 8.9 %all-to-all-done.3 = bf16[32,48,128]{2,1,0:T(8,128)(2,1)S(1)} async-done(((bf16[32,48,128]{2,1,0:T(8,128)(2,1)}), bf16[32,48,128]{2,1,0:T(8,128)(2,1)S(1)}, u32[]{:S(2)}, u32[]{:S(2)}) %all-to-all-start.3) | async-done | bytes 393248 | tf_op jit(solution)/shard_map/all_to_all | solution.py:535
  (67 shorter events, 17.7 us)
Async XLA Ops:
  2.4 16.3 %all-to-all-start = ((bf16[32,16,128]{2,1,0:T(8,128)(2,1)}), bf16[32,16,128]{2,1,0:T(8,128)(2,1)S(1)}, u32[]{:S(2)}, u32[]{:S(2)}) async-start(bf16[32,16,128]{2,1,0:T(8,128)(2,1)} %bitcast), calls=%async_computation | async-start | bytes 262144 | tf_op jit(solution)/shard_map/all_to_all | solution.py:427
  15.8 16.4 %copy-start.4 = (bf16[4096,128]{1,0:T(8,128)(2,1)S(1)}, bf16[4096,128]{1,0:T(8,128)(2,1)}, u32[]{:S(2)}) copy-start(bf16[4096,128]{1,0:T(8,128)(2,1)} %edges_ref.3) | copy-start | bytes 3145732
  15.8 16.4 %copy-start.8 = (bf16[384,128]{1,0:T(8,128)(2,1)S(1)}, bf16[384,128]{1,0:T(8,128)(2,1)}, u32[]{:S(2)}) copy-start(bf16[384,128]{1,0:T(8,128)(2,1)} %w1_ref.7) | copy-start | bytes 294916
  15.8 16.4 %copy-start.9 = (bf16[256,128]{1,0:T(8,128)(2,1)S(1)}, bf16[256,128]{1,0:T(8,128)(2,1)}, u32[]{:S(2)}) copy-start(bf16[256,128]{1,0:T(8,128)(2,1)} %v1_ref.3) | copy-start | bytes 196612
  15.9 16.4 %copy-start.10 = (bf16[128,128]{1,0:T(8,128)(2,1)S(1)}, bf16[128,128]{1,0:T(8,128)(2,1)}, u32[]{:S(2)}) copy-start(bf16[128,128]{1,0:T(8,128)(2,1)} %w2_ref.5) | copy-start | bytes 98308
  15.9 16.4 %copy-start.11 = (bf16[128,128]{1,0:T(8,128)(2,1)S(1)}, bf16[128,128]{1,0:T(8,128)(2,1)}, u32[]{:S(2)}) copy-start(bf16[128,128]{1,0:T(8,128)(2,1)} %v2_ref.3) | copy-start | bytes 98308
  15.9 16.4 %copy-start.12 = (s32[4096]{0:T(1024)S(1)}, s32[4096]{0:T(1024)}, u32[]{:S(2)}) copy-start(s32[4096]{0:T(1024)} %param.28) | copy-start | bytes 49156
  15.9 16.4 %copy-start.13 = (s32[4096]{0:T(1024)S(1)}, s32[4096]{0:T(1024)}, u32[]{:S(2)}) copy-start(s32[4096]{0:T(1024)} %param.29) | copy-start | bytes 49156
  19.9 12.3 %all-to-all-start.1 = ((bf16[32,16,128]{2,1,0:T(8,128)(2,1)}), bf16[32,16,128]{2,1,0:T(8,128)(2,1)S(1)}, u32[]{:S(2)}, u32[]{:S(2)}) async-start(bf16[32,16,128]{2,1,0:T(8,128)(2,1)} %bitcast.5), calls=%async_computation.1 | async-start | bytes 262144 | tf_op jit(solution)/shard_map/all_to_all | solution.py:449
  24.6 14.1 %collective-permute-start.2 = (s32[4,512]{1,0:T(4,128)S(1)}, s32[4,512]{1,0:T(4,128)S(1)}, u32[]{:S(2)}, u32[]{:S(2)}) collective-permute-start(s32[4,512]{1,0:T(4,128)S(1)} %bitcast.21), channel_id=1, source_target_pairs={{0,32},{32,64},{64,96},{96,0},{1,33},{33,65},{65,97},{97,1},{2,34}... | collective-permute-start | bytes 24584 | tf_op jit(solution)/shard_map/ppermute | solution.py:447
  26.3 12.4 %collective-permute-start.1 = (s32[4,512]{1,0:T(4,128)S(1)}, s32[4,512]{1,0:T(4,128)S(1)}, u32[]{:S(2)}, u32[]{:S(2)}) collective-permute-start(s32[4,512]{1,0:T(4,128)S(1)} %bitcast.22), channel_id=1, source_target_pairs={{0,64},{32,96},{64,0},{96,32},{1,65},{33,97},{65,1},{97,33},{2,66}... | collective-permute-start | bytes 24584 | tf_op jit(solution)/shard_map/ppermute | solution.py:447
  29.6 9.1 %collective-permute-start = (s32[4,512]{1,0:T(4,128)S(1)}, s32[4,512]{1,0:T(4,128)S(1)}, u32[]{:S(2)}, u32[]{:S(2)}) collective-permute-start(s32[4,512]{1,0:T(4,128)S(1)} %bitcast.23), channel_id=1, source_target_pairs={{0,96},{32,0},{64,32},{96,64},{1,97},{33,1},{65,33},{97,65},{2,98}... | collective-permute-start | bytes 24584 | tf_op jit(solution)/shard_map/ppermute | solution.py:447
  38.8 21.4 %copy-start.5 = (bf16[4096,128]{1,0:T(8,128)(2,1)S(1)}, bf16[4096,128]{1,0:T(8,128)(2,1)}, u32[]{:S(2)}) copy-start(bf16[4096,128]{1,0:T(8,128)(2,1)} %cot_ref.5) | copy-start | bytes 3145732
  40.7 7.4 %collective-permute-start.3 = (bf16[512,128]{1,0:T(8,128)(2,1)S(1)}, bf16[512,128]{1,0:T(8,128)(2,1)S(1)}, u32[]{:S(2)}, u32[]{:S(2)}) collective-permute-start(bf16[512,128]{1,0:T(8,128)(2,1)S(1)} %get-tuple-element.49), channel_id=1, source_target_pairs={{0,32},{32,64},{64,96},{96,0},{1,33},{33,65},{65,97},{97,1},{2,34}... | collective-permute-start | bytes 393224 | tf_op jit(solution)/shard_map/ppermute | solution.py:473
  42.4 9.3 %collective-permute-start.4 = (bf16[512,128]{1,0:T(8,128)(2,1)S(1)}, bf16[512,128]{1,0:T(8,128)(2,1)S(1)}, u32[]{:S(2)}, u32[]{:S(2)}) collective-permute-start(bf16[512,128]{1,0:T(8,128)(2,1)S(1)} %get-tuple-element.50), channel_id=1, source_target_pairs={{0,64},{32,96},{64,0},{96,32},{1,65},{33,97},{65,1},{97,33},{2,66}... | collective-permute-start | bytes 393224 | tf_op jit(solution)/shard_map/ppermute | solution.py:473
  45.7 6.0 %collective-permute-start.5 = (bf16[512,128]{1,0:T(8,128)(2,1)S(1)}, bf16[512,128]{1,0:T(8,128)(2,1)S(1)}, u32[]{:S(2)}, u32[]{:S(2)}) collective-permute-start(bf16[512,128]{1,0:T(8,128)(2,1)S(1)} %get-tuple-element.51), channel_id=1, source_target_pairs={{0,96},{32,0},{64,32},{96,64},{1,97},{33,1},{65,33},{97,65},{2,98}... | collective-permute-start | bytes 393224 | tf_op jit(solution)/shard_map/ppermute | solution.py:473
  53.0 4.3 %collective-permute-start.8 = (bf16[256,128]{1,0:T(8,128)(2,1)S(1)}, bf16[256,128]{1,0:T(8,128)(2,1)S(1)}, u32[]{:S(2)}, u32[]{:S(2)}) collective-permute-start(bf16[256,128]{1,0:T(8,128)(2,1)S(1)} %get-tuple-element.54.rest_0_), channel_id=1, source_target_pairs={{0,32},{32,64},{64,96},{96,0},{1,33},{33,65},{65,97},{97,1},{2,34}... | collective-permute-start | bytes 196616 | tf_op jit(solution)/shard_map/ppermute | solution.py:483
  54.3 4.9 %collective-permute-start.7 = (bf16[256,128]{1,0:T(8,128)(2,1)S(1)}, bf16[256,128]{1,0:T(8,128)(2,1)S(1)}, u32[]{:S(2)}, u32[]{:S(2)}) collective-permute-start(bf16[256,128]{1,0:T(8,128)(2,1)S(1)} %get-tuple-element.54.rest_0_), channel_id=1, source_target_pairs={{0,64},{32,96},{64,0},{96,32},{1,65},{33,97},{65,1},{97,33},{2,66}... | collective-permute-start | bytes 196616 | tf_op jit(solution)/shard_map/ppermute | solution.py:483
  56.4 3.8 %collective-permute-start.6 = (bf16[256,128]{1,0:T(8,128)(2,1)S(1)}, bf16[256,128]{1,0:T(8,128)(2,1)S(1)}, u32[]{:S(2)}, u32[]{:S(2)}) collective-permute-start(bf16[256,128]{1,0:T(8,128)(2,1)S(1)} %get-tuple-element.54.rest_0_), channel_id=1, source_target_pairs={{0,96},{32,0},{64,32},{96,64},{1,97},{33,1},{65,33},{97,65},{2,98}... | collective-permute-start | bytes 196616 | tf_op jit(solution)/shard_map/ppermute | solution.py:483
  69.8 17.5 %all-to-all-start.2 = ((bf16[32,64,128]{2,1,0:T(8,128)(2,1)}), bf16[32,64,128]{2,1,0:T(8,128)(2,1)S(1)}, u32[]{:S(2)}, u32[]{:S(2)}) async-start(bf16[32,64,128]{2,1,0:T(8,128)(2,1)} %get-tuple-element.55), calls=%async_computation.2 | async-start | bytes 1048576 | tf_op jit(solution)/shard_map/all_to_all | solution.py:523
  87.4 4.0 %collective-permute-start.11 = (f32[48,128]{1,0:T(8,128)S(1)}, f32[48,128]{1,0:T(8,128)S(1)}, u32[]{:S(2)}, u32[]{:S(2)}) collective-permute-start(f32[48,128]{1,0:T(8,128)S(1)} %add_parts.1.refs_0_), channel_id=1, source_target_pairs={{0,32},{32,64},{64,96},{96,0},{1,33},{33,65},{65,97},{97,1},{2,34}... | collective-permute-start | bytes 73736 | tf_op jit(solution)/shard_map/ppermute | solution.py:529
  87.7 4.6 %collective-permute-start.10 = (f32[48,128]{1,0:T(8,128)S(1)}, f32[48,128]{1,0:T(8,128)S(1)}, u32[]{:S(2)}, u32[]{:S(2)}) collective-permute-start(f32[48,128]{1,0:T(8,128)S(1)} %add_parts.1.refs_0_), channel_id=1, source_target_pairs={{0,64},{32,96},{64,0},{96,32},{1,65},{33,97},{65,1},{97,33},{2,66}... | collective-permute-start | bytes 73736 | tf_op jit(solution)/shard_map/ppermute | solution.py:529
  90.5 2.7 %collective-permute-start.9 = (f32[48,128]{1,0:T(8,128)S(1)}, f32[48,128]{1,0:T(8,128)S(1)}, u32[]{:S(2)}, u32[]{:S(2)}) collective-permute-start(f32[48,128]{1,0:T(8,128)S(1)} %add_parts.1.refs_0_), channel_id=1, source_target_pairs={{0,96},{32,0},{64,32},{96,64},{1,97},{33,1},{65,33},{97,65},{2,98}... | collective-permute-start | bytes 73736 | tf_op jit(solution)/shard_map/ppermute | solution.py:529
  94.0 15.6 %all-to-all-start.3 = ((bf16[32,48,128]{2,1,0:T(8,128)(2,1)}), bf16[32,48,128]{2,1,0:T(8,128)(2,1)S(1)}, u32[]{:S(2)}, u32[]{:S(2)}) async-start(bf16[32,48,128]{2,1,0:T(8,128)(2,1)} %add_groups.1), calls=%async_computation.3 | async-start | bytes 786432 | tf_op jit(solution)/shard_map/all_to_all | solution.py:535
  (15 other events, 96.6 us)

commit v5 on v4

--- a/solution.py
+++ b/solution.py
@@ -230,8 +230,33 @@
     back_ref[...] = (grad_in[:, LANES:] * POOL_SHARE).astype(BF)
 
 
+def slopes_kernel(
+    pre_ref, w2_ref, nodes_ref, summed_ref, v1_ref, v2_ref,
+    slope_ref, hidden_ref, normed_ref, std_ref,
+    node_slope_ref, node_hidden_ref, node_normed_ref, node_std_ref,
+):
+    def fill(pre, weights, out_refs, here):
+        sig = sigmoid(pre)
+        hidden = (pre * sig).astype(BF)
+        normed, inv_std = norm_parts(nn(hidden, weights))
+        parts = (slope(pre, sig), hidden, normed, jnp.broadcast_to(inv_std, normed.shape))
+        for out_ref, part in zip(out_refs, parts):
+            out_ref[here, :] = part
+
+    for part in range(0, pre_ref.shape[0], SECOND_SUB):
+        here = slice(part, part + SECOND_SUB)
+        fill(pre_ref[here, :], w2_ref[...], (slope_ref, hidden_ref, normed_ref, std_ref), here)
+    joined = jnp.concatenate([nodes_ref[...], summed_ref[...]], axis=1)
+    fill(
+        nn(joined, v1_ref[...]), v2_ref[...],
+        (node_slope_ref, node_hidden_ref, node_normed_ref, node_std_ref),
+        slice(0, nodes_ref.shape[0]),
+    )
+
+
 def edge_back_kernel(
-    source_ref, target_ref, pre_ref, src_ref, tgt_ref, edges_ref, cot_ref, w1_ref, w2_ref,
+    node_slope_ref, node_hidden_ref, node_normed_ref, node_std_ref,
+    source_ref, target_ref, slope_ref, hidden_ref, normed_ref, std_ref, src_ref, tgt_ref, edges_ref, cot_ref, w1_ref, w2_ref,
     goal_ref, node_cot_ref, nodes_ref, summed_ref, v1_ref, v2_ref, c1_ref, c2_ref, *rest,
 ):
     gp_refs = rest[:-10]
@@ -248,35 +273,26 @@
         from_coarse = pick_rows(spread_column(goal_ref[...]), table)
         updated_grad = node_cot_ref[...].astype(F32) + from_coarse
         joined = jnp.concatenate([nodes_ref[...], summed_ref[...]], axis=1)
-        pre = nn(joined, v1_ref[...])
-        sig = sigmoid(pre)
-        hidden = (pre * sig).astype(BF)
-        normed, inv_std = norm_parts(nn(hidden, v2_ref[...]))
-        grad_norm = norm_back(normed, inv_std, updated_grad).astype(BF)
-        gv2[...] = tn(hidden, grad_norm)
-        grad_pre = (nt(grad_norm, v2_ref[...]) * slope(pre, sig)).astype(BF)
+        grad_norm = norm_back(node_normed_ref[...], node_std_ref[...], updated_grad).astype(BF)
+        gv2[...] = tn(node_hidden_ref[...], grad_norm)
+        grad_pre = (nt(grad_norm, v2_ref[...]) * node_slope_ref[...]).astype(BF)
         gv1[...] = tn(joined, grad_pre)
         grad_in = nt(grad_pre, v1_ref[...])
         local_ref[...] = updated_grad + grad_in[:, :LANES]
         wide[...] = halves(grad_in[:, LANES:].astype(BF))
 
     target = spread_column(target_ref[...])
-    hiddens, grad_norms, grad_pres = [], [], []
+    grad_norms, grad_pres = [], []
     for part in range(0, target.shape[0], BACK_SUB):
         here = slice(part, part + BACK_SUB)
         message_grad = cot_ref[here, :].astype(F32) + pick_rows(target[here], wide[...])
-        pre = pre_ref[here, :]
-        sig = sigmoid(pre)
-        hidden = (pre * sig).astype(BF)
-        normed, inv_std = norm_parts(nn(hidden, w2_ref[...]))
-        grad_norm = norm_back(normed, inv_std, message_grad).astype(BF)
-        grad_pre = (nt(grad_norm, w2_ref[...]) * slope(pre, sig)).astype(BF)
-        hiddens.append(hidden)
+        grad_norm = norm_back(normed_ref[here, :], std_ref[here, :], message_grad).astype(BF)
+        grad_pre = (nt(grad_norm, w2_ref[...]) * slope_ref[here, :]).astype(BF)
         grad_norms.append(grad_norm)
         grad_pres.append(grad_pre)
     grad_pre = jnp.concatenate(grad_pres, axis=0)
     grad_pre_ref[...] = grad_pre
-    gw2[...] += tn(jnp.concatenate(hiddens, axis=0), jnp.concatenate(grad_norms, axis=0))
+    gw2[...] += tn(hidden_ref[...], jnp.concatenate(grad_norms, axis=0))
     stacked = jnp.concatenate([src_ref[...], tgt_ref[0], edges_ref[...]], axis=1)
     gw1[...] += tn(stacked, grad_pre)
     source = source_ref[...] - rows
@@ -469,9 +485,16 @@
         + [pl.BlockSpec(memory_space=pltpu.VMEM)] * (3 + groups),
         flops=10**9, bytes_accessed=10**6, name="pool", vmem=16,
     )
+    slopes = call(
+        slopes_kernel,
+        [shape((size, latent), kind) for size in (edges, rows) for kind in (F32, BF, F32, F32)],
+        pre, edge_w_two, node_features, summed, node_w_one, node_w_two,
+        flops=10**9, bytes_accessed=10**7, name="slopes",
+    )
     got = [send[0]] + [
         lax.ppermute(send[ahead], "group", turned(-ahead)) for ahead in range(1, groups)
     ]
+    got, slopes = lax.optimization_barrier((got, slopes))
     grad_coarse, coarse_back, grad_c_one, grad_c_two = call(
         coarse_kernel,
         [shape((coarse, latent), F32), shape((coarse, latent), BF),
@@ -489,11 +512,12 @@
     grad_pre, node_local, joint = call(
         edge_back_kernel,
         [shape((edges, latent), BF), shape((rows, latent), F32), shape(joint_shape, BF)],
-        source, target, pre, src_rows, own_rows, edge_features, edge_cotangent, edge_w_one, edge_w_two,
+        *slopes[4:], source, target, *slopes[:4], src_rows, own_rows, edge_features, edge_cotangent, edge_w_one, edge_w_two,
         goal, node_cotangent, node_features, summed, node_w_one, node_w_two,
         grad_c_one, grad_c_two, *returned,
         grid=grid,
-        in_specs=[index_spec, index_spec, edge_spec, edge_spec,
+        in_specs=[whole((rows, latent))] * 4
+        + [index_spec, index_spec] + [edge_spec] * 5 + [
                   pl.BlockSpec((1, edges, latent), lambda i: (1, 0, 0)), edge_spec, edge_spec,
                   whole((3 * latent, latent)), whole((latent, latent)),
                   whole((1, rows)),

time: 111 us -> 112 us (level)
  waiting for transfers between devices: 29.5 us -> 26.3 us
  Pallas kernels: 30.6 us -> 33.4 us
  local copies, waits for them, and re-layouts: 6.48 us -> 7.82 us
    ppermute x3, waiting for transfers between devices: 5.32 us -> 2.1 us  [local(): lax.ppermute(send[ahead], 'group', turned(-ahead))]
    pallas_call x12 -> x13, Pallas kernels: 30.6 us -> 33.4 us  [call(): pl.pallas_call(kernel, out_shape=out_shapes if single else list(out_shape...]
    unnamed x47 -> x49, local copies, waits for them, and re-layouts: 6.48 us -> 7.82 us
  transfers between devices with their start and end apart: 16 -> 16, of which waited for: 12 -> 11; matrix products, arithmetic and copies ran while one was open for 0% -> 0% of each run, Pallas kernels for 14% -> 16%
where the time goes in v5:
time: 112 us; the launch traced here: 111 us
  starting transfers between devices  43 us (38%)
  Pallas kernels  33.4 us (30%)
  waiting for transfers between devices  26.3 us (23%)
  local copies, waits for them, and re-layouts  7.82 us (7%)
    pallas_call x13, Pallas kernels, call(): pl.pallas_call(kernel, out_shape=out_shapes if single else list(out_shape...  33.4 us
    all_to_all x1, waiting for transfers between devices, local(): pack_all = exchange(pack_sum, 'dom').reshape(pack_rows, latent)  8.96 us
    all_to_all x1, starting transfers between devices, local(): exchange(spread.reshape(domains, slots, latent), 'dom')  8.59 us
    unnamed x49, local copies, waits for them, and re-layouts  7.82 us
    all_to_all x1, starting transfers between devices, local(): exchange(joint, 'dom')  5.86 us
    ppermute x3, starting transfers between devices, local(): lax.ppermute(send[ahead], 'group', turned(-ahead))  5.74 us
    ppermute x3, starting transfers between devices, local(): lax.ppermute(slot_list, 'group', turned(ahead))  5.74 us
    all_to_all x1, starting transfers between devices, local(): pack_all = exchange(pack_sum, 'dom').reshape(pack_rows, latent)  5.28 us
  transfers between devices with their start and end apart: 16, of which 11 were waited for; matrix products, arithmetic and copies ran while one was open for 0% of the time, Pallas kernels for 16%

profile of v5, /device:TPU:1, one launch (start us, length us, event | category | flops | bytes accessed | tf_op | source)
XLA Modules:
  0.0 111.4 jit_solution(9952681263110418091)
XLA Ops:
  2.4 8.6 %all-to-all-start = ((bf16[32,16,128]{2,1,0:T(8,128)(2,1)}), bf16[32,16,128]{2,1,0:T(8,128)(2,1)S(1)}, u32[]{:S(2)}, u32[]{:S(2)}) async-start(bf16[32,16,128]{2,1,0:T(8,128)(2,1)} %bitcast), calls=%async_computation | async-start | bytes 262144 | tf_op jit(solution)/shard_map/all_to_all | solution.py:443
  11.0 4.8 %edge_first.1.own_ref.tgt_ref = bf16[2,4096,128]{2,1,0:T(8,128)(2,1)} custom-call(s32[1,4096]{1,0:T(1,128)} %bitcast.13, s32[1,4096]{1,0:T(1,128)} %bitcast.17, bf16[1024,128]{1,0:T(8,128)(2,1)} %nodes_ref.9), custom_call_target="tpu_custom_call" | custom-call | flops 4000000000 | bytes 3000000 | tf_op jit(solution)/shard_map/edge_first/pallas_call | solution.py:396
  15.9 2.8 %all-to-all-done = bf16[32,16,128]{2,1,0:T(8,128)(2,1)S(1)} async-done(((bf16[32,16,128]{2,1,0:T(8,128)(2,1)}), bf16[32,16,128]{2,1,0:T(8,128)(2,1)S(1)}, u32[]{:S(2)}, u32[]{:S(2)}) %all-to-all-start) | async-done | bytes 131104 | tf_op jit(solution)/shard_map/all_to_all | solution.py:443
  19.9 4.6 %all-to-all-start.1 = ((bf16[32,16,128]{2,1,0:T(8,128)(2,1)}), bf16[32,16,128]{2,1,0:T(8,128)(2,1)S(1)}, u32[]{:S(2)}, u32[]{:S(2)}) async-start(bf16[32,16,128]{2,1,0:T(8,128)(2,1)} %bitcast.6), calls=%async_computation.1 | async-start | bytes 262144 | tf_op jit(solution)/shard_map/all_to_all | solution.py:465
  24.6 1.7 %collective-permute-start.2 = (s32[4,512]{1,0:T(4,128)S(1)}, s32[4,512]{1,0:T(4,128)S(1)}, u32[]{:S(2)}, u32[]{:S(2)}) collective-permute-start(s32[4,512]{1,0:T(4,128)S(1)} %bitcast.21), channel_id=1, source_target_pairs={{0,32},{32,64},{64,96},{96,0},{1,33},{33,65},{65,97},{97,1},{2,34}... | collective-permute-start | bytes 24584 | tf_op jit(solution)/shard_map/ppermute | solution.py:463
  26.3 3.3 %collective-permute-start.1 = (s32[4,512]{1,0:T(4,128)S(1)}, s32[4,512]{1,0:T(4,128)S(1)}, u32[]{:S(2)}, u32[]{:S(2)}) collective-permute-start(s32[4,512]{1,0:T(4,128)S(1)} %bitcast.22), channel_id=1, source_target_pairs={{0,64},{32,96},{64,0},{96,32},{1,65},{33,97},{65,1},{97,33},{2,66}... | collective-permute-start | bytes 24584 | tf_op jit(solution)/shard_map/ppermute | solution.py:463
  30.3 1.9 %all-to-all-done.1 = bf16[32,16,128]{2,1,0:T(8,128)(2,1)S(1)} async-done(((bf16[32,16,128]{2,1,0:T(8,128)(2,1)}), bf16[32,16,128]{2,1,0:T(8,128)(2,1)S(1)}, u32[]{:S(2)}, u32[]{:S(2)}) %all-to-all-start.1) | async-done | bytes 131104 | tf_op jit(solution)/shard_map/all_to_all | solution.py:465
  32.3 1.6 %copy-done.19 = bf16[2,4096,128]{2,1,0:T(8,128)(2,1)S(1)} copy-done((bf16[2,4096,128]{2,1,0:T(8,128)(2,1)S(1)}, bf16[2,4096,128]{2,1,0:T(8,128)(2,1)}, u32[]{:S(2)}) %copy-start.19) | copy-done | bytes 2097176
  33.9 4.8 %edge_second.1 = (f32[4096,128]{1,0:T(8,128)S(1)}, bf16[4096,128]{1,0:T(8,128)(2,1)S(1)}, bf16[1024,128]{1,0:T(8,128)(2,1)S(1)}, bf16[1024,128]{1,0:T(8,128)(2,1)S(1)}) custom-call(s32[1,4096]{1,0:T(1,128)S(1)} %bitcast.14, s32[1,4096]{1,0:T(1,128)S(1)} %bitcast.18, bf16[2,4096,128]{2,1,0:T(8,128)(2,1)S(1)} %copy-done.19, bf16[4096,128]{1,0:T(8,128)(2,1)S(1)} %copy-done.4, ...), custom_call_target="tpu_custom_call" | custom-call | flops 5000000000 | bytes 8000000 | tf_op jit(solution)/shard_map/edge_second/pallas_call | solution.py:396
  38.7 1.9 %pool.1 = (s32[1,1024]{1,0:T(1,128)S(1)}, bf16[512,128]{1,0:T(8,128)(2,1)S(1)}, bf16[512,128]{1,0:T(8,128)(2,1)S(1)}, bf16[512,128]{1,0:T(8,128)(2,1)S(1)}, bf16[512,128]{1,0:T(8,128)(2,1)S(1)}) custom-call(s32[1,1]{1,0:T(1,128)} %bitcast.4.group_ref, s32[1,4]{1,0:T(1,128)S(1)} %copy-done.17, s32[1,1024]{1,0:T(1,128)S(1)} %copy-done.15, ...), custom_call_target="tpu_custom_call" | custom-call | flops 1000000000 | bytes 1000000 | tf_op jit(solution)/shard_map/pool/pallas_call | solution.py:396
  40.7 1.7 %collective-permute-start.3 = (bf16[512,128]{1,0:T(8,128)(2,1)S(1)}, bf16[512,128]{1,0:T(8,128)(2,1)S(1)}, u32[]{:S(2)}, u32[]{:S(2)}) collective-permute-start(bf16[512,128]{1,0:T(8,128)(2,1)S(1)} %get-tuple-element.65), channel_id=1, source_target_pairs={{0,32},{32,64},{64,96},{96,0},{1,33},{33,65},{65,97},{97,1},{2,34}... | collective-permute-start | bytes 393224 | tf_op jit(solution)/shard_map/ppermute | solution.py:495
  42.4 3.3 %collective-permute-start.4 = (bf16[512,128]{1,0:T(8,128)(2,1)S(1)}, bf16[512,128]{1,0:T(8,128)(2,1)S(1)}, u32[]{:S(2)}, u32[]{:S(2)}) collective-permute-start(bf16[512,128]{1,0:T(8,128)(2,1)S(1)} %get-tuple-element.66), channel_id=1, source_target_pairs={{0,64},{32,96},{64,0},{96,32},{1,65},{33,97},{65,1},{97,33},{2,66}... | collective-permute-start | bytes 393224 | tf_op jit(solution)/shard_map/ppermute | solution.py:495
  46.5 1.8 %slopes.1 = (f32[4096,128]{1,0:T(8,128)S(1)}, bf16[4096,128]{1,0:T(8,128)(2,1)S(1)}, f32[4096,128]{1,0:T(8,128)S(1)}, f32[4096,128]{1,0:T(8,128)S(1)}, f32[1024,...) custom-call(f32[4096,128]{1,0:T(8,128)S(1)} %get-tuple-element.68.pre_ref, ...), custom_call_target="tpu_custom_call" | custom-call | flops 1000000000 | bytes 10000000 | tf_op jit(solution)/shard_map/slopes/pallas_call | solution.py:396
  49.7 2.1 %collective-permute-done.4.refs_2_ = bf16[512,128]{1,0:T(8,128)(2,1)S(1)} collective-permute-done((bf16[512,128]{1,0:T(8,128)(2,1)S(1)}, bf16[512,128]{1,0:T(8,128)(2,1)S(1)}, u32[]{:S(2)}, u32[]{:S(2)}) %collective-permute-start.4) | collective-permute-done | bytes 131104 | tf_op jit(solution)/shard_map/ppermute | solution.py:495
  54.4 2.0 %collective-permute-start.7 = (bf16[256,128]{1,0:T(8,128)(2,1)S(1)}, bf16[256,128]{1,0:T(8,128)(2,1)S(1)}, u32[]{:S(2)}, u32[]{:S(2)}) collective-permute-start(bf16[256,128]{1,0:T(8,128)(2,1)S(1)} %get-tuple-element.94.rest_0_), channel_id=1, source_target_pairs={{0,64},{32,96},{64,0},{96,32},{1,65},{33,97},{65,1},{97,33},{2,66}... | collective-permute-start | bytes 196616 | tf_op jit(solution)/shard_map/ppermute | solution.py:506
  57.4 1.9 %collective-permute-done.7.rest_2_ = bf16[256,128]{1,0:T(8,128)(2,1)S(1)} collective-permute-done((bf16[256,128]{1,0:T(8,128)(2,1)S(1)}, bf16[256,128]{1,0:T(8,128)(2,1)S(1)}, u32[]{:S(2)}, u32[]{:S(2)}) %collective-permute-start.7) | collective-permute-done | bytes 65568 | tf_op jit(solution)/shard_map/ppermute | solution.py:506
  60.2 8.8 %edge_back.1 = (bf16[4096,128]{1,0:T(8,128)(2,1)S(1)}, f32[1024,128]{1,0:T(8,128)S(1)}, bf16[32,64,128]{2,1,0:T(8,128)(2,1)}) custom-call(f32[1024,128]{1,0:T(8,128)S(1)} %get-tuple-element.78.node_slope_ref, bf16[1024,128]{1,0:T(8,128)(2,1)S(1)} %get-tuple-element.79.node_hidden_ref, f32[1024,128]{1,0:T(8,128)S(1)} %get-tuple-element.80.node_normed_ref, ...), custom_call_target="tpu_custom_call" | custom-call | flops 6000000000 | bytes 10000000 | tf_op jit(solution)/shard_map/edge_back/pallas_call | solution.py:396
  70.8 5.9 %all-to-all-start.2 = ((bf16[32,64,128]{2,1,0:T(8,128)(2,1)}), bf16[32,64,128]{2,1,0:T(8,128)(2,1)S(1)}, u32[]{:S(2)}, u32[]{:S(2)}) async-start(bf16[32,64,128]{2,1,0:T(8,128)(2,1)} %get-tuple-element.95), calls=%async_computation.2 | async-start | bytes 1048576 | tf_op jit(solution)/shard_map/all_to_all | solution.py:547
  78.9 4.7 %own_back.1 = (f32[1024,128]{1,0:T(8,128)S(1)}, f32[4096,128]{1,0:T(8,128)}) custom-call(s32[1,4096]{1,0:T(1,128)S(1)} %bitcast.16, s32[1,4096]{1,0:T(1,128)S(1)} %bitcast.20, bf16[4096,128]{1,0:T(8,128)(2,1)S(1)} %copy-done.21, bf16[4096,128]{1,0:T(8,128)(2,1)S(1)} %copy-done.5, f32[1024,128]{1,0:T(8,128)S(1)} %copy-done.23, bf16[384,128]{1,0:T(8,128)(2,1)S(1)} %copy-done.8), custom_call_target="tpu_custom_call" | custom-call | flops 4000000000 | bytes 5000000 | tf_op jit(solution)/shard_map/own_back/pallas_call | solution.py:396
  83.7 4.6 %all-to-all-done.2.got_ref = bf16[32,64,128]{2,1,0:T(8,128)(2,1)S(1)} async-done(((bf16[32,64,128]{2,1,0:T(8,128)(2,1)}), bf16[32,64,128]{2,1,0:T(8,128)(2,1)S(1)}, u32[]{:S(2)}, u32[]{:S(2)}) %all-to-all-start.2) | async-done | bytes 524320 | tf_op jit(solution)/shard_map/all_to_all | solution.py:547
  88.7 2.9 %collective-permute-start.10 = (f32[48,128]{1,0:T(8,128)S(1)}, f32[48,128]{1,0:T(8,128)S(1)}, u32[]{:S(2)}, u32[]{:S(2)}) collective-permute-start(f32[48,128]{1,0:T(8,128)S(1)} %add_parts.1.refs_0_), channel_id=1, source_target_pairs={{0,64},{32,96},{64,0},{96,32},{1,65},{33,97},{65,1},{97,33},{2,66}... | collective-permute-start | bytes 73736 | tf_op jit(solution)/shard_map/ppermute | solution.py:553
  95.0 5.3 %all-to-all-start.3 = ((bf16[32,48,128]{2,1,0:T(8,128)(2,1)}), bf16[32,48,128]{2,1,0:T(8,128)(2,1)S(1)}, u32[]{:S(2)}, u32[]{:S(2)}) async-start(bf16[32,48,128]{2,1,0:T(8,128)(2,1)} %add_groups.1), calls=%async_computation.3 | async-start | bytes 786432 | tf_op jit(solution)/shard_map/all_to_all | solution.py:559
  100.3 1.3 %add_back.1 = f32[1024,128]{1,0:T(8,128)} custom-call(s32[1,256]{1,0:T(1,128)S(1)} %copy-done.16, bf16[512,128]{1,0:T(8,128)(2,1)S(1)} %bitcast.11, bf16[32,64,128]{2,1,0:T(8,128)(2,1)S(1)} %all-to-all-done.2.got_ref, f32[1024,128]{1,0:T(8,128)S(1)} %get-tuple-element.100.local_ref), custom_call_target="tpu_custom_call" | custom-call | flops 1000000000 | bytes 1000000 | tf_op jit(solution)/shard_map/add_back/pallas_call | solution.py:396
  101.6 9.0 %all-to-all-done.3 = bf16[32,48,128]{2,1,0:T(8,128)(2,1)S(1)} async-done(((bf16[32,48,128]{2,1,0:T(8,128)(2,1)}), bf16[32,48,128]{2,1,0:T(8,128)(2,1)S(1)}, u32[]{:S(2)}, u32[]{:S(2)}) %all-to-all-start.3) | async-done | bytes 393248 | tf_op jit(solution)/shard_map/all_to_all | solution.py:559
  (70 shorter events, 19.0 us)
Async XLA Ops:
  2.4 16.3 %all-to-all-start = ((bf16[32,16,128]{2,1,0:T(8,128)(2,1)}), bf16[32,16,128]{2,1,0:T(8,128)(2,1)S(1)}, u32[]{:S(2)}, u32[]{:S(2)}) async-start(bf16[32,16,128]{2,1,0:T(8,128)(2,1)} %bitcast), calls=%async_computation | async-start | bytes 262144 | tf_op jit(solution)/shard_map/all_to_all | solution.py:443
  15.8 16.4 %copy-start.4 = (bf16[4096,128]{1,0:T(8,128)(2,1)S(1)}, bf16[4096,128]{1,0:T(8,128)(2,1)}, u32[]{:S(2)}) copy-start(bf16[4096,128]{1,0:T(8,128)(2,1)} %edges_ref.3) | copy-start | bytes 3145732
  15.8 16.4 %copy-start.8 = (bf16[384,128]{1,0:T(8,128)(2,1)S(1)}, bf16[384,128]{1,0:T(8,128)(2,1)}, u32[]{:S(2)}) copy-start(bf16[384,128]{1,0:T(8,128)(2,1)} %w1_ref.7) | copy-start | bytes 294916
  15.9 16.4 %copy-start.9 = (bf16[256,128]{1,0:T(8,128)(2,1)S(1)}, bf16[256,128]{1,0:T(8,128)(2,1)}, u32[]{:S(2)}) copy-start(bf16[256,128]{1,0:T(8,128)(2,1)} %v1_ref.5) | copy-start | bytes 196612
  15.9 16.4 %copy-start.10 = (bf16[128,128]{1,0:T(8,128)(2,1)S(1)}, bf16[128,128]{1,0:T(8,128)(2,1)}, u32[]{:S(2)}) copy-start(bf16[128,128]{1,0:T(8,128)(2,1)} %w2_ref.7) | copy-start | bytes 98308
  15.9 16.4 %copy-start.11 = (bf16[128,128]{1,0:T(8,128)(2,1)S(1)}, bf16[128,128]{1,0:T(8,128)(2,1)}, u32[]{:S(2)}) copy-start(bf16[128,128]{1,0:T(8,128)(2,1)} %v2_ref.5) | copy-start | bytes 98308
  15.9 16.4 %copy-start.12 = (s32[4096]{0:T(1024)S(1)}, s32[4096]{0:T(1024)}, u32[]{:S(2)}) copy-start(s32[4096]{0:T(1024)} %param.28) | copy-start | bytes 49156
  15.9 16.4 %copy-start.13 = (s32[4096]{0:T(1024)S(1)}, s32[4096]{0:T(1024)}, u32[]{:S(2)}) copy-start(s32[4096]{0:T(1024)} %param.29) | copy-start | bytes 49156
  19.9 12.3 %all-to-all-start.1 = ((bf16[32,16,128]{2,1,0:T(8,128)(2,1)}), bf16[32,16,128]{2,1,0:T(8,128)(2,1)S(1)}, u32[]{:S(2)}, u32[]{:S(2)}) async-start(bf16[32,16,128]{2,1,0:T(8,128)(2,1)} %bitcast.6), calls=%async_computation.1 | async-start | bytes 262144 | tf_op jit(solution)/shard_map/all_to_all | solution.py:465
  24.6 14.1 %collective-permute-start.2 = (s32[4,512]{1,0:T(4,128)S(1)}, s32[4,512]{1,0:T(4,128)S(1)}, u32[]{:S(2)}, u32[]{:S(2)}) collective-permute-start(s32[4,512]{1,0:T(4,128)S(1)} %bitcast.21), channel_id=1, source_target_pairs={{0,32},{32,64},{64,96},{96,0},{1,33},{33,65},{65,97},{97,1},{2,34}... | collective-permute-start | bytes 24584 | tf_op jit(solution)/shard_map/ppermute | solution.py:463
  26.3 12.4 %collective-permute-start.1 = (s32[4,512]{1,0:T(4,128)S(1)}, s32[4,512]{1,0:T(4,128)S(1)}, u32[]{:S(2)}, u32[]{:S(2)}) collective-permute-start(s32[4,512]{1,0:T(4,128)S(1)} %bitcast.22), channel_id=1, source_target_pairs={{0,64},{32,96},{64,0},{96,32},{1,65},{33,97},{65,1},{97,33},{2,66}... | collective-permute-start | bytes 24584 | tf_op jit(solution)/shard_map/ppermute | solution.py:463
  29.6 9.1 %collective-permute-start = (s32[4,512]{1,0:T(4,128)S(1)}, s32[4,512]{1,0:T(4,128)S(1)}, u32[]{:S(2)}, u32[]{:S(2)}) collective-permute-start(s32[4,512]{1,0:T(4,128)S(1)} %bitcast.23), channel_id=1, source_target_pairs={{0,96},{32,0},{64,32},{96,64},{1,97},{33,1},{65,33},{97,65},{2,98}... | collective-permute-start | bytes 24584 | tf_op jit(solution)/shard_map/ppermute | solution.py:463
  40.7 8.9 %collective-permute-start.3 = (bf16[512,128]{1,0:T(8,128)(2,1)S(1)}, bf16[512,128]{1,0:T(8,128)(2,1)S(1)}, u32[]{:S(2)}, u32[]{:S(2)}) collective-permute-start(bf16[512,128]{1,0:T(8,128)(2,1)S(1)} %get-tuple-element.65), channel_id=1, source_target_pairs={{0,32},{32,64},{64,96},{96,0},{1,33},{33,65},{65,97},{97,1},{2,34}... | collective-permute-start | bytes 393224 | tf_op jit(solution)/shard_map/ppermute | solution.py:495
  42.4 9.3 %collective-permute-start.4 = (bf16[512,128]{1,0:T(8,128)(2,1)S(1)}, bf16[512,128]{1,0:T(8,128)(2,1)S(1)}, u32[]{:S(2)}, u32[]{:S(2)}) collective-permute-start(bf16[512,128]{1,0:T(8,128)(2,1)S(1)} %get-tuple-element.66), channel_id=1, source_target_pairs={{0,64},{32,96},{64,0},{96,32},{1,65},{33,97},{65,1},{97,33},{2,66}... | collective-permute-start | bytes 393224 | tf_op jit(solution)/shard_map/ppermute | solution.py:495
  45.7 6.0 %collective-permute-start.5 = (bf16[512,128]{1,0:T(8,128)(2,1)S(1)}, bf16[512,128]{1,0:T(8,128)(2,1)S(1)}, u32[]{:S(2)}, u32[]{:S(2)}) collective-permute-start(bf16[512,128]{1,0:T(8,128)(2,1)S(1)} %get-tuple-element.67), channel_id=1, source_target_pairs={{0,96},{32,0},{64,32},{96,64},{1,97},{33,1},{65,33},{97,65},{2,98}... | collective-permute-start | bytes 393224 | tf_op jit(solution)/shard_map/ppermute | solution.py:495
  46.5 13.8 %copy-start.5 = (bf16[4096,128]{1,0:T(8,128)(2,1)S(1)}, bf16[4096,128]{1,0:T(8,128)(2,1)}, u32[]{:S(2)}) copy-start(bf16[4096,128]{1,0:T(8,128)(2,1)} %cot_ref.5) | copy-start | bytes 3145732
  53.1 4.3 %collective-permute-start.8 = (bf16[256,128]{1,0:T(8,128)(2,1)S(1)}, bf16[256,128]{1,0:T(8,128)(2,1)S(1)}, u32[]{:S(2)}, u32[]{:S(2)}) collective-permute-start(bf16[256,128]{1,0:T(8,128)(2,1)S(1)} %get-tuple-element.94.rest_0_), channel_id=1, source_target_pairs={{0,32},{32,64},{64,96},{96,0},{1,33},{33,65},{65,97},{97,1},{2,34}... | collective-permute-start | bytes 196616 | tf_op jit(solution)/shard_map/ppermute | solution.py:506
  54.4 4.9 %collective-permute-start.7 = (bf16[256,128]{1,0:T(8,128)(2,1)S(1)}, bf16[256,128]{1,0:T(8,128)(2,1)S(1)}, u32[]{:S(2)}, u32[]{:S(2)}) collective-permute-start(bf16[256,128]{1,0:T(8,128)(2,1)S(1)} %get-tuple-element.94.rest_0_), channel_id=1, source_target_pairs={{0,64},{32,96},{64,0},{96,32},{1,65},{33,97},{65,1},{97,33},{2,66}... | collective-permute-start | bytes 196616 | tf_op jit(solution)/shard_map/ppermute | solution.py:506
  56.4 3.8 %collective-permute-start.6 = (bf16[256,128]{1,0:T(8,128)(2,1)S(1)}, bf16[256,128]{1,0:T(8,128)(2,1)S(1)}, u32[]{:S(2)}, u32[]{:S(2)}) collective-permute-start(bf16[256,128]{1,0:T(8,128)(2,1)S(1)} %get-tuple-element.94.rest_0_), channel_id=1, source_target_pairs={{0,96},{32,0},{64,32},{96,64},{1,97},{33,1},{65,33},{97,65},{2,98}... | collective-permute-start | bytes 196616 | tf_op jit(solution)/shard_map/ppermute | solution.py:506
  70.8 17.5 %all-to-all-start.2 = ((bf16[32,64,128]{2,1,0:T(8,128)(2,1)}), bf16[32,64,128]{2,1,0:T(8,128)(2,1)S(1)}, u32[]{:S(2)}, u32[]{:S(2)}) async-start(bf16[32,64,128]{2,1,0:T(8,128)(2,1)} %get-tuple-element.95), calls=%async_computation.2 | async-start | bytes 1048576 | tf_op jit(solution)/shard_map/all_to_all | solution.py:547
  88.4 4.0 %collective-permute-start.11 = (f32[48,128]{1,0:T(8,128)S(1)}, f32[48,128]{1,0:T(8,128)S(1)}, u32[]{:S(2)}, u32[]{:S(2)}) collective-permute-start(f32[48,128]{1,0:T(8,128)S(1)} %add_parts.1.refs_0_), channel_id=1, source_target_pairs={{0,32},{32,64},{64,96},{96,0},{1,33},{33,65},{65,97},{97,1},{2,34}... | collective-permute-start | bytes 73736 | tf_op jit(solution)/shard_map/ppermute | solution.py:553
  88.7 4.6 %collective-permute-start.10 = (f32[48,128]{1,0:T(8,128)S(1)}, f32[48,128]{1,0:T(8,128)S(1)}, u32[]{:S(2)}, u32[]{:S(2)}) collective-permute-start(f32[48,128]{1,0:T(8,128)S(1)} %add_parts.1.refs_0_), channel_id=1, source_target_pairs={{0,64},{32,96},{64,0},{96,32},{1,65},{33,97},{65,1},{97,33},{2,66}... | collective-permute-start | bytes 73736 | tf_op jit(solution)/shard_map/ppermute | solution.py:553
  91.5 2.7 %collective-permute-start.9 = (f32[48,128]{1,0:T(8,128)S(1)}, f32[48,128]{1,0:T(8,128)S(1)}, u32[]{:S(2)}, u32[]{:S(2)}) collective-permute-start(f32[48,128]{1,0:T(8,128)S(1)} %add_parts.1.refs_0_), channel_id=1, source_target_pairs={{0,96},{32,0},{64,32},{96,64},{1,97},{33,1},{65,33},{97,65},{2,98}... | collective-permute-start | bytes 73736 | tf_op jit(solution)/shard_map/ppermute | solution.py:553
  95.0 15.6 %all-to-all-start.3 = ((bf16[32,48,128]{2,1,0:T(8,128)(2,1)}), bf16[32,48,128]{2,1,0:T(8,128)(2,1)S(1)}, u32[]{:S(2)}, u32[]{:S(2)}) async-start(bf16[32,48,128]{2,1,0:T(8,128)(2,1)} %add_groups.1), calls=%async_computation.3 | async-start | bytes 786432 | tf_op jit(solution)/shard_map/all_to_all | solution.py:559
  (16 other events, 89.9 us)

commit v6 on v4

--- a/solution.py
+++ b/solution.py
@@ -129,24 +129,70 @@
     out_ref[...] = nn(hit_columns(wanted, border), shared).astype(BF)
 
 
-def pool_kernel(group_ref, count_ref, order_ref, updated_ref, node_cot_ref, *refs):
+def choose(index, lines):
+    found = lines[0]
+    for k in range(1, len(lines)):
+        found = jnp.where(index == k, lines[k], found)
+    return found
+
+
+def order_kernel(group_ref, count_ref, order_ref, slot_ref, node_cot_ref, *out_refs):
+    groups, capacity = slot_ref.shape
+    rows = order_ref.shape[1]
+    here = group_ref[0, 0]
+    table = halves(node_cot_ref[...])
+    order = jnp.broadcast_to(order_ref[...], (8, rows))
+    place = lax.broadcasted_iota(I32, (1, capacity), 1)
+    slots = jnp.concatenate(
+        [slot_ref[k : k + 1, at : at + LANES] for k in range(groups) for at in range(0, capacity, LANES)],
+        axis=0,
+    ).astype(F32).astype(BF)
+    for ahead, out_ref in enumerate(out_refs):
+        k = lax.rem(here + (groups - ahead), groups)
+        start = 0
+        for other in range(groups - 1):
+            start = start + jnp.where(other < k, count_ref[0, other], 0)
+        line = pltpu.roll(order, lax.rem(rows - start, rows), 1)[0:1, :capacity]
+        line = jnp.where(place < count_ref[0, k], line, -1)
+        out_ref[:capacity, :] = pick_rows(spread_column(line), table).astype(BF)
+        out_ref[capacity:, :] = slots
+
+
+def cot_pool_kernel(group_ref, slot_ref, *refs):
+    got_refs, out_ref = refs[:-1], refs[-1]
+    groups, capacity = slot_ref.shape
+    lines = [slot_ref[k : k + 1, :] for k in range(groups)]
+    total = jnp.zeros(out_ref.shape, F32)
+    for ahead, got_ref in enumerate(got_refs):
+        line = choose(lax.rem(group_ref[0, 0] + ahead, groups), lines)
+        total = total + nn(hit_rows(line, out_ref.shape[0]), got_ref[:capacity, :])
+    out_ref[...] = total
+
+
+def pool_kernel(group_ref, count_ref, order_ref, updated_ref, *refs):
     groups = (len(refs) - 1) // 2
-    slot_refs, out_ref, send_refs = refs[:groups], refs[groups], refs[groups + 1 :]
-    coarse = send_refs[0].shape[0] // 2
-    capacity = slot_refs[0].shape[1]
+    got_refs, out_ref, send_refs = refs[:groups], refs[groups], refs[groups + 1 :]
+    coarse = send_refs[0].shape[0]
     rows = order_ref.shape[1]
+    capacity = rows // 2
+    pieces = capacity // LANES
     here = group_ref[0, 0]
     place = lax.broadcasted_iota(I32, (8, rows), 1)
     owner = jnp.zeros((8, rows), I32)
     goal = jnp.zeros((8, rows), I32)
-    for ahead, slot_ref in enumerate(slot_refs):
+    for ahead, got_ref in enumerate(got_refs):
         k = lax.rem(here + ahead, groups)
         start = 0
         for other in range(groups - 1):
             start = start + jnp.where(other < k, count_ref[0, other], 0)
-        line = jnp.concatenate(
-            [slot_ref[pl.ds(here, 1), :], jnp.zeros((1, rows - capacity), I32)], axis=1
-        )
+        listed = got_ref[capacity:, :].astype(F32)
+        line = choose(here, [
+            jnp.concatenate(
+                [listed[j * pieces + i : j * pieces + i + 1, :] for i in range(pieces)], axis=1
+            )
+            for j in range(groups)
+        ]).astype(I32)
+        line = jnp.concatenate([line, jnp.zeros((1, rows - capacity), I32)], axis=1)
         line = pltpu.roll(jnp.broadcast_to(line, (8, rows)), start, 1)
         inside = (place >= start) & (place < start + count_ref[0, k])
         owner = jnp.where(inside, ahead, owner)
@@ -155,11 +201,9 @@
     by_row = nt(digits.astype(F32).astype(BF), hit_rows(order_ref[...], rows))
     goal = (by_row[0:1, :] * coarse + by_row[1:2, :]).astype(I32)
     out_ref[...] = goal
-    both = jnp.concatenate([updated_ref[...], node_cot_ref[...]], axis=1)
-    pooled = nn(hit_rows(goal, groups * coarse), both).astype(BF)
+    pooled = nn(hit_rows(goal, groups * coarse), updated_ref[...]).astype(BF)
     for k, send_ref in enumerate(send_refs):
-        send_ref[:coarse, :] = pooled[k * coarse : (k + 1) * coarse, :LANES]
-        send_ref[coarse:, :] = pooled[k * coarse : (k + 1) * coarse, LANES:]
+        send_ref[...] = pooled[k * coarse : (k + 1) * coarse, :]
 
 
 def edge_first_kernel(source_ref, target_ref, nodes_ref, out_ref):
@@ -209,15 +253,14 @@
         updated_ref[...] = (nodes.astype(F32) + normed).astype(BF)
 
 
-def coarse_kernel(feat_ref, cot_ref, w1_ref, w2_ref, *refs):
+def coarse_kernel(feat_ref, cot_ref, from_fine_ref, w1_ref, w2_ref, *refs):
     got_refs, (grad_ref, back_ref, g1_ref, g2_ref) = refs[:-4], refs[-4:]
-    coarse = feat_ref.shape[0]
     got = got_refs[0][...].astype(F32)
     for got_ref in got_refs[1:]:
         got = got + got_ref[...].astype(F32)
-    pooled = (got[:coarse] * POOL_SHARE).astype(BF)
+    pooled = (got * POOL_SHARE).astype(BF)
     cot = cot_ref[...].astype(F32)
-    grad_out = (cot + got[coarse:]).astype(BF)
+    grad_out = (cot + from_fine_ref[...]).astype(BF)
     joined = jnp.concatenate([feat_ref[...], pooled], axis=1)
     pre = nn(joined, w1_ref[...])
     sig = sigmoid(pre)
@@ -437,14 +480,21 @@
         out_specs=pl.BlockSpec((2, grid_block, latent), lambda i: (0, i, 0)),
         flops=4 * 10**9, bytes_accessed=3 * 10**6, name="edge_first", vmem=61,
     )
-    asked, own_rows = lax.optimization_barrier((asked, own_rows))
+    messages = call(
+        order_kernel, [shape((rows // 2 + 16, latent), BF)] * groups,
+        here, restr_count, restr_order, slot_list, node_cotangent,
+        in_specs=[pl.BlockSpec(memory_space=pltpu.SMEM)] * 2
+        + [pl.BlockSpec(memory_space=pltpu.VMEM)] * 3,
+        flops=10**9, bytes_accessed=10**6, name="order", vmem=16,
+    )
+    asked, own_rows, messages = lax.optimization_barrier((asked, own_rows, messages))
     share = call(
         share_kernel, shape((ghosts, latent), BF), boundary, asked, node_features,
         flops=10**9, bytes_accessed=10**6, name="share", vmem=16,
     )
-    share, slot_list = lax.optimization_barrier((share, slot_list))
-    slot_lists = [slot_list] + [
-        lax.ppermute(slot_list, "group", turned(ahead)) for ahead in range(1, groups)
+    share, messages = lax.optimization_barrier((share, messages))
+    messages = [messages[0]] + [
+        lax.ppermute(messages[ahead], "group", turned(ahead)) for ahead in range(1, groups)
     ]
     ghost_rows = exchange(share.reshape(domains, slots, latent), "dom").reshape(ghosts, latent)
     grid, index_spec, edge_spec = edge_blocks(4096)
@@ -463,20 +513,27 @@
         flops=5 * 10**9, bytes_accessed=8 * 10**6, name="edge_second",
     )
     goal, *send = call(
-        pool_kernel, [shape((1, rows), I32)] + [shape((2 * coarse, latent), BF)] * groups,
-        here, restr_count, restr_order, updated, node_cotangent, *slot_lists,
+        pool_kernel, [shape((1, rows), I32)] + [shape((coarse, latent), BF)] * groups,
+        here, restr_count, restr_order, updated, *messages,
         in_specs=[pl.BlockSpec(memory_space=pltpu.SMEM)] * 2
-        + [pl.BlockSpec(memory_space=pltpu.VMEM)] * (3 + groups),
+        + [pl.BlockSpec(memory_space=pltpu.VMEM)] * (2 + groups),
         flops=10**9, bytes_accessed=10**6, name="pool", vmem=16,
     )
     got = [send[0]] + [
         lax.ppermute(send[ahead], "group", turned(-ahead)) for ahead in range(1, groups)
     ]
+    from_fine = call(
+        cot_pool_kernel, shape((coarse, latent), F32), here, slot_list, *messages,
+        in_specs=[pl.BlockSpec(memory_space=pltpu.SMEM)]
+        + [pl.BlockSpec(memory_space=pltpu.VMEM)] * (1 + groups),
+        flops=10**9, bytes_accessed=10**6, name="cot_pool", vmem=16,
+    )
+    got, from_fine = lax.optimization_barrier((got, from_fine))
     grad_coarse, coarse_back, grad_c_one, grad_c_two = call(
         coarse_kernel,
         [shape((coarse, latent), F32), shape((coarse, latent), BF),
          shape((2 * latent, latent), F32), shape((latent, latent), F32)],
-        coarse_features, coarse_cotangent, coarse_w_one, coarse_w_two, *got,
+        coarse_features, coarse_cotangent, from_fine, coarse_w_one, coarse_w_two, *got,
         flops=10**8, bytes_accessed=10**6, name="coarse", vmem=16,
     )
     returned = [coarse_back] + [

time: 111 us -> 110 us (level)
  waiting for transfers between devices: 29.5 us -> 24.2 us
  Pallas kernels: 30.6 us -> 32.5 us
  starting transfers between devices: 42.9 us -> 44.3 us
    ppermute x3, waiting for transfers between devices: 5.32 us -> 1.33 us  [local(): lax.ppermute(send[ahead], 'group', turned(-ahead))]
    pallas_call x12 -> x14, Pallas kernels: 30.6 us -> 32.5 us  [call(): pl.pallas_call(kernel, out_shape=out_shapes if single else list(out_shape...]
    all_to_all x1, waiting for transfers between devices: 2.77 us -> 1.24 us  [local(): exchange(spread.reshape(domains, slots, latent), 'dom')]
    all_to_all x1, starting transfers between devices: 4.63 us -> 6.16 us  [local(): exchange(share.reshape(domains, slots, latent), 'dom')]
    all_to_all x1, starting transfers between devices: 5.86 us -> 7.38 us  [local(): exchange(joint, 'dom')]
    all_to_all x1, waiting for transfers between devices: 1.95 us -> 3.17 us  [local(): exchange(share.reshape(domains, slots, latent), 'dom')]
    ppermute x3, starting transfers between devices: 5.74 us -> 4.53 us  [local(): lax.ppermute(messages[ahead], 'group', turned(ahead))]
    unnamed x47 -> x57, local copies, waits for them, and re-layouts: 6.48 us -> 7.41 us
  transfers between devices with their start and end apart: 16 -> 16, of which waited for: 12 -> 12; matrix products, arithmetic and copies ran while one was open for 0% -> 0% of each run, Pallas kernels for 14% -> 16%
where the time goes in v6:
time: 110 us; the launch traced here: 109 us
  starting transfers between devices  44.3 us (40%)
  Pallas kernels  32.5 us (30%)
  waiting for transfers between devices  24.2 us (22%)
  local copies, waits for them, and re-layouts  7.41 us (7%)
    pallas_call x14, Pallas kernels, call(): pl.pallas_call(kernel, out_shape=out_shapes if single else list(out_shape...  32.5 us
    all_to_all x1, waiting for transfers between devices, local(): pack_all = exchange(pack_sum, 'dom').reshape(pack_rows, latent)  8.97 us
    all_to_all x1, starting transfers between devices, local(): exchange(spread.reshape(domains, slots, latent), 'dom')  8.59 us
    unnamed x57, local copies, waits for them, and re-layouts  7.41 us
    all_to_all x1, starting transfers between devices, local(): exchange(joint, 'dom')  7.38 us
    all_to_all x1, starting transfers between devices, local(): exchange(share.reshape(domains, slots, latent), 'dom')  6.16 us
    ppermute x3, starting transfers between devices, local(): lax.ppermute(send[ahead], 'group', turned(-ahead))  5.74 us
    all_to_all x1, starting transfers between devices, local(): pack_all = exchange(pack_sum, 'dom').reshape(pack_rows, latent)  5.23 us
  transfers between devices with their start and end apart: 16, of which 12 were waited for; matrix products, arithmetic and copies ran while one was open for 0% of the time, Pallas kernels for 16%

profile of v6, /device:TPU:1, one launch (start us, length us, event | category | flops | bytes accessed | tf_op | source)
XLA Modules:
  0.0 109.4 jit_solution(9015727968220487095)
XLA Ops:
  2.4 8.6 %all-to-all-start = ((bf16[32,16,128]{2,1,0:T(8,128)(2,1)}), bf16[32,16,128]{2,1,0:T(8,128)(2,1)S(1)}, u32[]{:S(2)}, u32[]{:S(2)}) async-start(bf16[32,16,128]{2,1,0:T(8,128)(2,1)} %bitcast), calls=%async_computation | async-start | bytes 262144 | tf_op jit(solution)/shard_map/all_to_all | solution.py:470
  11.0 4.9 %edge_first.1.own_ref.tgt_ref = bf16[2,4096,128]{2,1,0:T(8,128)(2,1)} custom-call(s32[1,4096]{1,0:T(1,128)} %bitcast.13, s32[1,4096]{1,0:T(1,128)} %bitcast.17, bf16[1024,128]{1,0:T(8,128)(2,1)} %nodes_ref.7), custom_call_target="tpu_custom_call" | custom-call | flops 4000000000 | bytes 3000000 | tf_op jit(solution)/shard_map/edge_first/pallas_call | solution.py:423
  15.9 1.4 %order.1 = (bf16[528,128]{1,0:T(8,128)(2,1)S(1)}, bf16[528,128]{1,0:T(8,128)(2,1)S(1)}, bf16[528,128]{1,0:T(8,128)(2,1)S(1)}, bf16[528,128]{1,0:T(8,128)(2,1)S(1)}) custom-call(s32[1,1]{1,0:T(1,128)} %bitcast.4.group_ref, s32[1,4]{1,0:T(1,128)S(1)} %copy-done.20, s32[1,1024]{1,0:T(1,128)S(1)} %copy-done.18, s32[4,512]{1,0:T(4,128)S(1)} %bitcast.21, ...), custom_call_target="tpu_custom_call" | custom-call | flops 1000000000 | bytes 1000000 | tf_op jit(solution)/shard_map/order/pallas_call | solution.py:423
  17.4 1.2 %all-to-all-done = bf16[32,16,128]{2,1,0:T(8,128)(2,1)S(1)} async-done(((bf16[32,16,128]{2,1,0:T(8,128)(2,1)}), bf16[32,16,128]{2,1,0:T(8,128)(2,1)S(1)}, u32[]{:S(2)}, u32[]{:S(2)}) %all-to-all-start) | async-done | bytes 131104 | tf_op jit(solution)/shard_map/all_to_all | solution.py:470
  18.7 1.2 %share.1 = bf16[512,128]{1,0:T(8,128)(2,1)} custom-call(s32[1,256]{1,0:T(1,128)S(1)} %copy-done.19, bf16[512,128]{1,0:T(8,128)(2,1)S(1)} %bitcast.10, bf16[1024,128]{1,0:T(8,128)(2,1)S(1)} %copy-done.6), custom_call_target="tpu_custom_call" | custom-call | flops 1000000000 | bytes 1000000 | tf_op jit(solution)/shard_map/share/pallas_call | solution.py:423
  19.9 6.2 %all-to-all-start.1 = ((bf16[32,16,128]{2,1,0:T(8,128)(2,1)}), bf16[32,16,128]{2,1,0:T(8,128)(2,1)S(1)}, u32[]{:S(2)}, u32[]{:S(2)}) async-start(bf16[32,16,128]{2,1,0:T(8,128)(2,1)} %bitcast.6), calls=%async_computation.1 | async-start | bytes 262144 | tf_op jit(solution)/shard_map/all_to_all | solution.py:499
  26.1 3.8 %collective-permute-start = (bf16[528,128]{1,0:T(8,128)(2,1)S(1)}, bf16[528,128]{1,0:T(8,128)(2,1)S(1)}, u32[]{:S(2)}, u32[]{:S(2)}) collective-permute-start(bf16[528,128]{1,0:T(8,128)(2,1)S(1)} %get-tuple-element.70), channel_id=1, source_target_pairs={{0,96},{32,0},{64,32},{96,64},{1,97},{33,1},{65,33},{97,65},{2,98}... | collective-permute-start | bytes 405512 | tf_op jit(solution)/shard_map/ppermute | solution.py:497
  30.6 3.2 %all-to-all-done.1 = bf16[32,16,128]{2,1,0:T(8,128)(2,1)S(1)} async-done(((bf16[32,16,128]{2,1,0:T(8,128)(2,1)}), bf16[32,16,128]{2,1,0:T(8,128)(2,1)S(1)}, u32[]{:S(2)}, u32[]{:S(2)}) %all-to-all-start.1) | async-done | bytes 131104 | tf_op jit(solution)/shard_map/all_to_all | solution.py:499
  33.9 1.6 %copy-done.23 = bf16[2,4096,128]{2,1,0:T(8,128)(2,1)S(1)} copy-done((bf16[2,4096,128]{2,1,0:T(8,128)(2,1)S(1)}, bf16[2,4096,128]{2,1,0:T(8,128)(2,1)}, u32[]{:S(2)}) %copy-start.23) | copy-done | bytes 2097176
  35.4 4.7 %edge_second.1 = (f32[4096,128]{1,0:T(8,128)S(1)}, bf16[4096,128]{1,0:T(8,128)(2,1)S(1)}, bf16[1024,128]{1,0:T(8,128)(2,1)S(1)}, bf16[1024,128]{1,0:T(8,128)(2,1)S(1)}) custom-call(s32[1,4096]{1,0:T(1,128)S(1)} %bitcast.14, s32[1,4096]{1,0:T(1,128)S(1)} %bitcast.18, bf16[2,4096,128]{2,1,0:T(8,128)(2,1)S(1)} %copy-done.23, bf16[4096,128]{1,0:T(8,128)(2,1)S(1)} %copy-done.4, ...), custom_call_target="tpu_custom_call" | custom-call | flops 5000000000 | bytes 8000000 | tf_op jit(solution)/shard_map/edge_second/pallas_call | solution.py:423
  40.2 1.9 %pool.1 = (s32[1,1024]{1,0:T(1,128)S(1)}, bf16[256,128]{1,0:T(8,128)(2,1)S(1)}, bf16[256,128]{1,0:T(8,128)(2,1)S(1)}, bf16[256,128]{1,0:T(8,128)(2,1)S(1)}, bf16[256,128]{1,0:T(8,128)(2,1)S(1)}) custom-call(s32[1,1]{1,0:T(1,128)} %bitcast.4.group_ref, s32[1,4]{1,0:T(1,128)S(1)} %copy-done.20, s32[1,1024]{1,0:T(1,128)S(1)} %copy-done.18, ...), custom_call_target="tpu_custom_call" | custom-call | flops 1000000000 | bytes 1000000 | tf_op jit(solution)/shard_map/pool/pallas_call | solution.py:423
  42.2 1.7 %collective-permute-start.3 = (bf16[256,128]{1,0:T(8,128)(2,1)S(1)}, bf16[256,128]{1,0:T(8,128)(2,1)S(1)}, u32[]{:S(2)}, u32[]{:S(2)}) collective-permute-start(bf16[256,128]{1,0:T(8,128)(2,1)S(1)} %get-tuple-element.76), channel_id=1, source_target_pairs={{0,32},{32,64},{64,96},{96,0},{1,33},{33,65},{65,97},{97,1},{2,34}... | collective-permute-start | bytes 196616 | tf_op jit(solution)/shard_map/ppermute | solution.py:523
  43.9 3.3 %collective-permute-start.4 = (bf16[256,128]{1,0:T(8,128)(2,1)S(1)}, bf16[256,128]{1,0:T(8,128)(2,1)S(1)}, u32[]{:S(2)}, u32[]{:S(2)}) collective-permute-start(bf16[256,128]{1,0:T(8,128)(2,1)S(1)} %get-tuple-element.77), channel_id=1, source_target_pairs={{0,64},{32,96},{64,0},{96,32},{1,65},{33,97},{65,1},{97,33},{2,66}... | collective-permute-start | bytes 196616 | tf_op jit(solution)/shard_map/ppermute | solution.py:523
  50.6 1.3 %coarse.1 = (f32[256,128]{1,0:T(8,128)}, bf16[256,128]{1,0:T(8,128)(2,1)S(1)}, f32[256,128]{1,0:T(8,128)S(1)}, f32[128,128]{1,0:T(8,128)S(1)}) custom-call(bf16[256,128]{1,0:T(8,128)(2,1)S(1)} %copy-done, bf16[256,128]{1,0:T(8,128)(2,1)S(1)} %copy-done.1, f32[256,128]{1,0:T(8,128)S(1)} %cot_pool.1.from_fine_ref, bf16[256,128]{1,0:T(8,128)(2,1)S(1)} %copy-done.2, ...), custom_call_target="tpu_custom_call" | custom-call | flops 100000000 | bytes 1000000 | tf_op jit(solution)/shard_map/coarse/pallas_call | solution.py:423
  52.5 2.3 %collective-permute-start.7 = (bf16[256,128]{1,0:T(8,128)(2,1)S(1)}, bf16[256,128]{1,0:T(8,128)(2,1)S(1)}, u32[]{:S(2)}, u32[]{:S(2)}) collective-permute-start(bf16[256,128]{1,0:T(8,128)(2,1)S(1)} %get-tuple-element.86.rest_0_), channel_id=1, source_target_pairs={{0,64},{32,96},{64,0},{96,32},{1,65},{33,97},{65,1},{97,33},{2,66}... | collective-permute-start | bytes 196616 | tf_op jit(solution)/shard_map/ppermute | solution.py:540
  58.2 7.9 %edge_back.1 = (bf16[4096,128]{1,0:T(8,128)(2,1)S(1)}, f32[1024,128]{1,0:T(8,128)S(1)}, bf16[32,64,128]{2,1,0:T(8,128)(2,1)}) custom-call(s32[1,4096]{1,0:T(1,128)S(1)} %bitcast.15, s32[1,4096]{1,0:T(1,128)S(1)} %bitcast.19, f32[4096,128]{1,0:T(8,128)S(1)} %get-tuple-element.66.pre_ref, bf16[4096,128]{1,0:T(8,128)(2,1)S(1)} %get-tuple-element.67.src_ref, ...), custom_call_target="tpu_custom_call" | custom-call | flops 6000000000 | bytes 10000000 | tf_op jit(solution)/shard_map/edge_back/pallas_call | solution.py:423
  67.8 7.4 %all-to-all-start.2 = ((bf16[32,64,128]{2,1,0:T(8,128)(2,1)}), bf16[32,64,128]{2,1,0:T(8,128)(2,1)S(1)}, u32[]{:S(2)}, u32[]{:S(2)}) async-start(bf16[32,64,128]{2,1,0:T(8,128)(2,1)} %get-tuple-element.87), calls=%async_computation.2 | async-start | bytes 1048576 | tf_op jit(solution)/shard_map/all_to_all | solution.py:580
  75.2 1.2 %copy-done.25 = bf16[4096,128]{1,0:T(8,128)(2,1)S(1)} copy-done((bf16[4096,128]{1,0:T(8,128)(2,1)S(1)}, bf16[4096,128]{1,0:T(8,128)(2,1)}, u32[]{:S(2)}) %copy-start.25) | copy-done | bytes 1048600
  77.5 4.7 %own_back.1 = (f32[1024,128]{1,0:T(8,128)S(1)}, f32[4096,128]{1,0:T(8,128)}) custom-call(s32[1,4096]{1,0:T(1,128)S(1)} %bitcast.16, s32[1,4096]{1,0:T(1,128)S(1)} %bitcast.20, bf16[4096,128]{1,0:T(8,128)(2,1)S(1)} %copy-done.25, bf16[4096,128]{1,0:T(8,128)(2,1)S(1)} %copy-done.5, f32[1024,128]{1,0:T(8,128)S(1)} %copy-done.27, bf16[384,128]{1,0:T(8,128)(2,1)S(1)} %copy-done.8), custom_call_target="tpu_custom_call" | custom-call | flops 4000000000 | bytes 5000000 | tf_op jit(solution)/shard_map/own_back/pallas_call | solution.py:423
  82.2 4.6 %all-to-all-done.2.got_ref = bf16[32,64,128]{2,1,0:T(8,128)(2,1)S(1)} async-done(((bf16[32,64,128]{2,1,0:T(8,128)(2,1)}), bf16[32,64,128]{2,1,0:T(8,128)(2,1)S(1)}, u32[]{:S(2)}, u32[]{:S(2)}) %all-to-all-start.2) | async-done | bytes 524320 | tf_op jit(solution)/shard_map/all_to_all | solution.py:580
  87.0 2.5 %collective-permute-start.10 = (f32[48,128]{1,0:T(8,128)S(1)}, f32[48,128]{1,0:T(8,128)S(1)}, u32[]{:S(2)}, u32[]{:S(2)}) collective-permute-start(f32[48,128]{1,0:T(8,128)S(1)} %add_parts.1.refs_0_), channel_id=1, source_target_pairs={{0,64},{32,96},{64,0},{96,32},{1,65},{33,97},{65,1},{97,33},{2,66}... | collective-permute-start | bytes 73736 | tf_op jit(solution)/shard_map/ppermute | solution.py:586
  93.0 5.2 %all-to-all-start.3 = ((bf16[32,48,128]{2,1,0:T(8,128)(2,1)}), bf16[32,48,128]{2,1,0:T(8,128)(2,1)S(1)}, u32[]{:S(2)}, u32[]{:S(2)}) async-start(bf16[32,48,128]{2,1,0:T(8,128)(2,1)} %add_groups.1), calls=%async_computation.3 | async-start | bytes 786432 | tf_op jit(solution)/shard_map/all_to_all | solution.py:592
  98.3 1.3 %add_back.1 = f32[1024,128]{1,0:T(8,128)} custom-call(s32[1,256]{1,0:T(1,128)S(1)} %copy-done.19, bf16[512,128]{1,0:T(8,128)(2,1)S(1)} %bitcast.11, bf16[32,64,128]{2,1,0:T(8,128)(2,1)S(1)} %all-to-all-done.2.got_ref, f32[1024,128]{1,0:T(8,128)S(1)} %get-tuple-element.92.local_ref), custom_call_target="tpu_custom_call" | custom-call | flops 1000000000 | bytes 1000000 | tf_op jit(solution)/shard_map/add_back/pallas_call | solution.py:423
  99.6 9.0 %all-to-all-done.3 = bf16[32,48,128]{2,1,0:T(8,128)(2,1)S(1)} async-done(((bf16[32,48,128]{2,1,0:T(8,128)(2,1)}), bf16[32,48,128]{2,1,0:T(8,128)(2,1)S(1)}, u32[]{:S(2)}, u32[]{:S(2)}) %all-to-all-start.3) | async-done | bytes 393248 | tf_op jit(solution)/shard_map/all_to_all | solution.py:592
  (79 shorter events, 17.3 us)
Async XLA Ops:
  2.4 16.3 %all-to-all-start = ((bf16[32,16,128]{2,1,0:T(8,128)(2,1)}), bf16[32,16,128]{2,1,0:T(8,128)(2,1)S(1)}, u32[]{:S(2)}, u32[]{:S(2)}) async-start(bf16[32,16,128]{2,1,0:T(8,128)(2,1)} %bitcast), calls=%async_computation | async-start | bytes 262144 | tf_op jit(solution)/shard_map/all_to_all | solution.py:470
  17.3 22.9 %copy-start.21 = (bf16[528,128]{1,0:T(8,128)(2,1)}, bf16[528,128]{1,0:T(8,128)(2,1)S(1)}, u32[]{:S(2)}) copy-start(bf16[528,128]{1,0:T(8,128)(2,1)S(1)} %get-tuple-element.69.refs_0_) | copy-start | bytes 405508
  17.4 16.4 %copy-start.4 = (bf16[4096,128]{1,0:T(8,128)(2,1)S(1)}, bf16[4096,128]{1,0:T(8,128)(2,1)}, u32[]{:S(2)}) copy-start(bf16[4096,128]{1,0:T(8,128)(2,1)} %edges_ref.3) | copy-start | bytes 3145732
  17.4 16.4 %copy-start.8 = (bf16[384,128]{1,0:T(8,128)(2,1)S(1)}, bf16[384,128]{1,0:T(8,128)(2,1)}, u32[]{:S(2)}) copy-start(bf16[384,128]{1,0:T(8,128)(2,1)} %w1_ref.7) | copy-start | bytes 294916
  17.4 16.4 %copy-start.9 = (bf16[256,128]{1,0:T(8,128)(2,1)S(1)}, bf16[256,128]{1,0:T(8,128)(2,1)}, u32[]{:S(2)}) copy-start(bf16[256,128]{1,0:T(8,128)(2,1)} %v1_ref.3) | copy-start | bytes 196612
  17.4 16.4 %copy-start.10 = (bf16[128,128]{1,0:T(8,128)(2,1)S(1)}, bf16[128,128]{1,0:T(8,128)(2,1)}, u32[]{:S(2)}) copy-start(bf16[128,128]{1,0:T(8,128)(2,1)} %w2_ref.5) | copy-start | bytes 98308
  17.4 16.4 %copy-start.11 = (bf16[128,128]{1,0:T(8,128)(2,1)S(1)}, bf16[128,128]{1,0:T(8,128)(2,1)}, u32[]{:S(2)}) copy-start(bf16[128,128]{1,0:T(8,128)(2,1)} %v2_ref.3) | copy-start | bytes 98308
  19.9 13.9 %all-to-all-start.1 = ((bf16[32,16,128]{2,1,0:T(8,128)(2,1)}), bf16[32,16,128]{2,1,0:T(8,128)(2,1)S(1)}, u32[]{:S(2)}, u32[]{:S(2)}) async-start(bf16[32,16,128]{2,1,0:T(8,128)(2,1)} %bitcast.6), calls=%async_computation.1 | async-start | bytes 262144 | tf_op jit(solution)/shard_map/all_to_all | solution.py:499
  26.1 14.1 %collective-permute-start = (bf16[528,128]{1,0:T(8,128)(2,1)S(1)}, bf16[528,128]{1,0:T(8,128)(2,1)S(1)}, u32[]{:S(2)}, u32[]{:S(2)}) collective-permute-start(bf16[528,128]{1,0:T(8,128)(2,1)S(1)} %get-tuple-element.70), channel_id=1, source_target_pairs={{0,96},{32,0},{64,32},{96,64},{1,97},{33,1},{65,33},{97,65},{2,98}... | collective-permute-start | bytes 405512 | tf_op jit(solution)/shard_map/ppermute | solution.py:497
  29.9 10.3 %collective-permute-start.1 = (bf16[528,128]{1,0:T(8,128)(2,1)S(1)}, bf16[528,128]{1,0:T(8,128)(2,1)S(1)}, u32[]{:S(2)}, u32[]{:S(2)}) collective-permute-start(bf16[528,128]{1,0:T(8,128)(2,1)S(1)} %get-tuple-element.71), channel_id=1, source_target_pairs={{0,64},{32,96},{64,0},{96,32},{1,65},{33,97},{65,1},{97,33},{2,66}... | collective-permute-start | bytes 405512 | tf_op jit(solution)/shard_map/ppermute | solution.py:497
  29.9 10.3 %collective-permute-start.2 = (bf16[528,128]{1,0:T(8,128)(2,1)S(1)}, bf16[528,128]{1,0:T(8,128)(2,1)S(1)}, u32[]{:S(2)}, u32[]{:S(2)}) collective-permute-start(bf16[528,128]{1,0:T(8,128)(2,1)S(1)} %get-tuple-element.72), channel_id=1, source_target_pairs={{0,32},{32,64},{64,96},{96,0},{1,33},{33,65},{65,97},{97,1},{2,34}... | collective-permute-start | bytes 405512 | tf_op jit(solution)/shard_map/ppermute | solution.py:497
  42.2 7.1 %collective-permute-start.3 = (bf16[256,128]{1,0:T(8,128)(2,1)S(1)}, bf16[256,128]{1,0:T(8,128)(2,1)S(1)}, u32[]{:S(2)}, u32[]{:S(2)}) collective-permute-start(bf16[256,128]{1,0:T(8,128)(2,1)S(1)} %get-tuple-element.76), channel_id=1, source_target_pairs={{0,32},{32,64},{64,96},{96,0},{1,33},{33,65},{65,97},{97,1},{2,34}... | collective-permute-start | bytes 196616 | tf_op jit(solution)/shard_map/ppermute | solution.py:523
  43.9 6.2 %collective-permute-start.4 = (bf16[256,128]{1,0:T(8,128)(2,1)S(1)}, bf16[256,128]{1,0:T(8,128)(2,1)S(1)}, u32[]{:S(2)}, u32[]{:S(2)}) collective-permute-start(bf16[256,128]{1,0:T(8,128)(2,1)S(1)} %get-tuple-element.77), channel_id=1, source_target_pairs={{0,64},{32,96},{64,0},{96,32},{1,65},{33,97},{65,1},{97,33},{2,66}... | collective-permute-start | bytes 196616 | tf_op jit(solution)/shard_map/ppermute | solution.py:523
  47.2 3.4 %collective-permute-start.5 = (bf16[256,128]{1,0:T(8,128)(2,1)S(1)}, bf16[256,128]{1,0:T(8,128)(2,1)S(1)}, u32[]{:S(2)}, u32[]{:S(2)}) collective-permute-start(bf16[256,128]{1,0:T(8,128)(2,1)S(1)} %get-tuple-element.78), channel_id=1, source_target_pairs={{0,96},{32,0},{64,32},{96,64},{1,97},{33,1},{65,33},{97,65},{2,98}... | collective-permute-start | bytes 196616 | tf_op jit(solution)/shard_map/ppermute | solution.py:523
  51.9 4.3 %collective-permute-start.8 = (bf16[256,128]{1,0:T(8,128)(2,1)S(1)}, bf16[256,128]{1,0:T(8,128)(2,1)S(1)}, u32[]{:S(2)}, u32[]{:S(2)}) collective-permute-start(bf16[256,128]{1,0:T(8,128)(2,1)S(1)} %get-tuple-element.86.rest_0_), channel_id=1, source_target_pairs={{0,32},{32,64},{64,96},{96,0},{1,33},{33,65},{65,97},{97,1},{2,34}... | collective-permute-start | bytes 196616 | tf_op jit(solution)/shard_map/ppermute | solution.py:540
  52.5 4.7 %collective-permute-start.7 = (bf16[256,128]{1,0:T(8,128)(2,1)S(1)}, bf16[256,128]{1,0:T(8,128)(2,1)S(1)}, u32[]{:S(2)}, u32[]{:S(2)}) collective-permute-start(bf16[256,128]{1,0:T(8,128)(2,1)S(1)} %get-tuple-element.86.rest_0_), channel_id=1, source_target_pairs={{0,64},{32,96},{64,0},{96,32},{1,65},{33,97},{65,1},{97,33},{2,66}... | collective-permute-start | bytes 196616 | tf_op jit(solution)/shard_map/ppermute | solution.py:540
  54.8 3.4 %collective-permute-start.6 = (bf16[256,128]{1,0:T(8,128)(2,1)S(1)}, bf16[256,128]{1,0:T(8,128)(2,1)S(1)}, u32[]{:S(2)}, u32[]{:S(2)}) collective-permute-start(bf16[256,128]{1,0:T(8,128)(2,1)S(1)} %get-tuple-element.86.rest_0_), channel_id=1, source_target_pairs={{0,96},{32,0},{64,32},{96,64},{1,97},{33,1},{65,33},{97,65},{2,98}... | collective-permute-start | bytes 196616 | tf_op jit(solution)/shard_map/ppermute | solution.py:540
  58.2 17.0 %copy-start.13 = (s32[4096]{0:T(1024)S(1)}, s32[4096]{0:T(1024)}, u32[]{:S(2)}) copy-start(s32[4096]{0:T(1024)} %param.28) | copy-start | bytes 49156
  58.2 17.0 %copy-start.16 = (s32[4096]{0:T(1024)S(1)}, s32[4096]{0:T(1024)}, u32[]{:S(2)}) copy-start(s32[4096]{0:T(1024)} %param.29) | copy-start | bytes 49156
  67.8 19.0 %all-to-all-start.2 = ((bf16[32,64,128]{2,1,0:T(8,128)(2,1)}), bf16[32,64,128]{2,1,0:T(8,128)(2,1)S(1)}, u32[]{:S(2)}, u32[]{:S(2)}) async-start(bf16[32,64,128]{2,1,0:T(8,128)(2,1)} %get-tuple-element.87), calls=%async_computation.2 | async-start | bytes 1048576 | tf_op jit(solution)/shard_map/all_to_all | solution.py:580
  86.9 4.0 %collective-permute-start.11 = (f32[48,128]{1,0:T(8,128)S(1)}, f32[48,128]{1,0:T(8,128)S(1)}, u32[]{:S(2)}, u32[]{:S(2)}) collective-permute-start(f32[48,128]{1,0:T(8,128)S(1)} %add_parts.1.refs_0_), channel_id=1, source_target_pairs={{0,32},{32,64},{64,96},{96,0},{1,33},{33,65},{65,97},{97,1},{2,34}... | collective-permute-start | bytes 73736 | tf_op jit(solution)/shard_map/ppermute | solution.py:586
  87.0 4.4 %collective-permute-start.10 = (f32[48,128]{1,0:T(8,128)S(1)}, f32[48,128]{1,0:T(8,128)S(1)}, u32[]{:S(2)}, u32[]{:S(2)}) collective-permute-start(f32[48,128]{1,0:T(8,128)S(1)} %add_parts.1.refs_0_), channel_id=1, source_target_pairs={{0,64},{32,96},{64,0},{96,32},{1,65},{33,97},{65,1},{97,33},{2,66}... | collective-permute-start | bytes 73736 | tf_op jit(solution)/shard_map/ppermute | solution.py:586
  89.5 2.8 %collective-permute-start.9 = (f32[48,128]{1,0:T(8,128)S(1)}, f32[48,128]{1,0:T(8,128)S(1)}, u32[]{:S(2)}, u32[]{:S(2)}) collective-permute-start(f32[48,128]{1,0:T(8,128)S(1)} %add_parts.1.refs_0_), channel_id=1, source_target_pairs={{0,96},{32,0},{64,32},{96,64},{1,97},{33,1},{65,33},{97,65},{2,98}... | collective-permute-start | bytes 73736 | tf_op jit(solution)/shard_map/ppermute | solution.py:586
  93.0 15.5 %all-to-all-start.3 = ((bf16[32,48,128]{2,1,0:T(8,128)(2,1)}), bf16[32,48,128]{2,1,0:T(8,128)(2,1)S(1)}, u32[]{:S(2)}, u32[]{:S(2)}) async-start(bf16[32,48,128]{2,1,0:T(8,128)(2,1)} %add_groups.1), calls=%async_computation.3 | async-start | bytes 786432 | tf_op jit(solution)/shard_map/all_to_all | solution.py:592
  (20 other events, 120.4 us)

commit v7 on v6

--- a/solution.py
+++ b/solution.py
@@ -94,7 +94,10 @@
 
 
 def norm_parts(values):
-    centred = values - mean_lanes(values)
+    return scaled(values - mean_lanes(values))
+
+
+def scaled(centred):
     inv_std = lax.rsqrt(mean_lanes(centred * centred) + NORM_EPSILON)
     return centred * inv_std, inv_std
 
@@ -273,8 +276,32 @@
     back_ref[...] = (grad_in[:, LANES:] * POOL_SHARE).astype(BF)
 
 
+def slopes_kernel(
+    pre_ref, w2_ref, nodes_ref, summed_ref, v1_ref, v2_ref,
+    slope_ref, hidden_ref, centred_ref, node_slope_ref, node_hidden_ref, node_centred_ref,
+):
+    def fill(pre, weights, out_refs, here):
+        sig = sigmoid(pre)
+        hidden = (pre * sig).astype(BF)
+        pre_norm = nn(hidden, weights)
+        parts = (slope(pre, sig), hidden, pre_norm - mean_lanes(pre_norm))
+        for out_ref, part in zip(out_refs, parts):
+            out_ref[here, :] = part
+
+    for part in range(0, pre_ref.shape[0], SECOND_SUB):
+        here = slice(part, part + SECOND_SUB)
+        fill(pre_ref[here, :], w2_ref[...], (slope_ref, hidden_ref, centred_ref), here)
+    joined = jnp.concatenate([nodes_ref[...], summed_ref[...]], axis=1)
+    fill(
+        nn(joined, v1_ref[...]), v2_ref[...],
+        (node_slope_ref, node_hidden_ref, node_centred_ref),
+        slice(0, nodes_ref.shape[0]),
+    )
+
+
 def edge_back_kernel(
-    source_ref, target_ref, pre_ref, src_ref, tgt_ref, edges_ref, cot_ref, w1_ref, w2_ref,
+    node_slope_ref, node_hidden_ref, node_centred_ref,
+    source_ref, target_ref, slope_ref, hidden_ref, centred_ref, src_ref, tgt_ref, edges_ref, cot_ref, w1_ref, w2_ref,
     goal_ref, node_cot_ref, nodes_ref, summed_ref, v1_ref, v2_ref, c1_ref, c2_ref, *rest,
 ):
     gp_refs = rest[:-10]
@@ -291,35 +318,26 @@
         from_coarse = pick_rows(spread_column(goal_ref[...]), table)
         updated_grad = node_cot_ref[...].astype(F32) + from_coarse
         joined = jnp.concatenate([nodes_ref[...], summed_ref[...]], axis=1)
-        pre = nn(joined, v1_ref[...])
-        sig = sigmoid(pre)
-        hidden = (pre * sig).astype(BF)
-        normed, inv_std = norm_parts(nn(hidden, v2_ref[...]))
-        grad_norm = norm_back(normed, inv_std, updated_grad).astype(BF)
-        gv2[...] = tn(hidden, grad_norm)
-        grad_pre = (nt(grad_norm, v2_ref[...]) * slope(pre, sig)).astype(BF)
+        grad_norm = norm_back(*scaled(node_centred_ref[...]), updated_grad).astype(BF)
+        gv2[...] = tn(node_hidden_ref[...], grad_norm)
+        grad_pre = (nt(grad_norm, v2_ref[...]) * node_slope_ref[...]).astype(BF)
         gv1[...] = tn(joined, grad_pre)
         grad_in = nt(grad_pre, v1_ref[...])
         local_ref[...] = updated_grad + grad_in[:, :LANES]
         wide[...] = halves(grad_in[:, LANES:].astype(BF))
 
     target = spread_column(target_ref[...])
-    hiddens, grad_norms, grad_pres = [], [], []
+    grad_norms, grad_pres = [], []
     for part in range(0, target.shape[0], BACK_SUB):
         here = slice(part, part + BACK_SUB)
         message_grad = cot_ref[here, :].astype(F32) + pick_rows(target[here], wide[...])
-        pre = pre_ref[here, :]
-        sig = sigmoid(pre)
-        hidden = (pre * sig).astype(BF)
-        normed, inv_std = norm_parts(nn(hidden, w2_ref[...]))
-        grad_norm = norm_back(normed, inv_std, message_grad).astype(BF)
-        grad_pre = (nt(grad_norm, w2_ref[...]) * slope(pre, sig)).astype(BF)
-        hiddens.append(hidden)
+        grad_norm = norm_back(*scaled(centred_ref[here, :]), message_grad).astype(BF)
+        grad_pre = (nt(grad_norm, w2_ref[...]) * slope_ref[here, :]).astype(BF)
         grad_norms.append(grad_norm)
         grad_pres.append(grad_pre)
     grad_pre = jnp.concatenate(grad_pres, axis=0)
     grad_pre_ref[...] = grad_pre
-    gw2[...] += tn(jnp.concatenate(hiddens, axis=0), jnp.concatenate(grad_norms, axis=0))
+    gw2[...] += tn(hidden_ref[...], jnp.concatenate(grad_norms, axis=0))
     stacked = jnp.concatenate([src_ref[...], tgt_ref[0], edges_ref[...]], axis=1)
     gw1[...] += tn(stacked, grad_pre)
     source = source_ref[...] - rows
@@ -519,6 +537,12 @@
         + [pl.BlockSpec(memory_space=pltpu.VMEM)] * (2 + groups),
         flops=10**9, bytes_accessed=10**6, name="pool", vmem=16,
     )
+    slopes = call(
+        slopes_kernel,
+        [shape((size, latent), kind) for size in (edges, rows) for kind in (F32, BF, F32)],
+        pre, edge_w_two, node_features, summed, node_w_one, node_w_two,
+        flops=10**9, bytes_accessed=10**7, name="slopes",
+    )
     got = [send[0]] + [
         lax.ppermute(send[ahead], "group", turned(-ahead)) for ahead in range(1, groups)
     ]
@@ -546,11 +570,12 @@
     grad_pre, node_local, joint = call(
         edge_back_kernel,
         [shape((edges, latent), BF), shape((rows, latent), F32), shape(joint_shape, BF)],
-        source, target, pre, src_rows, own_rows, edge_features, edge_cotangent, edge_w_one, edge_w_two,
+        *slopes[3:], source, target, *slopes[:3], src_rows, own_rows, edge_features, edge_cotangent, edge_w_one, edge_w_two,
         goal, node_cotangent, node_features, summed, node_w_one, node_w_two,
         grad_c_one, grad_c_two, *returned,
         grid=grid,
-        in_specs=[index_spec, index_spec, edge_spec, edge_spec,
+        in_specs=[whole((rows, latent))] * 3
+        + [index_spec, index_spec] + [edge_spec] * 4 + [
                   pl.BlockSpec((1, edges, latent), lambda i: (1, 0, 0)), edge_spec, edge_spec,
                   whole((3 * latent, latent)), whole((latent, latent)),
                   whole((1, rows)),

time: 110 us -> 111 us (level)
  Pallas kernels: 32.5 us -> 34.4 us
    pallas_call x14 -> x15, Pallas kernels: 32.5 us -> 34.4 us  [call(): pl.pallas_call(kernel, out_shape=out_shapes if single else list(out_shape...]
    ppermute x3, waiting for transfers between devices: 2.98 us -> 1.64 us  [local(): lax.ppermute(coarse_back, 'group', turned(ahead))]
    unnamed x57 -> x47, local copies, waits for them, and re-layouts: 7.41 us -> 6.5 us
  transfers between devices with their start and end apart: 16 -> 16, of which waited for: 12 -> 11; matrix products, arithmetic and copies ran while one was open for 0% -> 0% of each run, Pallas kernels for 16% -> 17%
where the time goes in v7:
time: 111 us; the launch traced here: 110 us
  starting transfers between devices  44.3 us (40%)
  Pallas kernels  34.4 us (31%)
  waiting for transfers between devices  23.8 us (21%)
  local copies, waits for them, and re-layouts  6.5 us (6%)
    pallas_call x15, Pallas kernels, call(): pl.pallas_call(kernel, out_shape=out_shapes if single else list(out_shape...  34.4 us
    all_to_all x1, waiting for transfers between devices, local(): pack_all = exchange(pack_sum, 'dom').reshape(pack_rows, latent)  8.96 us
    all_to_all x1, starting transfers between devices, local(): exchange(spread.reshape(domains, slots, latent), 'dom')  8.59 us
    all_to_all x1, starting transfers between devices, local(): exchange(joint, 'dom')  7.4 us
    unnamed x47, local copies, waits for them, and re-layouts  6.5 us
    all_to_all x1, starting transfers between devices, local(): exchange(share.reshape(domains, slots, latent), 'dom')  6.16 us
    ppermute x3, starting transfers between devices, local(): lax.ppermute(send[ahead], 'group', turned(-ahead))  5.74 us
    all_to_all x1, starting transfers between devices, local(): pack_all = exchange(pack_sum, 'dom').reshape(pack_rows, latent)  5.23 us
  transfers between devices with their start and end apart: 16, of which 11 were waited for; matrix products, arithmetic and copies ran while one was open for 0% of the time, Pallas kernels for 17%

profile of v7, /device:TPU:1, one launch (start us, length us, event | category | flops | bytes accessed | tf_op | source)
XLA Modules:
  0.0 110.0 jit_solution(3174270878736814456)
XLA Ops:
  2.4 8.6 %all-to-all-start = ((bf16[32,16,128]{2,1,0:T(8,128)(2,1)}), bf16[32,16,128]{2,1,0:T(8,128)(2,1)S(1)}, u32[]{:S(2)}, u32[]{:S(2)}) async-start(bf16[32,16,128]{2,1,0:T(8,128)(2,1)} %bitcast), calls=%async_computation | async-start | bytes 262144 | tf_op jit(solution)/shard_map/all_to_all | solution.py:488
  11.0 4.9 %edge_first.1.own_ref.tgt_ref = bf16[2,4096,128]{2,1,0:T(8,128)(2,1)} custom-call(s32[1,4096]{1,0:T(1,128)} %bitcast.13, s32[1,4096]{1,0:T(1,128)} %bitcast.17, bf16[1024,128]{1,0:T(8,128)(2,1)} %nodes_ref.9), custom_call_target="tpu_custom_call" | custom-call | flops 4000000000 | bytes 3000000 | tf_op jit(solution)/shard_map/edge_first/pallas_call | solution.py:441
  15.9 1.4 %order.1 = (bf16[528,128]{1,0:T(8,128)(2,1)S(1)}, bf16[528,128]{1,0:T(8,128)(2,1)S(1)}, bf16[528,128]{1,0:T(8,128)(2,1)S(1)}, bf16[528,128]{1,0:T(8,128)(2,1)S(1)}) custom-call(s32[1,1]{1,0:T(1,128)} %bitcast.4.group_ref, s32[1,4]{1,0:T(1,128)S(1)} %copy-done.17, s32[1,1024]{1,0:T(1,128)S(1)} %copy-done.15, s32[4,512]{1,0:T(4,128)S(1)} %bitcast.21, ...), custom_call_target="tpu_custom_call" | custom-call | flops 1000000000 | bytes 1000000 | tf_op jit(solution)/shard_map/order/pallas_call | solution.py:441
  17.4 1.3 %all-to-all-done = bf16[32,16,128]{2,1,0:T(8,128)(2,1)S(1)} async-done(((bf16[32,16,128]{2,1,0:T(8,128)(2,1)}), bf16[32,16,128]{2,1,0:T(8,128)(2,1)S(1)}, u32[]{:S(2)}, u32[]{:S(2)}) %all-to-all-start) | async-done | bytes 131104 | tf_op jit(solution)/shard_map/all_to_all | solution.py:488
  19.9 6.2 %all-to-all-start.1 = ((bf16[32,16,128]{2,1,0:T(8,128)(2,1)}), bf16[32,16,128]{2,1,0:T(8,128)(2,1)S(1)}, u32[]{:S(2)}, u32[]{:S(2)}) async-start(bf16[32,16,128]{2,1,0:T(8,128)(2,1)} %bitcast.6), calls=%async_computation.1 | async-start | bytes 262144 | tf_op jit(solution)/shard_map/all_to_all | solution.py:517
  26.1 3.8 %collective-permute-start = (bf16[528,128]{1,0:T(8,128)(2,1)S(1)}, bf16[528,128]{1,0:T(8,128)(2,1)S(1)}, u32[]{:S(2)}, u32[]{:S(2)}) collective-permute-start(bf16[528,128]{1,0:T(8,128)(2,1)S(1)} %get-tuple-element.83), channel_id=1, source_target_pairs={{0,96},{32,0},{64,32},{96,64},{1,97},{33,1},{65,33},{97,65},{2,98}... | collective-permute-start | bytes 405512 | tf_op jit(solution)/shard_map/ppermute | solution.py:515
  30.6 3.2 %all-to-all-done.1 = bf16[32,16,128]{2,1,0:T(8,128)(2,1)S(1)} async-done(((bf16[32,16,128]{2,1,0:T(8,128)(2,1)}), bf16[32,16,128]{2,1,0:T(8,128)(2,1)S(1)}, u32[]{:S(2)}, u32[]{:S(2)}) %all-to-all-start.1) | async-done | bytes 131104 | tf_op jit(solution)/shard_map/all_to_all | solution.py:517
  33.9 1.6 %copy-done.18 = bf16[2,4096,128]{2,1,0:T(8,128)(2,1)S(1)} copy-done((bf16[2,4096,128]{2,1,0:T(8,128)(2,1)S(1)}, bf16[2,4096,128]{2,1,0:T(8,128)(2,1)}, u32[]{:S(2)}) %copy-start.18) | copy-done | bytes 2097176
  35.4 4.7 %edge_second.1 = (f32[4096,128]{1,0:T(8,128)S(1)}, bf16[4096,128]{1,0:T(8,128)(2,1)S(1)}, bf16[1024,128]{1,0:T(8,128)(2,1)S(1)}, bf16[1024,128]{1,0:T(8,128)(2,1)S(1)}) custom-call(s32[1,4096]{1,0:T(1,128)S(1)} %bitcast.14, s32[1,4096]{1,0:T(1,128)S(1)} %bitcast.18, bf16[2,4096,128]{2,1,0:T(8,128)(2,1)S(1)} %copy-done.18, bf16[4096,128]{1,0:T(8,128)(2,1)S(1)} %copy-done.4, ...), custom_call_target="tpu_custom_call" | custom-call | flops 5000000000 | bytes 8000000 | tf_op jit(solution)/shard_map/edge_second/pallas_call | solution.py:441
  40.2 1.9 %pool.1 = (s32[1,1024]{1,0:T(1,128)S(1)}, bf16[256,128]{1,0:T(8,128)(2,1)S(1)}, bf16[256,128]{1,0:T(8,128)(2,1)S(1)}, bf16[256,128]{1,0:T(8,128)(2,1)S(1)}, bf16[256,128]{1,0:T(8,128)(2,1)S(1)}) custom-call(s32[1,1]{1,0:T(1,128)} %bitcast.4.group_ref, s32[1,4]{1,0:T(1,128)S(1)} %copy-done.17, s32[1,1024]{1,0:T(1,128)S(1)} %copy-done.15, ...), custom_call_target="tpu_custom_call" | custom-call | flops 1000000000 | bytes 1000000 | tf_op jit(solution)/shard_map/pool/pallas_call | solution.py:441
  42.2 1.7 %collective-permute-start.3 = (bf16[256,128]{1,0:T(8,128)(2,1)S(1)}, bf16[256,128]{1,0:T(8,128)(2,1)S(1)}, u32[]{:S(2)}, u32[]{:S(2)}) collective-permute-start(bf16[256,128]{1,0:T(8,128)(2,1)S(1)} %get-tuple-element.88), channel_id=1, source_target_pairs={{0,32},{32,64},{64,96},{96,0},{1,33},{33,65},{65,97},{97,1},{2,34}... | collective-permute-start | bytes 196616 | tf_op jit(solution)/shard_map/ppermute | solution.py:547
  43.9 3.3 %collective-permute-start.4 = (bf16[256,128]{1,0:T(8,128)(2,1)S(1)}, bf16[256,128]{1,0:T(8,128)(2,1)S(1)}, u32[]{:S(2)}, u32[]{:S(2)}) collective-permute-start(bf16[256,128]{1,0:T(8,128)(2,1)S(1)} %get-tuple-element.89), channel_id=1, source_target_pairs={{0,64},{32,96},{64,0},{96,32},{1,65},{33,97},{65,1},{97,33},{2,66}... | collective-permute-start | bytes 196616 | tf_op jit(solution)/shard_map/ppermute | solution.py:547
  48.4 1.7 %collective-permute-done.4.refs_2_ = bf16[256,128]{1,0:T(8,128)(2,1)S(1)} collective-permute-done((bf16[256,128]{1,0:T(8,128)(2,1)S(1)}, bf16[256,128]{1,0:T(8,128)(2,1)S(1)}, u32[]{:S(2)}, u32[]{:S(2)}) %collective-permute-start.4) | collective-permute-done | bytes 65568 | tf_op jit(solution)/shard_map/ppermute | solution.py:547
  50.6 1.3 %coarse.1 = (f32[256,128]{1,0:T(8,128)}, bf16[256,128]{1,0:T(8,128)(2,1)S(1)}, f32[256,128]{1,0:T(8,128)S(1)}, f32[128,128]{1,0:T(8,128)S(1)}) custom-call(bf16[256,128]{1,0:T(8,128)(2,1)S(1)} %copy-done, bf16[256,128]{1,0:T(8,128)(2,1)S(1)} %copy-done.1, f32[256,128]{1,0:T(8,128)S(1)} %cot_pool.1.from_fine_ref, bf16[256,128]{1,0:T(8,128)(2,1)S(1)} %copy-done.2, ...), custom_call_target="tpu_custom_call" | custom-call | flops 100000000 | bytes 1000000 | tf_op jit(solution)/shard_map/coarse/pallas_call | solution.py:441
  52.4 2.3 %collective-permute-start.7 = (bf16[256,128]{1,0:T(8,128)(2,1)S(1)}, bf16[256,128]{1,0:T(8,128)(2,1)S(1)}, u32[]{:S(2)}, u32[]{:S(2)}) collective-permute-start(bf16[256,128]{1,0:T(8,128)(2,1)S(1)} %get-tuple-element.98.rest_0_), channel_id=1, source_target_pairs={{0,64},{32,96},{64,0},{96,32},{1,65},{33,97},{65,1},{97,33},{2,66}... | collective-permute-start | bytes 196616 | tf_op jit(solution)/shard_map/ppermute | solution.py:564
  55.2 1.3 %slopes.1 = (f32[4096,128]{1,0:T(8,128)S(1)}, bf16[4096,128]{1,0:T(8,128)(2,1)S(1)}, f32[4096,128]{1,0:T(8,128)S(1)}, f32[1024,128]{1,0:T(8,128)S(1)}, bf16[1024...) custom-call(f32[4096,128]{1,0:T(8,128)S(1)} %get-tuple-element.72.pre_ref, bf16[128,128]{1,0:T(8,128)(2,1)S(1)} %copy-done.10, ...), custom_call_target="tpu_custom_call" | custom-call | flops 1000000000 | bytes 10000000 | tf_op jit(solution)/shard_map/slopes/pallas_call | solution.py:441
  58.2 8.5 %edge_back.1 = (bf16[4096,128]{1,0:T(8,128)(2,1)S(1)}, f32[1024,128]{1,0:T(8,128)S(1)}, bf16[32,64,128]{2,1,0:T(8,128)(2,1)}) custom-call(f32[1024,128]{1,0:T(8,128)S(1)} %get-tuple-element.74.node_slope_ref, bf16[1024,128]{1,0:T(8,128)(2,1)S(1)} %get-tuple-element.75.node_hidden_ref, f32[1024,128]{1,0:T(8,128)S(1)} %get-tuple-element.76.node_centred_ref, ...), custom_call_target="tpu_custom_call" | custom-call | flops 6000000000 | bytes 10000000 | tf_op jit(solution)/shard_map/edge_back/pallas_call | solution.py:441
  68.4 7.4 %all-to-all-start.2 = ((bf16[32,64,128]{2,1,0:T(8,128)(2,1)}), bf16[32,64,128]{2,1,0:T(8,128)(2,1)S(1)}, u32[]{:S(2)}, u32[]{:S(2)}) async-start(bf16[32,64,128]{2,1,0:T(8,128)(2,1)} %get-tuple-element.99), calls=%async_computation.2 | async-start | bytes 1048576 | tf_op jit(solution)/shard_map/all_to_all | solution.py:605
  78.1 4.7 %own_back.1 = (f32[1024,128]{1,0:T(8,128)S(1)}, f32[4096,128]{1,0:T(8,128)}) custom-call(s32[1,4096]{1,0:T(1,128)S(1)} %bitcast.16, s32[1,4096]{1,0:T(1,128)S(1)} %bitcast.20, bf16[4096,128]{1,0:T(8,128)(2,1)S(1)} %copy-done.20, bf16[4096,128]{1,0:T(8,128)(2,1)S(1)} %copy-done.5, f32[1024,128]{1,0:T(8,128)S(1)} %copy-done.22, bf16[384,128]{1,0:T(8,128)(2,1)S(1)} %copy-done.8), custom_call_target="tpu_custom_call" | custom-call | flops 4000000000 | bytes 5000000 | tf_op jit(solution)/shard_map/own_back/pallas_call | solution.py:441
  82.8 4.6 %all-to-all-done.2.got_ref = bf16[32,64,128]{2,1,0:T(8,128)(2,1)S(1)} async-done(((bf16[32,64,128]{2,1,0:T(8,128)(2,1)}), bf16[32,64,128]{2,1,0:T(8,128)(2,1)S(1)}, u32[]{:S(2)}, u32[]{:S(2)}) %all-to-all-start.2) | async-done | bytes 524320 | tf_op jit(solution)/shard_map/all_to_all | solution.py:605
  87.6 2.5 %collective-permute-start.10 = (f32[48,128]{1,0:T(8,128)S(1)}, f32[48,128]{1,0:T(8,128)S(1)}, u32[]{:S(2)}, u32[]{:S(2)}) collective-permute-start(f32[48,128]{1,0:T(8,128)S(1)} %add_parts.1.refs_0_), channel_id=1, source_target_pairs={{0,64},{32,96},{64,0},{96,32},{1,65},{33,97},{65,1},{97,33},{2,66}... | collective-permute-start | bytes 73736 | tf_op jit(solution)/shard_map/ppermute | solution.py:611
  93.6 5.2 %all-to-all-start.3 = ((bf16[32,48,128]{2,1,0:T(8,128)(2,1)}), bf16[32,48,128]{2,1,0:T(8,128)(2,1)S(1)}, u32[]{:S(2)}, u32[]{:S(2)}) async-start(bf16[32,48,128]{2,1,0:T(8,128)(2,1)} %add_groups.1), calls=%async_computation.3 | async-start | bytes 786432 | tf_op jit(solution)/shard_map/all_to_all | solution.py:617
  98.8 1.3 %add_back.1 = f32[1024,128]{1,0:T(8,128)} custom-call(s32[1,256]{1,0:T(1,128)S(1)} %copy-done.16, bf16[512,128]{1,0:T(8,128)(2,1)S(1)} %bitcast.11, bf16[32,64,128]{2,1,0:T(8,128)(2,1)S(1)} %all-to-all-done.2.got_ref, f32[1024,128]{1,0:T(8,128)S(1)} %get-tuple-element.104.local_ref), custom_call_target="tpu_custom_call" | custom-call | flops 1000000000 | bytes 1000000 | tf_op jit(solution)/shard_map/add_back/pallas_call | solution.py:441
  100.2 9.0 %all-to-all-done.3 = bf16[32,48,128]{2,1,0:T(8,128)(2,1)S(1)} async-done(((bf16[32,48,128]{2,1,0:T(8,128)(2,1)}), bf16[32,48,128]{2,1,0:T(8,128)(2,1)S(1)}, u32[]{:S(2)}, u32[]{:S(2)}) %all-to-all-start.3) | async-done | bytes 393248 | tf_op jit(solution)/shard_map/all_to_all | solution.py:617
  (70 shorter events, 16.6 us)
Async XLA Ops:
  2.4 16.3 %all-to-all-start = ((bf16[32,16,128]{2,1,0:T(8,128)(2,1)}), bf16[32,16,128]{2,1,0:T(8,128)(2,1)S(1)}, u32[]{:S(2)}, u32[]{:S(2)}) async-start(bf16[32,16,128]{2,1,0:T(8,128)(2,1)} %bitcast), calls=%async_computation | async-start | bytes 262144 | tf_op jit(solution)/shard_map/all_to_all | solution.py:488
  17.3 16.5 %copy-start.4 = (bf16[4096,128]{1,0:T(8,128)(2,1)S(1)}, bf16[4096,128]{1,0:T(8,128)(2,1)}, u32[]{:S(2)}) copy-start(bf16[4096,128]{1,0:T(8,128)(2,1)} %edges_ref.3) | copy-start | bytes 3145732
  17.3 16.4 %copy-start.8 = (bf16[384,128]{1,0:T(8,128)(2,1)S(1)}, bf16[384,128]{1,0:T(8,128)(2,1)}, u32[]{:S(2)}) copy-start(bf16[384,128]{1,0:T(8,128)(2,1)} %w1_ref.7) | copy-start | bytes 294916
  17.4 16.4 %copy-start.9 = (bf16[256,128]{1,0:T(8,128)(2,1)S(1)}, bf16[256,128]{1,0:T(8,128)(2,1)}, u32[]{:S(2)}) copy-start(bf16[256,128]{1,0:T(8,128)(2,1)} %v1_ref.5) | copy-start | bytes 196612
  17.4 16.4 %copy-start.10 = (bf16[128,128]{1,0:T(8,128)(2,1)S(1)}, bf16[128,128]{1,0:T(8,128)(2,1)}, u32[]{:S(2)}) copy-start(bf16[128,128]{1,0:T(8,128)(2,1)} %w2_ref.7) | copy-start | bytes 98308
  17.4 16.4 %copy-start.11 = (bf16[128,128]{1,0:T(8,128)(2,1)S(1)}, bf16[128,128]{1,0:T(8,128)(2,1)}, u32[]{:S(2)}) copy-start(bf16[128,128]{1,0:T(8,128)(2,1)} %v2_ref.5) | copy-start | bytes 98308
  17.4 16.4 %copy-start.12 = (s32[4096]{0:T(1024)S(1)}, s32[4096]{0:T(1024)}, u32[]{:S(2)}) copy-start(s32[4096]{0:T(1024)} %param.28) | copy-start | bytes 49156
  17.4 16.4 %copy-start.13 = (s32[4096]{0:T(1024)S(1)}, s32[4096]{0:T(1024)}, u32[]{:S(2)}) copy-start(s32[4096]{0:T(1024)} %param.29) | copy-start | bytes 49156
  19.9 13.9 %all-to-all-start.1 = ((bf16[32,16,128]{2,1,0:T(8,128)(2,1)}), bf16[32,16,128]{2,1,0:T(8,128)(2,1)S(1)}, u32[]{:S(2)}, u32[]{:S(2)}) async-start(bf16[32,16,128]{2,1,0:T(8,128)(2,1)} %bitcast.6), calls=%async_computation.1 | async-start | bytes 262144 | tf_op jit(solution)/shard_map/all_to_all | solution.py:517
  26.1 14.1 %collective-permute-start = (bf16[528,128]{1,0:T(8,128)(2,1)S(1)}, bf16[528,128]{1,0:T(8,128)(2,1)S(1)}, u32[]{:S(2)}, u32[]{:S(2)}) collective-permute-start(bf16[528,128]{1,0:T(8,128)(2,1)S(1)} %get-tuple-element.83), channel_id=1, source_target_pairs={{0,96},{32,0},{64,32},{96,64},{1,97},{33,1},{65,33},{97,65},{2,98}... | collective-permute-start | bytes 405512 | tf_op jit(solution)/shard_map/ppermute | solution.py:515
  29.9 10.3 %collective-permute-start.1 = (bf16[528,128]{1,0:T(8,128)(2,1)S(1)}, bf16[528,128]{1,0:T(8,128)(2,1)S(1)}, u32[]{:S(2)}, u32[]{:S(2)}) collective-permute-start(bf16[528,128]{1,0:T(8,128)(2,1)S(1)} %get-tuple-element.84), channel_id=1, source_target_pairs={{0,64},{32,96},{64,0},{96,32},{1,65},{33,97},{65,1},{97,33},{2,66}... | collective-permute-start | bytes 405512 | tf_op jit(solution)/shard_map/ppermute | solution.py:515
  29.9 10.3 %collective-permute-start.2 = (bf16[528,128]{1,0:T(8,128)(2,1)S(1)}, bf16[528,128]{1,0:T(8,128)(2,1)S(1)}, u32[]{:S(2)}, u32[]{:S(2)}) collective-permute-start(bf16[528,128]{1,0:T(8,128)(2,1)S(1)} %get-tuple-element.85), channel_id=1, source_target_pairs={{0,32},{32,64},{64,96},{96,0},{1,33},{33,65},{65,97},{97,1},{2,34}... | collective-permute-start | bytes 405512 | tf_op jit(solution)/shard_map/ppermute | solution.py:515
  42.1 8.5 %copy-start = (bf16[256,128]{1,0:T(8,128)(2,1)S(1)}, bf16[256,128]{1,0:T(8,128)(2,1)}, u32[]{:S(2)}) copy-start(bf16[256,128]{1,0:T(8,128)(2,1)} %feat_ref.1) | copy-start | bytes 196612
  42.2 6.2 %collective-permute-start.3 = (bf16[256,128]{1,0:T(8,128)(2,1)S(1)}, bf16[256,128]{1,0:T(8,128)(2,1)S(1)}, u32[]{:S(2)}, u32[]{:S(2)}) collective-permute-start(bf16[256,128]{1,0:T(8,128)(2,1)S(1)} %get-tuple-element.88), channel_id=1, source_target_pairs={{0,32},{32,64},{64,96},{96,0},{1,33},{33,65},{65,97},{97,1},{2,34}... | collective-permute-start | bytes 196616 | tf_op jit(solution)/shard_map/ppermute | solution.py:547
  43.9 6.2 %collective-permute-start.4 = (bf16[256,128]{1,0:T(8,128)(2,1)S(1)}, bf16[256,128]{1,0:T(8,128)(2,1)S(1)}, u32[]{:S(2)}, u32[]{:S(2)}) collective-permute-start(bf16[256,128]{1,0:T(8,128)(2,1)S(1)} %get-tuple-element.89), channel_id=1, source_target_pairs={{0,64},{32,96},{64,0},{96,32},{1,65},{33,97},{65,1},{97,33},{2,66}... | collective-permute-start | bytes 196616 | tf_op jit(solution)/shard_map/ppermute | solution.py:547
  47.2 3.4 %collective-permute-start.5 = (bf16[256,128]{1,0:T(8,128)(2,1)S(1)}, bf16[256,128]{1,0:T(8,128)(2,1)S(1)}, u32[]{:S(2)}, u32[]{:S(2)}) collective-permute-start(bf16[256,128]{1,0:T(8,128)(2,1)S(1)} %get-tuple-element.90), channel_id=1, source_target_pairs={{0,96},{32,0},{64,32},{96,64},{1,97},{33,1},{65,33},{97,65},{2,98}... | collective-permute-start | bytes 196616 | tf_op jit(solution)/shard_map/ppermute | solution.py:547
  51.9 4.6 %collective-permute-start.8 = (bf16[256,128]{1,0:T(8,128)(2,1)S(1)}, bf16[256,128]{1,0:T(8,128)(2,1)S(1)}, u32[]{:S(2)}, u32[]{:S(2)}) collective-permute-start(bf16[256,128]{1,0:T(8,128)(2,1)S(1)} %get-tuple-element.98.rest_0_), channel_id=1, source_target_pairs={{0,32},{32,64},{64,96},{96,0},{1,33},{33,65},{65,97},{97,1},{2,34}... | collective-permute-start | bytes 196616 | tf_op jit(solution)/shard_map/ppermute | solution.py:564
  52.4 4.7 %collective-permute-start.7 = (bf16[256,128]{1,0:T(8,128)(2,1)S(1)}, bf16[256,128]{1,0:T(8,128)(2,1)S(1)}, u32[]{:S(2)}, u32[]{:S(2)}) collective-permute-start(bf16[256,128]{1,0:T(8,128)(2,1)S(1)} %get-tuple-element.98.rest_0_), channel_id=1, source_target_pairs={{0,64},{32,96},{64,0},{96,32},{1,65},{33,97},{65,1},{97,33},{2,66}... | collective-permute-start | bytes 196616 | tf_op jit(solution)/shard_map/ppermute | solution.py:564
  54.7 3.4 %collective-permute-start.6 = (bf16[256,128]{1,0:T(8,128)(2,1)S(1)}, bf16[256,128]{1,0:T(8,128)(2,1)S(1)}, u32[]{:S(2)}, u32[]{:S(2)}) collective-permute-start(bf16[256,128]{1,0:T(8,128)(2,1)S(1)} %get-tuple-element.98.rest_0_), channel_id=1, source_target_pairs={{0,96},{32,0},{64,32},{96,64},{1,97},{33,1},{65,33},{97,65},{2,98}... | collective-permute-start | bytes 196616 | tf_op jit(solution)/shard_map/ppermute | solution.py:564
  68.4 19.0 %all-to-all-start.2 = ((bf16[32,64,128]{2,1,0:T(8,128)(2,1)}), bf16[32,64,128]{2,1,0:T(8,128)(2,1)S(1)}, u32[]{:S(2)}, u32[]{:S(2)}) async-start(bf16[32,64,128]{2,1,0:T(8,128)(2,1)} %get-tuple-element.99), calls=%async_computation.2 | async-start | bytes 1048576 | tf_op jit(solution)/shard_map/all_to_all | solution.py:605
  87.5 4.0 %collective-permute-start.11 = (f32[48,128]{1,0:T(8,128)S(1)}, f32[48,128]{1,0:T(8,128)S(1)}, u32[]{:S(2)}, u32[]{:S(2)}) collective-permute-start(f32[48,128]{1,0:T(8,128)S(1)} %add_parts.1.refs_0_), channel_id=1, source_target_pairs={{0,32},{32,64},{64,96},{96,0},{1,33},{33,65},{65,97},{97,1},{2,34}... | collective-permute-start | bytes 73736 | tf_op jit(solution)/shard_map/ppermute | solution.py:611
  87.6 4.4 %collective-permute-start.10 = (f32[48,128]{1,0:T(8,128)S(1)}, f32[48,128]{1,0:T(8,128)S(1)}, u32[]{:S(2)}, u32[]{:S(2)}) collective-permute-start(f32[48,128]{1,0:T(8,128)S(1)} %add_parts.1.refs_0_), channel_id=1, source_target_pairs={{0,64},{32,96},{64,0},{96,32},{1,65},{33,97},{65,1},{97,33},{2,66}... | collective-permute-start | bytes 73736 | tf_op jit(solution)/shard_map/ppermute | solution.py:611
  90.1 2.8 %collective-permute-start.9 = (f32[48,128]{1,0:T(8,128)S(1)}, f32[48,128]{1,0:T(8,128)S(1)}, u32[]{:S(2)}, u32[]{:S(2)}) collective-permute-start(f32[48,128]{1,0:T(8,128)S(1)} %add_parts.1.refs_0_), channel_id=1, source_target_pairs={{0,96},{32,0},{64,32},{96,64},{1,97},{33,1},{65,33},{97,65},{2,98}... | collective-permute-start | bytes 73736 | tf_op jit(solution)/shard_map/ppermute | solution.py:611
  93.6 15.5 %all-to-all-start.3 = ((bf16[32,48,128]{2,1,0:T(8,128)(2,1)}), bf16[32,48,128]{2,1,0:T(8,128)(2,1)S(1)}, u32[]{:S(2)}, u32[]{:S(2)}) async-start(bf16[32,48,128]{2,1,0:T(8,128)(2,1)} %add_groups.1), calls=%async_computation.3 | async-start | bytes 786432 | tf_op jit(solution)/shard_map/all_to_all | solution.py:617
  (15 other events, 63.8 us)

commit v8 on v6

--- a/solution.py
+++ b/solution.py
@@ -465,7 +465,7 @@
     target = edge_target.reshape(1, edges)
     spread = call(
         spread_kernel, shape((ghosts, latent), BF), ghost_pos,
-        flops=10**6, bytes_accessed=10**5, name="spread", vmem=8,
+        flops=10**6, bytes_accessed=10**5, name="spread", vmem=61,
     )
     asked = exchange(spread.reshape(domains, slots, latent), "dom").reshape(ghosts, latent)
     slot_list = coarse_slot.reshape(groups, -1)

time: 110 us -> 111 us (level)
  no operation moved by 1% of the time
where the time goes in v8:
time: 111 us
  starting transfers between devices  44.3 us (40%)
  Pallas kernels  33.3 us (30%)
  waiting for transfers between devices  24.2 us (22%)
  local copies, waits for them, and re-layouts  8.02 us (7%)
    pallas_call x14, Pallas kernels, call(): pl.pallas_call(kernel, out_shape=out_shapes if single else list(out_shape...  33.3 us
    all_to_all x1, waiting for transfers between devices, local(): pack_all = exchange(pack_sum, 'dom').reshape(pack_rows, latent)  8.96 us
    all_to_all x1, starting transfers between devices, local(): exchange(spread.reshape(domains, slots, latent), 'dom')  8.59 us
    unnamed x57, local copies, waits for them, and re-layouts  8.02 us
    all_to_all x1, starting transfers between devices, local(): exchange(joint, 'dom')  7.38 us
    all_to_all x1, starting transfers between devices, local(): exchange(share.reshape(domains, slots, latent), 'dom')  6.16 us
    ppermute x3, starting transfers between devices, local(): lax.ppermute(send[ahead], 'group', turned(-ahead))  5.74 us
    all_to_all x1, starting transfers between devices, local(): pack_all = exchange(pack_sum, 'dom').reshape(pack_rows, latent)  5.23 us
  transfers between devices with their start and end apart: 16, of which 12 were waited for; matrix products, arithmetic and copies ran while one was open for 0% of the time, Pallas kernels for 16%

profile of v8, /device:TPU:1, one launch (start us, length us, event | category | flops | bytes accessed | tf_op | source)
XLA Modules:
  0.0 110.8 jit_solution(1267641173402853135)
XLA Ops:
  0.6 1.4 %copy.28.wanted_ref = s32[1,32,16]{2,1,0:T(8,128)} copy(s32[1,32,16]{1,2,0:T(8,128)} %param.31) | data formatting | bytes 4096 | tf_op args[12]
  2.0 1.7 %spread.1 = bf16[512,128]{1,0:T(8,128)(2,1)} custom-call(s32[1,32,16]{2,1,0:T(8,128)} %copy.28.wanted_ref), custom_call_target="tpu_custom_call" | custom-call | flops 1000000 | bytes 100000 | tf_op jit(solution)/shard_map/spread/pallas_call | solution.py:423
  3.7 8.6 %all-to-all-start = ((bf16[32,16,128]{2,1,0:T(8,128)(2,1)}), bf16[32,16,128]{2,1,0:T(8,128)(2,1)S(1)}, u32[]{:S(2)}, u32[]{:S(2)}) async-start(bf16[32,16,128]{2,1,0:T(8,128)(2,1)} %bitcast.23), calls=%async_computation | async-start | bytes 262144 | tf_op jit(solution)/shard_map/all_to_all | solution.py:470
  12.3 4.9 %edge_first.1.own_ref.tgt_ref = bf16[2,4096,128]{2,1,0:T(8,128)(2,1)} custom-call(s32[1,4096]{1,0:T(1,128)} %bitcast.13, s32[1,4096]{1,0:T(1,128)} %bitcast.17, bf16[1024,128]{1,0:T(8,128)(2,1)} %nodes_ref.7), custom_call_target="tpu_custom_call" | custom-call | flops 4000000000 | bytes 3000000 | tf_op jit(solution)/shard_map/edge_first/pallas_call | solution.py:423
  17.2 1.4 %order.1 = (bf16[528,128]{1,0:T(8,128)(2,1)S(1)}, bf16[528,128]{1,0:T(8,128)(2,1)S(1)}, bf16[528,128]{1,0:T(8,128)(2,1)S(1)}, bf16[528,128]{1,0:T(8,128)(2,1)S(1)}) custom-call(s32[1,1]{1,0:T(1,128)} %bitcast.4.group_ref, s32[1,4]{1,0:T(1,128)S(1)} %copy-done.20, s32[1,1024]{1,0:T(1,128)S(1)} %copy-done.18, s32[4,512]{1,0:T(4,128)S(1)} %bitcast.21, ...), custom_call_target="tpu_custom_call" | custom-call | flops 1000000000 | bytes 1000000 | tf_op jit(solution)/shard_map/order/pallas_call | solution.py:423
  18.8 1.2 %all-to-all-done = bf16[32,16,128]{2,1,0:T(8,128)(2,1)S(1)} async-done(((bf16[32,16,128]{2,1,0:T(8,128)(2,1)}), bf16[32,16,128]{2,1,0:T(8,128)(2,1)S(1)}, u32[]{:S(2)}, u32[]{:S(2)}) %all-to-all-start) | async-done | bytes 131104 | tf_op jit(solution)/shard_map/all_to_all | solution.py:470
  21.2 6.2 %all-to-all-start.1 = ((bf16[32,16,128]{2,1,0:T(8,128)(2,1)}), bf16[32,16,128]{2,1,0:T(8,128)(2,1)S(1)}, u32[]{:S(2)}, u32[]{:S(2)}) async-start(bf16[32,16,128]{2,1,0:T(8,128)(2,1)} %bitcast.6), calls=%async_computation.1 | async-start | bytes 262144 | tf_op jit(solution)/shard_map/all_to_all | solution.py:499
  27.4 3.8 %collective-permute-start = (bf16[528,128]{1,0:T(8,128)(2,1)S(1)}, bf16[528,128]{1,0:T(8,128)(2,1)S(1)}, u32[]{:S(2)}, u32[]{:S(2)}) collective-permute-start(bf16[528,128]{1,0:T(8,128)(2,1)S(1)} %get-tuple-element.70), channel_id=1, source_target_pairs={{0,96},{32,0},{64,32},{96,64},{1,97},{33,1},{65,33},{97,65},{2,98}... | collective-permute-start | bytes 405512 | tf_op jit(solution)/shard_map/ppermute | solution.py:497
  31.9 3.2 %all-to-all-done.1 = bf16[32,16,128]{2,1,0:T(8,128)(2,1)S(1)} async-done(((bf16[32,16,128]{2,1,0:T(8,128)(2,1)}), bf16[32,16,128]{2,1,0:T(8,128)(2,1)S(1)}, u32[]{:S(2)}, u32[]{:S(2)}) %all-to-all-start.1) | async-done | bytes 131104 | tf_op jit(solution)/shard_map/all_to_all | solution.py:499
  35.2 1.6 %copy-done.23 = bf16[2,4096,128]{2,1,0:T(8,128)(2,1)S(1)} copy-done((bf16[2,4096,128]{2,1,0:T(8,128)(2,1)S(1)}, bf16[2,4096,128]{2,1,0:T(8,128)(2,1)}, u32[]{:S(2)}) %copy-start.23) | copy-done | bytes 2097176
  36.8 4.7 %edge_second.1 = (f32[4096,128]{1,0:T(8,128)S(1)}, bf16[4096,128]{1,0:T(8,128)(2,1)S(1)}, bf16[1024,128]{1,0:T(8,128)(2,1)S(1)}, bf16[1024,128]{1,0:T(8,128)(2,1)S(1)}) custom-call(s32[1,4096]{1,0:T(1,128)S(1)} %bitcast.14, s32[1,4096]{1,0:T(1,128)S(1)} %bitcast.18, bf16[2,4096,128]{2,1,0:T(8,128)(2,1)S(1)} %copy-done.23, bf16[4096,128]{1,0:T(8,128)(2,1)S(1)} %copy-done.4, ...), custom_call_target="tpu_custom_call" | custom-call | flops 5000000000 | bytes 8000000 | tf_op jit(solution)/shard_map/edge_second/pallas_call | solution.py:423
  41.5 1.9 %pool.1 = (s32[1,1024]{1,0:T(1,128)S(1)}, bf16[256,128]{1,0:T(8,128)(2,1)S(1)}, bf16[256,128]{1,0:T(8,128)(2,1)S(1)}, bf16[256,128]{1,0:T(8,128)(2,1)S(1)}, bf16[256,128]{1,0:T(8,128)(2,1)S(1)}) custom-call(s32[1,1]{1,0:T(1,128)} %bitcast.4.group_ref, s32[1,4]{1,0:T(1,128)S(1)} %copy-done.20, s32[1,1024]{1,0:T(1,128)S(1)} %copy-done.18, ...), custom_call_target="tpu_custom_call" | custom-call | flops 1000000000 | bytes 1000000 | tf_op jit(solution)/shard_map/pool/pallas_call | solution.py:423
  43.5 1.7 %collective-permute-start.3 = (bf16[256,128]{1,0:T(8,128)(2,1)S(1)}, bf16[256,128]{1,0:T(8,128)(2,1)S(1)}, u32[]{:S(2)}, u32[]{:S(2)}) collective-permute-start(bf16[256,128]{1,0:T(8,128)(2,1)S(1)} %get-tuple-element.76), channel_id=1, source_target_pairs={{0,32},{32,64},{64,96},{96,0},{1,33},{33,65},{65,97},{97,1},{2,34}... | collective-permute-start | bytes 196616 | tf_op jit(solution)/shard_map/ppermute | solution.py:523
  45.2 3.3 %collective-permute-start.4 = (bf16[256,128]{1,0:T(8,128)(2,1)S(1)}, bf16[256,128]{1,0:T(8,128)(2,1)S(1)}, u32[]{:S(2)}, u32[]{:S(2)}) collective-permute-start(bf16[256,128]{1,0:T(8,128)(2,1)S(1)} %get-tuple-element.77), channel_id=1, source_target_pairs={{0,64},{32,96},{64,0},{96,32},{1,65},{33,97},{65,1},{97,33},{2,66}... | collective-permute-start | bytes 196616 | tf_op jit(solution)/shard_map/ppermute | solution.py:523
  52.0 1.3 %coarse.1 = (f32[256,128]{1,0:T(8,128)}, bf16[256,128]{1,0:T(8,128)(2,1)S(1)}, f32[256,128]{1,0:T(8,128)S(1)}, f32[128,128]{1,0:T(8,128)S(1)}) custom-call(bf16[256,128]{1,0:T(8,128)(2,1)S(1)} %copy-done, bf16[256,128]{1,0:T(8,128)(2,1)S(1)} %copy-done.1, f32[256,128]{1,0:T(8,128)S(1)} %cot_pool.1.from_fine_ref, bf16[256,128]{1,0:T(8,128)(2,1)S(1)} %copy-done.2, ...), custom_call_target="tpu_custom_call" | custom-call | flops 100000000 | bytes 1000000 | tf_op jit(solution)/shard_map/coarse/pallas_call | solution.py:423
  53.8 2.3 %collective-permute-start.7 = (bf16[256,128]{1,0:T(8,128)(2,1)S(1)}, bf16[256,128]{1,0:T(8,128)(2,1)S(1)}, u32[]{:S(2)}, u32[]{:S(2)}) collective-permute-start(bf16[256,128]{1,0:T(8,128)(2,1)S(1)} %get-tuple-element.86.rest_0_), channel_id=1, source_target_pairs={{0,64},{32,96},{64,0},{96,32},{1,65},{33,97},{65,1},{97,33},{2,66}... | collective-permute-start | bytes 196616 | tf_op jit(solution)/shard_map/ppermute | solution.py:540
  59.5 7.9 %edge_back.1 = (bf16[4096,128]{1,0:T(8,128)(2,1)S(1)}, f32[1024,128]{1,0:T(8,128)S(1)}, bf16[32,64,128]{2,1,0:T(8,128)(2,1)}) custom-call(s32[1,4096]{1,0:T(1,128)S(1)} %bitcast.15, s32[1,4096]{1,0:T(1,128)S(1)} %bitcast.19, f32[4096,128]{1,0:T(8,128)S(1)} %get-tuple-element.66.pre_ref, bf16[4096,128]{1,0:T(8,128)(2,1)S(1)} %get-tuple-element.67.src_ref, ...), custom_call_target="tpu_custom_call" | custom-call | flops 6000000000 | bytes 10000000 | tf_op jit(solution)/shard_map/edge_back/pallas_call | solution.py:423
  69.2 7.4 %all-to-all-start.2 = ((bf16[32,64,128]{2,1,0:T(8,128)(2,1)}), bf16[32,64,128]{2,1,0:T(8,128)(2,1)S(1)}, u32[]{:S(2)}, u32[]{:S(2)}) async-start(bf16[32,64,128]{2,1,0:T(8,128)(2,1)} %get-tuple-element.87), calls=%async_computation.2 | async-start | bytes 1048576 | tf_op jit(solution)/shard_map/all_to_all | solution.py:580
  78.9 4.7 %own_back.1 = (f32[1024,128]{1,0:T(8,128)S(1)}, f32[4096,128]{1,0:T(8,128)}) custom-call(s32[1,4096]{1,0:T(1,128)S(1)} %bitcast.16, s32[1,4096]{1,0:T(1,128)S(1)} %bitcast.20, bf16[4096,128]{1,0:T(8,128)(2,1)S(1)} %copy-done.25, bf16[4096,128]{1,0:T(8,128)(2,1)S(1)} %copy-done.5, f32[1024,128]{1,0:T(8,128)S(1)} %copy-done.27, bf16[384,128]{1,0:T(8,128)(2,1)S(1)} %copy-done.8), custom_call_target="tpu_custom_call" | custom-call | flops 4000000000 | bytes 5000000 | tf_op jit(solution)/shard_map/own_back/pallas_call | solution.py:423
  83.6 4.6 %all-to-all-done.2.got_ref = bf16[32,64,128]{2,1,0:T(8,128)(2,1)S(1)} async-done(((bf16[32,64,128]{2,1,0:T(8,128)(2,1)}), bf16[32,64,128]{2,1,0:T(8,128)(2,1)S(1)}, u32[]{:S(2)}, u32[]{:S(2)}) %all-to-all-start.2) | async-done | bytes 524320 | tf_op jit(solution)/shard_map/all_to_all | solution.py:580
  88.4 2.5 %collective-permute-start.10 = (f32[48,128]{1,0:T(8,128)S(1)}, f32[48,128]{1,0:T(8,128)S(1)}, u32[]{:S(2)}, u32[]{:S(2)}) collective-permute-start(f32[48,128]{1,0:T(8,128)S(1)} %add_parts.1.refs_0_), channel_id=1, source_target_pairs={{0,64},{32,96},{64,0},{96,32},{1,65},{33,97},{65,1},{97,33},{2,66}... | collective-permute-start | bytes 73736 | tf_op jit(solution)/shard_map/ppermute | solution.py:586
  94.4 5.2 %all-to-all-start.3 = ((bf16[32,48,128]{2,1,0:T(8,128)(2,1)}), bf16[32,48,128]{2,1,0:T(8,128)(2,1)S(1)}, u32[]{:S(2)}, u32[]{:S(2)}) async-start(bf16[32,48,128]{2,1,0:T(8,128)(2,1)} %add_groups.1), calls=%async_computation.3 | async-start | bytes 786432 | tf_op jit(solution)/shard_map/all_to_all | solution.py:592
  99.7 1.3 %add_back.1 = f32[1024,128]{1,0:T(8,128)} custom-call(s32[1,256]{1,0:T(1,128)S(1)} %copy-done.19, bf16[512,128]{1,0:T(8,128)(2,1)S(1)} %bitcast.11, bf16[32,64,128]{2,1,0:T(8,128)(2,1)S(1)} %all-to-all-done.2.got_ref, f32[1024,128]{1,0:T(8,128)S(1)} %get-tuple-element.92.local_ref), custom_call_target="tpu_custom_call" | custom-call | flops 1000000000 | bytes 1000000 | tf_op jit(solution)/shard_map/add_back/pallas_call | solution.py:423
  101.0 9.0 %all-to-all-done.3 = bf16[32,48,128]{2,1,0:T(8,128)(2,1)S(1)} async-done(((bf16[32,48,128]{2,1,0:T(8,128)(2,1)}), bf16[32,48,128]{2,1,0:T(8,128)(2,1)S(1)}, u32[]{:S(2)}, u32[]{:S(2)}) %all-to-all-start.3) | async-done | bytes 393248 | tf_op jit(solution)/shard_map/all_to_all | solution.py:592
  (79 shorter events, 18.0 us)
Async XLA Ops:
  3.7 16.3 %all-to-all-start = ((bf16[32,16,128]{2,1,0:T(8,128)(2,1)}), bf16[32,16,128]{2,1,0:T(8,128)(2,1)S(1)}, u32[]{:S(2)}, u32[]{:S(2)}) async-start(bf16[32,16,128]{2,1,0:T(8,128)(2,1)} %bitcast.23), calls=%async_computation | async-start | bytes 262144 | tf_op jit(solution)/shard_map/all_to_all | solution.py:470
  18.7 22.9 %copy-start.21 = (bf16[528,128]{1,0:T(8,128)(2,1)}, bf16[528,128]{1,0:T(8,128)(2,1)S(1)}, u32[]{:S(2)}) copy-start(bf16[528,128]{1,0:T(8,128)(2,1)S(1)} %get-tuple-element.69.refs_0_) | copy-start | bytes 405508
  18.7 16.4 %copy-start.4 = (bf16[4096,128]{1,0:T(8,128)(2,1)S(1)}, bf16[4096,128]{1,0:T(8,128)(2,1)}, u32[]{:S(2)}) copy-start(bf16[4096,128]{1,0:T(8,128)(2,1)} %edges_ref.3) | copy-start | bytes 3145732
  18.7 16.4 %copy-start.8 = (bf16[384,128]{1,0:T(8,128)(2,1)S(1)}, bf16[384,128]{1,0:T(8,128)(2,1)}, u32[]{:S(2)}) copy-start(bf16[384,128]{1,0:T(8,128)(2,1)} %w1_ref.7) | copy-start | bytes 294916
  18.7 16.4 %copy-start.9 = (bf16[256,128]{1,0:T(8,128)(2,1)S(1)}, bf16[256,128]{1,0:T(8,128)(2,1)}, u32[]{:S(2)}) copy-start(bf16[256,128]{1,0:T(8,128)(2,1)} %v1_ref.3) | copy-start | bytes 196612
  18.7 16.4 %copy-start.10 = (bf16[128,128]{1,0:T(8,128)(2,1)S(1)}, bf16[128,128]{1,0:T(8,128)(2,1)}, u32[]{:S(2)}) copy-start(bf16[128,128]{1,0:T(8,128)(2,1)} %w2_ref.5) | copy-start | bytes 98308
  18.7 16.4 %copy-start.11 = (bf16[128,128]{1,0:T(8,128)(2,1)S(1)}, bf16[128,128]{1,0:T(8,128)(2,1)}, u32[]{:S(2)}) copy-start(bf16[128,128]{1,0:T(8,128)(2,1)} %v2_ref.3) | copy-start | bytes 98308
  21.2 13.9 %all-to-all-start.1 = ((bf16[32,16,128]{2,1,0:T(8,128)(2,1)}), bf16[32,16,128]{2,1,0:T(8,128)(2,1)S(1)}, u32[]{:S(2)}, u32[]{:S(2)}) async-start(bf16[32,16,128]{2,1,0:T(8,128)(2,1)} %bitcast.6), calls=%async_computation.1 | async-start | bytes 262144 | tf_op jit(solution)/shard_map/all_to_all | solution.py:499
  27.4 14.1 %collective-permute-start = (bf16[528,128]{1,0:T(8,128)(2,1)S(1)}, bf16[528,128]{1,0:T(8,128)(2,1)S(1)}, u32[]{:S(2)}, u32[]{:S(2)}) collective-permute-start(bf16[528,128]{1,0:T(8,128)(2,1)S(1)} %get-tuple-element.70), channel_id=1, source_target_pairs={{0,96},{32,0},{64,32},{96,64},{1,97},{33,1},{65,33},{97,65},{2,98}... | collective-permute-start | bytes 405512 | tf_op jit(solution)/shard_map/ppermute | solution.py:497
  31.2 10.3 %collective-permute-start.1 = (bf16[528,128]{1,0:T(8,128)(2,1)S(1)}, bf16[528,128]{1,0:T(8,128)(2,1)S(1)}, u32[]{:S(2)}, u32[]{:S(2)}) collective-permute-start(bf16[528,128]{1,0:T(8,128)(2,1)S(1)} %get-tuple-element.71), channel_id=1, source_target_pairs={{0,64},{32,96},{64,0},{96,32},{1,65},{33,97},{65,1},{97,33},{2,66}... | collective-permute-start | bytes 405512 | tf_op jit(solution)/shard_map/ppermute | solution.py:497
  31.3 10.3 %collective-permute-start.2 = (bf16[528,128]{1,0:T(8,128)(2,1)S(1)}, bf16[528,128]{1,0:T(8,128)(2,1)S(1)}, u32[]{:S(2)}, u32[]{:S(2)}) collective-permute-start(bf16[528,128]{1,0:T(8,128)(2,1)S(1)} %get-tuple-element.72), channel_id=1, source_target_pairs={{0,32},{32,64},{64,96},{96,0},{1,33},{33,65},{65,97},{97,1},{2,34}... | collective-permute-start | bytes 405512 | tf_op jit(solution)/shard_map/ppermute | solution.py:497
  43.5 7.1 %collective-permute-start.3 = (bf16[256,128]{1,0:T(8,128)(2,1)S(1)}, bf16[256,128]{1,0:T(8,128)(2,1)S(1)}, u32[]{:S(2)}, u32[]{:S(2)}) collective-permute-start(bf16[256,128]{1,0:T(8,128)(2,1)S(1)} %get-tuple-element.76), channel_id=1, source_target_pairs={{0,32},{32,64},{64,96},{96,0},{1,33},{33,65},{65,97},{97,1},{2,34}... | collective-permute-start | bytes 196616 | tf_op jit(solution)/shard_map/ppermute | solution.py:523
  45.2 6.2 %collective-permute-start.4 = (bf16[256,128]{1,0:T(8,128)(2,1)S(1)}, bf16[256,128]{1,0:T(8,128)(2,1)S(1)}, u32[]{:S(2)}, u32[]{:S(2)}) collective-permute-start(bf16[256,128]{1,0:T(8,128)(2,1)S(1)} %get-tuple-element.77), channel_id=1, source_target_pairs={{0,64},{32,96},{64,0},{96,32},{1,65},{33,97},{65,1},{97,33},{2,66}... | collective-permute-start | bytes 196616 | tf_op jit(solution)/shard_map/ppermute | solution.py:523
  48.5 3.4 %collective-permute-start.5 = (bf16[256,128]{1,0:T(8,128)(2,1)S(1)}, bf16[256,128]{1,0:T(8,128)(2,1)S(1)}, u32[]{:S(2)}, u32[]{:S(2)}) collective-permute-start(bf16[256,128]{1,0:T(8,128)(2,1)S(1)} %get-tuple-element.78), channel_id=1, source_target_pairs={{0,96},{32,0},{64,32},{96,64},{1,97},{33,1},{65,33},{97,65},{2,98}... | collective-permute-start | bytes 196616 | tf_op jit(solution)/shard_map/ppermute | solution.py:523
  53.2 4.3 %collective-permute-start.8 = (bf16[256,128]{1,0:T(8,128)(2,1)S(1)}, bf16[256,128]{1,0:T(8,128)(2,1)S(1)}, u32[]{:S(2)}, u32[]{:S(2)}) collective-permute-start(bf16[256,128]{1,0:T(8,128)(2,1)S(1)} %get-tuple-element.86.rest_0_), channel_id=1, source_target_pairs={{0,32},{32,64},{64,96},{96,0},{1,33},{33,65},{65,97},{97,1},{2,34}... | collective-permute-start | bytes 196616 | tf_op jit(solution)/shard_map/ppermute | solution.py:540
  53.8 4.6 %collective-permute-start.7 = (bf16[256,128]{1,0:T(8,128)(2,1)S(1)}, bf16[256,128]{1,0:T(8,128)(2,1)S(1)}, u32[]{:S(2)}, u32[]{:S(2)}) collective-permute-start(bf16[256,128]{1,0:T(8,128)(2,1)S(1)} %get-tuple-element.86.rest_0_), channel_id=1, source_target_pairs={{0,64},{32,96},{64,0},{96,32},{1,65},{33,97},{65,1},{97,33},{2,66}... | collective-permute-start | bytes 196616 | tf_op jit(solution)/shard_map/ppermute | solution.py:540
  56.1 3.4 %collective-permute-start.6 = (bf16[256,128]{1,0:T(8,128)(2,1)S(1)}, bf16[256,128]{1,0:T(8,128)(2,1)S(1)}, u32[]{:S(2)}, u32[]{:S(2)}) collective-permute-start(bf16[256,128]{1,0:T(8,128)(2,1)S(1)} %get-tuple-element.86.rest_0_), channel_id=1, source_target_pairs={{0,96},{32,0},{64,32},{96,64},{1,97},{33,1},{65,33},{97,65},{2,98}... | collective-permute-start | bytes 196616 | tf_op jit(solution)/shard_map/ppermute | solution.py:540
  59.5 17.1 %copy-start.13 = (s32[4096]{0:T(1024)S(1)}, s32[4096]{0:T(1024)}, u32[]{:S(2)}) copy-start(s32[4096]{0:T(1024)} %param.28) | copy-start | bytes 49156
  59.5 17.1 %copy-start.16 = (s32[4096]{0:T(1024)S(1)}, s32[4096]{0:T(1024)}, u32[]{:S(2)}) copy-start(s32[4096]{0:T(1024)} %param.29) | copy-start | bytes 49156
  69.2 19.0 %all-to-all-start.2 = ((bf16[32,64,128]{2,1,0:T(8,128)(2,1)}), bf16[32,64,128]{2,1,0:T(8,128)(2,1)S(1)}, u32[]{:S(2)}, u32[]{:S(2)}) async-start(bf16[32,64,128]{2,1,0:T(8,128)(2,1)} %get-tuple-element.87), calls=%async_computation.2 | async-start | bytes 1048576 | tf_op jit(solution)/shard_map/all_to_all | solution.py:580
  88.3 4.0 %collective-permute-start.11 = (f32[48,128]{1,0:T(8,128)S(1)}, f32[48,128]{1,0:T(8,128)S(1)}, u32[]{:S(2)}, u32[]{:S(2)}) collective-permute-start(f32[48,128]{1,0:T(8,128)S(1)} %add_parts.1.refs_0_), channel_id=1, source_target_pairs={{0,32},{32,64},{64,96},{96,0},{1,33},{33,65},{65,97},{97,1},{2,34}... | collective-permute-start | bytes 73736 | tf_op jit(solution)/shard_map/ppermute | solution.py:586
  88.4 4.4 %collective-permute-start.10 = (f32[48,128]{1,0:T(8,128)S(1)}, f32[48,128]{1,0:T(8,128)S(1)}, u32[]{:S(2)}, u32[]{:S(2)}) collective-permute-start(f32[48,128]{1,0:T(8,128)S(1)} %add_parts.1.refs_0_), channel_id=1, source_target_pairs={{0,64},{32,96},{64,0},{96,32},{1,65},{33,97},{65,1},{97,33},{2,66}... | collective-permute-start | bytes 73736 | tf_op jit(solution)/shard_map/ppermute | solution.py:586
  90.8 2.8 %collective-permute-start.9 = (f32[48,128]{1,0:T(8,128)S(1)}, f32[48,128]{1,0:T(8,128)S(1)}, u32[]{:S(2)}, u32[]{:S(2)}) collective-permute-start(f32[48,128]{1,0:T(8,128)S(1)} %add_parts.1.refs_0_), channel_id=1, source_target_pairs={{0,96},{32,0},{64,32},{96,64},{1,97},{33,1},{65,33},{97,65},{2,98}... | collective-permute-start | bytes 73736 | tf_op jit(solution)/shard_map/ppermute | solution.py:586
  94.4 15.5 %all-to-all-start.3 = ((bf16[32,48,128]{2,1,0:T(8,128)(2,1)}), bf16[32,48,128]{2,1,0:T(8,128)(2,1)S(1)}, u32[]{:S(2)}, u32[]{:S(2)}) async-start(bf16[32,48,128]{2,1,0:T(8,128)(2,1)} %add_groups.1), calls=%async_computation.3 | async-start | bytes 786432 | tf_op jit(solution)/shard_map/all_to_all | solution.py:592
  (20 other events, 120.4 us)
